TPU v7x, 32 devices: a whole 2x2x4 slice. The times are simulated.
32 devices in a mesh: seq: 8 (over y, x, core), pos: 4 (over z).
Axes of the slice: x: 2, y: 2, z: 4, core: 2. Of those that a mesh axis runs over, the one named last changes fastest.
Arguments:
- block_input: bfloat16 [8192, 1024], P(('seq', 'pos')), may hold values from -6 to 6
- cotangent: bfloat16 [8192, 1024], P(('seq', 'pos')), may hold values from -6 to 6
- lengths: int32 [8], P('seq'), may hold values from 769 to 1024, as said below
- in_proj: bfloat16 [1024, 3, 1024], P('seq', None, 'pos'), may hold values from -0.1875 to 0.1875
- out_proj: bfloat16 [1024, 1024], P('pos', 'seq'), may hold values from -0.1875 to 0.1875
- up_proj: bfloat16 [1024, 4096], P('seq', 'pos'), may hold values from -0.1875 to 0.1875
- down_proj: bfloat16 [4096, 1024], P('pos', 'seq'), may hold values from -0.09375 to 0.09375
- first_gain: float32 [1024], replicated, may hold values from 0.1 to 1.9
- second_gain: float32 [1024], replicated, may hold values from 0.1 to 1.9
- short_filter: float32 [3, 3072], replicated, may hold values from -3 to 3
- skip_bias: float32 [1024], replicated, may hold values from -4 to 4
- filter_in: float32 [33, 64], replicated, may hold values from -1 to 1
- filter_in_bias: float32 [64], replicated, may hold values from -3.140625 to 3.140625
- filter_mid: float32 [64, 64], replicated, may hold values from -0.75 to 0.75
- filter_mid_bias: float32 [64], replicated, may hold values from -3.140625 to 3.140625
- filter_out: float32 [64, 1024], replicated, may hold values from -0.0625 to 0.0625
Outputs:
- block_output: bfloat16 [8192, 1024], P(('seq', 'pos'))
- input_grad: bfloat16 [8192, 1024], P(('seq', 'pos'))
- in_proj_grad: float32 [1024, 3, 1024], P('seq', None, 'pos')
- out_proj_grad: float32 [1024, 1024], P('pos', 'seq')
- up_proj_grad: float32 [1024, 4096], P('seq', 'pos')
- down_proj_grad: float32 [4096, 1024], P('pos', 'seq')
- first_gain_grad: float32 [1024], replicated
- second_gain_grad: float32 [1024], replicated
- short_filter_grad: float32 [3, 3072], replicated
- skip_bias_grad: float32 [1024], replicated
- filter_in_grad: float32 [33, 64], replicated
- filter_in_bias_grad: float32 [64], replicated
- filter_mid_grad: float32 [64, 64], replicated
- filter_mid_bias_grad: float32 [64], replicated
- filter_out_grad: float32 [64, 1024], replicated
Inputs may be any that keep to these rules, and one draw needn't show every extreme that they name: `lengths`: the largest entry is exactly 1024.
All inputs are finite; a program needn't handle non-finite values.
Results may differ from a plain program's by a relative error of at most 0.014.
Values may be sent and summed in bfloat16 or wider, within the bound.
No kernel may reach another device: no remote copies, remote signals or barrier semaphores. Data moves between devices by JAX's collectives and lax.ppermute only.
A program may use at most 192 MiB of HBM per device.

v0:
```python
import functools
import math

import jax
import jax.numpy as jnp
import ml_dtypes
import numpy as np
from jax import lax
from jax.experimental import pallas as pl
from jax.experimental.pallas import tpu as pltpu
from jax.sharding import PartitionSpec as P

EMB = 33
LSEQ = 1024
RING = 4
CUBE = 8
PLANE = 4
SCALE = 1.0

epsilon = 1e-05
highest = lax.Precision.HIGHEST
f32 = jnp.float32
bf16 = jnp.bfloat16

OWNED = 80
GAINS = 8
SHARED = 64
PACKED = OWNED + GAINS + SHARED


def nt_dot(left, right):
    return lax.dot_general(left, right, (((1,), (1,)), ((), ())), preferred_element_type=f32)


def tn_dot(left, right):
    return lax.dot_general(left, right, (((0,), (0,)), ((), ())), preferred_element_type=f32)


def nn_dot(left, right):
    return jnp.dot(left, right, preferred_element_type=f32)


def full_dot(left, right, dims=((1,), (0,))):
    return lax.dot_general(left, right, (dims, ((), ())), precision=highest, preferred_element_type=f32)


def embedding(seq_len):
    positions = np.concatenate([np.arange(0, seq_len, 2), np.arange(1, seq_len, 2)])
    timeline = positions / (seq_len - 1)
    band_count = (EMB - 1) // 2
    bands = np.linspace(0.0001, band_count - 1, band_count)
    phases = (2.0 * math.pi / seq_len * positions)[:, None] * bands[None, :]
    features = np.concatenate([timeline[:, None], np.cos(phases), -np.sin(phases)], 1)
    return features.astype(np.float32), timeline.astype(np.float32)[:, None]


def spectral_tables(length):
    half = length // 2
    freq = 2 * np.arange(half) + 1
    tables = []
    for offset in (1, 3):
        angle = (freq[:, None] * (4 * np.arange(half) + offset)[None, :]) % (8 * length)
        angle = angle * (math.pi / (4 * length))
        tables.append(np.concatenate([np.cos(angle), np.sin(angle)]))
    tables += [tables[0].T / length, tables[1].T / length]
    split = []
    for table in tables:
        top = table.astype(ml_dtypes.bfloat16)
        split += [top, (table - top.astype(np.float64)).astype(ml_dtypes.bfloat16)]
    order = np.concatenate([np.arange(half), length - 1 - np.arange(half)])
    turn = (2.0 * order + 1.0) * (math.pi / (4 * length))
    turns = np.stack([np.cos(turn), np.sin(turn)]).astype(np.float32)[:, :, None]
    return split, turns


def split_dot(table_top, table_low, value):
    top = value.astype(bf16)
    low = (value - top.astype(f32)).astype(bf16)
    return nn_dot(table_top, top) + nn_dot(table_top, low) + nn_dot(table_low, top)


def transform(tables, even, odd):
    half = even.shape[0]
    even_sums = split_dot(tables[0][...], tables[1][...], even)
    odd_sums = split_dot(tables[2][...], tables[3][...], odd)
    even_cos, even_sin = even_sums[:half], even_sums[half:]
    odd_cos, odd_sin = odd_sums[:half], odd_sums[half:]
    real = jnp.concatenate([even_cos + odd_cos, even_sin - odd_sin], 0)
    imag = jnp.concatenate([-(even_sin + odd_sin), odd_cos - even_cos], 0)
    return real, imag


def restore(tables, real, imag):
    half = real.shape[0] // 2
    real_low, real_up, imag_low, imag_up = real[:half], real[half:], imag[:half], imag[half:]
    even = jnp.concatenate([real_low - imag_up, real_up - imag_low], 0)
    odd = jnp.concatenate([real_low + imag_up, -(real_up + imag_low)], 0)
    return (
        split_dot(tables[4][...], tables[5][...], even),
        split_dot(tables[6][...], tables[7][...], odd),
    )


def later(value):
    row = lax.broadcasted_iota(jnp.int32, value.shape, 0)
    return jnp.where(row == 0, 0.0, pltpu.roll(value, 1, 0))


def sooner(value):
    row = lax.broadcasted_iota(jnp.int32, value.shape, 0)
    last = value.shape[0] - 1
    return jnp.where(row == last, 0.0, pltpu.roll(value, last, 0))


def mix_streams(even, odd, lags):
    mixed_even = lags[0] * even + lags[1] * later(odd) + lags[2] * later(even)
    mixed_odd = lags[0] * odd + lags[1] * even + lags[2] * later(odd)
    return mixed_even, mixed_odd


def valid_rows(length, half, offset):
    place = 2 * lax.broadcasted_iota(jnp.int32, (half, 1), 0) + offset
    return jnp.where(place < length, 1.0, 0.0)


def row_order(rows, dtype):
    left = lax.broadcasted_iota(jnp.int32, (rows, rows), 0)
    right = lax.broadcasted_iota(jnp.int32, (rows, rows), 1)
    half = rows // 2
    source = jnp.where(left < half, 2 * left, 2 * (left - half) + 1)
    return jnp.where(right == source, 1.0, 0.0).astype(dtype)


def standardize(values):
    centred = values - jnp.mean(values, axis=-1, keepdims=True)
    scaling = lax.rsqrt(jnp.mean(centred * centred, axis=-1, keepdims=True) + epsilon)
    return centred * scaling, scaling


def scale_back(unit, scaling, weighted):
    return scaling * (
        weighted
        - jnp.mean(weighted, axis=-1, keepdims=True)
        - unit * jnp.mean(weighted * unit, axis=-1, keepdims=True)
    )


def piece(place, size):
    return pl.ds(pl.multiple_of(place * size, size), size)


def rows_kernel(rows_in, cot_in, gains, normed, inputs, cot):
    order = row_order(rows_in.shape[0], bf16)
    inputs[...] = nn_dot(order, rows_in[...]).astype(bf16)
    cot[...] = nn_dot(order, cot_in[...]).astype(bf16)
    unit, _ = standardize(inputs[...].astype(f32))
    normed[...] = (unit * gains[...]).astype(bf16)


def weights_kernel(in_w, up_w, down_w, in_rows, layer_rows):
    streams, channels = in_w.shape[0], in_w.shape[2]
    for k in range(streams):
        in_rows[pl.ds(k * channels, channels), :] = in_w[k].T
    turned = up_w[...].T
    part = turned.shape[0] // CUBE
    for m in range(CUBE):
        layer_rows[pl.ds(2 * m * part, part), :] = turned[m * part : (m + 1) * part]
        layer_rows[pl.ds((2 * m + 1) * part, part), :] = down_w[pl.ds(m * part, part), :]


def side_by_side(ref, out):
    count, lane = ref.shape[0] // CUBE, ref.shape[1]
    for m in range(CUBE):
        out[:, pl.ds(m * lane, lane)] = ref[pl.ds(m * count, count), :]


def decay_of(info, times, channels, width):
    lanes = lax.broadcasted_iota(jnp.int32, (1, channels), 1) + info[2] * channels
    slowest = math.log(0.01) / 1.5
    fastest = math.log(0.01) / 0.3
    rates = jnp.abs(slowest + (fastest - slowest) * lanes.astype(f32) / (width - 1))
    return jnp.exp(-times[...] * rates)


def pair_dot(left, right):
    half = left.shape[0] // 2
    return jnp.concatenate([full_dot(left[:half], right), full_dot(left[half:], right)], 1)


def unpair(value):
    lanes = value.shape[1] // 2
    return jnp.concatenate([value[:, :lanes], value[:, lanes:]], 0)


def hidden_kernel(features, first, bias_one, middle, bias_two, hidden):
    inner = middle.shape[0]
    twice = lambda ref: jnp.concatenate([ref[...], ref[...]], 1)
    angle = pair_dot(features[...], first[...]) + twice(bias_one)
    one = unpair(jnp.sin(angle))
    hidden[:, pl.ds(0, inner)] = one
    hidden[:, pl.ds(inner, inner)] = unpair(jnp.cos(angle))
    angle = pair_dot(one, middle[...]) + twice(bias_two)
    hidden[:, pl.ds(2 * inner, inner)] = unpair(jnp.sin(angle))
    hidden[:, pl.ds(3 * inner, inner)] = unpair(jnp.cos(angle))


def taps_kernel(info, width, hidden, times, last, turns, *refs):
    tables, (spectrum,) = refs[:8], refs[8:]
    half = hidden.shape[0] // 2
    inner = last.shape[0]
    taps = full_dot(hidden[:, pl.ds(2 * inner, inner)], last[...]) * decay_of(info, times, last.shape[1], width)
    real, imag = transform(tables, taps[:half], taps[half:])
    spectrum[0] = real * turns[0] - imag * turns[1]
    spectrum[1] = real * turns[1] + imag * turns[0]


def ring_blocks(info, count):
    return [piece((info[2] + j) & (RING - 1), count) for j in range(RING)]


def conv_kernel(info, *refs):
    slots, (in_all, lags, skip, spectrum), refs = refs[:4], refs[4:8], refs[8:]
    tables = refs[:8]
    projected, long_conv, driven_spectrum, gated, in_full = refs[8:]
    length = info[3]
    half_rows = slots[0].shape[0] // 2
    half = projected.shape[0] // 2
    channels = skip.shape[1]
    side_by_side(in_all, in_full)
    for j, slot in enumerate(slots):
        total = nt_dot(slot[...], in_full[...]).astype(bf16)
        block = (info[2] + j) & (RING - 1)
        projected[piece(block, half_rows), :] = total[:half_rows]
        projected[pl.ds(pl.multiple_of(half + block * half_rows, half_rows), half_rows), :] = total[half_rows:]
    streams = []
    for k in range(3):
        lanes = pl.ds(k * channels, channels)
        streams.append(
            mix_streams(
                projected[pl.ds(0, half), lanes].astype(f32),
                projected[pl.ds(half, half), lanes].astype(f32),
                [lags[pl.ds(i, 1), lanes] for i in range(3)],
            )
        )
    (outer_even, outer_odd), (inner_even, inner_odd), (value_even, value_odd) = streams
    even = value_even * inner_even * valid_rows(length, half, 0)
    odd = value_odd * inner_odd * valid_rows(length, half, 1)
    real, imag = transform(tables, even, odd)
    driven_spectrum[0] = real
    driven_spectrum[1] = imag
    taps_real, taps_imag = spectrum[0], spectrum[1]
    back_even, back_odd = restore(
        tables, real * taps_real - imag * taps_imag, real * taps_imag + imag * taps_real
    )
    back_even += skip[...] * even
    back_odd += skip[...] * odd
    long_conv[pl.ds(0, half), :] = back_even
    long_conv[pl.ds(half, half), :] = back_odd
    even, odd = (back_even * outer_even).astype(bf16), (back_odd * outer_odd).astype(bf16)
    for z in range(RING):
        here = slice(z * half_rows, (z + 1) * half_rows)
        gated[pl.ds(2 * z * half_rows, half_rows), :] = even[here]
        gated[pl.ds((2 * z + 1) * half_rows, half_rows), :] = odd[here]


def out_kernel(info, gated, out_all, inputs, gains, residual, second):
    rows, width = inputs.shape
    lane = out_all.shape[1]
    wide = jnp.concatenate([gated[block, :] for block in ring_blocks(info, rows)], 1)
    for m in range(CUBE):
        lanes = pl.ds(m * lane, lane)
        residual[:, lanes] = inputs[:, lanes].astype(f32) + nn_dot(wide, out_all[pl.ds(m * width, width), :])
    unit, _ = standardize(residual[...])
    second[...] = (unit * gains[...]).astype(bf16)


def layer_kernel(info, *refs):
    rows_in, (cot_all, *slots), refs = refs[:10], refs[10:15], refs[15:]
    out_kept, out_given, back_kept, back_given, grads, up_sum, down_sum = refs
    own, sib, across, across_sib, along, along_sib, top, low, top_sib, low_sib = rows_in
    rows = own.shape[0]
    part = slots[0].shape[0] // 2
    ups = jnp.concatenate([slot[pl.ds(0, part), :] for slot in slots], 0)
    downs = jnp.concatenate([slot[pl.ds(part, part), :] for slot in slots], 0)
    chips = ((own, sib), (across, across_sib), (along, along_sib), (top, low, top_sib, low_sib))
    for r, parts in enumerate(chips):
        second = jnp.concatenate([ref[...] for ref in parts], 0)
        cot = jnp.concatenate([cot_all[piece(info[1] ^ (2 * r + i), rows), :] for i in range(2)], 0)
        pre_act = nt_dot(second, ups)
        grad_act = nt_dot(cot, downs)
        lower = 0.5 * (1.0 + lax.erf(pre_act * math.sqrt(0.5)))
        density = jnp.exp(-0.5 * pre_act * pre_act) * (1.0 / math.sqrt(2.0 * math.pi))
        activated = (pre_act * lower).astype(bf16)
        grad_pre = (grad_act * (lower + pre_act * density)).astype(bf16)
        here = pl.ds(r * rows, rows)
        out = nn_dot(activated, downs)
        out_kept[here, :] = out[:rows].astype(bf16)
        out_given[here, :] = out[rows:].astype(bf16)
        back = nn_dot(grad_pre, ups)
        back_kept[here, :] = back[:rows].astype(bf16)
        back_given[here, :] = back[rows:].astype(bf16)
        up_grad = tn_dot(grad_pre, second)
        down_grad = tn_dot(activated, cot)
        up_sum[...] = up_grad if r == 0 else up_sum[...] + up_grad
        down_sum[...] = down_grad if r == 0 else down_sum[...] + down_grad
    for j, block in enumerate(ring_blocks(info, 2 * part)):
        here = pl.ds(j * part, part)
        both = jnp.concatenate([up_sum[here, :], down_sum[here, :]], 0)
        grads[block, :] = both.astype(bf16)


def share_kernel(kept, got, own, across, along, top, low):
    rows = own.shape[0]
    for r, ref in enumerate((own, across, along)):
        here = pl.ds(r * rows, rows)
        ref[...] = (kept[here, :].astype(f32) + got[here, :].astype(f32)).astype(bf16)
    for i, ref in enumerate((top, low)):
        here = pl.ds(3 * rows + i * rows // 2, rows // 2)
        ref[...] = (kept[here, :].astype(f32) + got[here, :].astype(f32)).astype(bf16)


def turn_kernel(across, along, top, low, across_sum, along_sum):
    half = top.shape[0]
    first, second = pl.ds(0, half), pl.ds(half, half)
    across_sum[first, :] = across[first, :]
    across_sum[second, :] = (across[second, :].astype(f32) + low[...].astype(f32)).astype(bf16)
    along_sum[first, :] = (along[first, :].astype(f32) + top[...].astype(f32)).astype(bf16)
    along_sum[second, :] = along[second, :]


def branch_kernel(
    info, own, across, along, residual, gains, cot, out_all, grad_res, branch, gain_grad, grad_gated
):
    rows, width = residual.shape
    lane = out_all.shape[1]
    channels = grad_gated.shape[1]
    back = own[...].astype(f32) + across[...].astype(f32) + along[...].astype(f32)
    unit, scaling = standardize(residual[...])
    gain_grad[...] = jnp.sum(back * unit, axis=0, keepdims=True)
    total = cot[...].astype(f32) + scale_back(unit, scaling, back * gains[...])
    grad_res[...] = total
    branch[...] = total.astype(bf16)
    total = None
    for m in range(CUBE):
        part = nt_dot(branch[:, pl.ds(m * lane, lane)], out_all[pl.ds(m * width, width), :])
        total = part if m == 0 else total + part
    total = total.astype(bf16)
    for j, block in enumerate(ring_blocks(info, rows)):
        grad_gated[block, :] = total[:, j * channels : (j + 1) * channels]


def finish_kernel(residual, own, across, along, block_output):
    total = own[...].astype(f32) + across[...].astype(f32) + along[...].astype(f32)
    total = (residual[...] + total).astype(bf16)
    block_output[...] = tn_dot(row_order(total.shape[0], bf16), total).astype(bf16)


def below(total, out):
    count, lane = total.shape[0], total.shape[1] // CUBE
    for m in range(CUBE):
        out[pl.ds(m * count, count), :] = total[:, m * lane : (m + 1) * lane].astype(out.dtype)


def below_kernel(total, out):
    below(total[...], out)


def out_grad_kernel(gated, branch, out_grad):
    rows = branch.shape[0]
    parts = [tn_dot(gated[pl.ds(z * rows, rows), :], branch[...]) for z in range(RING)]
    below(jnp.concatenate(parts, 0).astype(bf16), out_grad)


def back_kernel(
    info, grad_gated, projected, long_conv, driven_spectrum, lags, skip, spectrum, turns, *refs
):
    tables = refs[:8]
    grad_projected, grad_taps, small = refs[8:]
    length = info[3]
    channels = grad_gated.shape[1]
    half = projected.shape[0] // 2
    half_rows = half // RING
    plain, mixed = [], []
    for k in range(3):
        lanes = pl.ds(k * channels, channels)
        even = projected[pl.ds(0, half), lanes].astype(f32)
        odd = projected[pl.ds(half, half), lanes].astype(f32)
        plain.append((even, odd))
        mixed.append(mix_streams(even, odd, [lags[pl.ds(i, 1), lanes] for i in range(3)]))
    (outer_even, outer_odd), (inner_even, inner_odd), (value_even, value_odd) = mixed
    valid_even, valid_odd = valid_rows(length, half, 0), valid_rows(length, half, 1)
    gated_even, gated_odd = (
        jnp.concatenate([grad_gated[pl.ds((2 * z + i) * half_rows, half_rows), :] for z in range(RING)], 0).astype(f32)
        for i in range(2)
    )
    conv_even, conv_odd = gated_even * outer_even, gated_odd * outer_odd
    real, imag = transform(tables, conv_even, conv_odd)
    taps_real, taps_imag = spectrum[0], spectrum[1]
    driven_even, driven_odd = restore(
        tables, real * taps_real + imag * taps_imag, imag * taps_real - real * taps_imag
    )
    driven_even = (driven_even + skip[...] * conv_even) * valid_even
    driven_odd = (driven_odd + skip[...] * conv_odd) * valid_odd
    small[pl.ds(9, 1), :] = jnp.sum(
        conv_even * value_even * inner_even * valid_even + conv_odd * value_odd * inner_odd * valid_odd,
        axis=0,
        keepdims=True,
    )
    small[pl.ds(10, 6), :] = jnp.zeros((6, channels), f32)
    grads = (
        (gated_even * long_conv[pl.ds(0, half), :], gated_odd * long_conv[pl.ds(half, half), :]),
        (driven_even * value_even, driven_odd * value_odd),
        (driven_even * inner_even, driven_odd * inner_odd),
    )
    for k, (even, odd) in enumerate(grads):
        lanes = pl.ds(k * channels, channels)
        lag = [lags[pl.ds(i, 1), lanes] for i in range(3)]
        plain_even, plain_odd = plain[k]
        sums = (
            even * plain_even + odd * plain_odd,
            even * later(plain_odd) + odd * plain_even,
            even * later(plain_even) + odd * later(plain_odd),
        )
        for i in range(3):
            small[pl.ds(3 * i + k, 1), :] = jnp.sum(sums[i], axis=0, keepdims=True)
        next_even, next_odd = sooner(even), sooner(odd)
        stream_even = (lag[0] * even + lag[1] * odd + lag[2] * next_even).astype(bf16)
        stream_odd = (lag[0] * odd + lag[1] * next_even + lag[2] * next_odd).astype(bf16)
        for z in range(RING):
            here = slice(z * half_rows, (z + 1) * half_rows)
            grad_projected[pl.ds(2 * z * half_rows, half_rows), lanes] = stream_even[here]
            grad_projected[pl.ds((2 * z + 1) * half_rows, half_rows), lanes] = stream_odd[here]
    base_real, base_imag = driven_spectrum[0], driven_spectrum[1]
    cross_real = real * base_real + imag * base_imag
    cross_imag = imag * base_real - real * base_imag
    taps_even, taps_odd = restore(
        tables,
        cross_real * turns[0] + cross_imag * turns[1],
        cross_imag * turns[0] - cross_real * turns[1],
    )
    grad_taps[pl.ds(0, half), :] = taps_even
    grad_taps[pl.ds(half, half), :] = taps_odd


def normed_kernel(info, grad_projected, in_full, n0, n1, n2, n3, gains, partial, gain_grad):
    rows = n0.shape[0]
    total_gain = None
    for j, (slot, block) in enumerate(zip((n0, n1, n2, n3), ring_blocks(info, rows))):
        total = nn_dot(grad_projected[block, :], in_full[...])
        partial[block, :] = total.astype(bf16)
        part = jnp.sum(total * slot[...].astype(f32), axis=0, keepdims=True)
        total_gain = part if j == 0 else total_gain + part
    gain_grad[...] = total_gain / gains[...]


def in_grad_kernel(info, grad_projected, n0, n1, n2, n3, in_grad):
    normed = jnp.concatenate([n0[...], n1[...], n2[...], n3[...]], 0)
    grad = jnp.concatenate([grad_projected[block, :] for block in ring_blocks(info, n0.shape[0])], 0)
    below(tn_dot(grad, normed).astype(bf16), in_grad)


def end_kernel(grad_normed, inputs, gains, grad_res, input_grad):
    grad = grad_normed[...].astype(f32)
    unit, scaling = standardize(inputs[...].astype(f32))
    total = (grad_res[...] + scale_back(unit, scaling, grad * gains[...])).astype(bf16)
    input_grad[...] = tn_dot(row_order(total.shape[0], bf16), total).astype(bf16)


def layer_end_kernel(parts, up_grad, down_grad):
    part = parts.shape[0] // CUBE // 2
    for m in range(CUBE):
        here = pl.ds(m * part, part)
        up_grad[:, here] = parts[pl.ds(2 * m * part, part), :].astype(f32).T
        down_grad[here, :] = parts[pl.ds((2 * m + 1) * part, part), :].astype(f32)


def out_sum_kernel(info, parts, own, p1, p2, p3):
    rows = parts.shape[0] // CUBE
    count = own.shape[0]
    for j, ref in enumerate((own, p1, p2, p3)):
        place = ((info[2] + j) & (RING - 1)) * count
        total = None
        for m in range(CUBE):
            here = pl.ds(pl.multiple_of(m * rows + place, count), count)
            part = parts[here, :].astype(f32)
            total = part if m == 0 else total + part
        ref[...] = total.astype(ref.dtype)


def out_end_kernel(own, p1, p2, p3, total):
    total[...] = own[...] + p1[...].astype(f32) + p2[...].astype(f32) + p3[...].astype(f32)


def in_end_kernel(parts, in_grad):
    channels = in_grad.shape[2]
    rows = parts.shape[0] // CUBE
    for k in range(in_grad.shape[0]):
        total = None
        for m in range(CUBE):
            part = parts[pl.ds(m * rows + k * channels, channels), :].astype(f32)
            total = part if m == 0 else total + part
        in_grad[k] = total.T


def pack_kernel(
    info, width, grad_taps, hidden, features, times, middle, last, small, gain_one, gain_two, packed
):
    inner = middle.shape[0]
    span = packed.shape[1]
    one, slope_one, two, slope_two = (hidden[:, pl.ds(i * inner, inner)] for i in range(4))
    grad_raw = grad_taps[...] * decay_of(info, times, span, width)
    rows = ((0,), (0,))
    packed[pl.ds(0, inner), :] = full_dot(two, grad_raw, rows)
    grad_two = full_dot(grad_raw, last[...], ((1,), (1,))) * slope_two
    grad_one = full_dot(grad_two, middle[...], ((1,), (1,))) * slope_one
    packed[pl.ds(64, 16), :] = small[...]
    for r in range(PLANE):
        lanes = pl.ds(r * span, span)
        packed[pl.ds(OWNED + r, 1), :] = gain_one[:, lanes]
        packed[pl.ds(OWNED + PLANE + r, 1), :] = gain_two[:, lanes]
    start = OWNED + GAINS
    packed[pl.ds(start, SHARED), :] = jnp.zeros((SHARED, span), f32)
    packed[pl.ds(start, inner), pl.ds(0, inner)] = full_dot(one, grad_two, rows)
    packed[pl.ds(start, EMB), pl.ds(inner, inner)] = full_dot(features[...], grad_one, rows)
    packed[pl.ds(start, 1), pl.ds(2 * inner, inner)] = jnp.sum(grad_one, axis=0, keepdims=True)
    packed[pl.ds(start, 1), pl.ds(3 * inner, inner)] = jnp.sum(grad_two, axis=0, keepdims=True)


def unpack_kernel(
    info, s0, s1, s2, s3, gain_one, gain_two, short, skip, first, bias_one, middle, bias_two, last, slots
):
    place = info[2]
    for j, ref in enumerate((s0, s1, s2, s3)):
        slots[place ^ j] = ref[...]
    channels = s0.shape[1]
    inner = middle.shape[0]
    for z in range(RING):
        lanes = pl.ds(z * channels, channels)
        last[:, lanes] = slots[z, pl.ds(0, 64), :]
        for i in range(3):
            for k in range(3):
                here = pl.ds((k * RING + z) * channels, channels)
                short[pl.ds(i, 1), here] = slots[z, pl.ds(64 + 3 * i + k, 1), :]
        skip[:, lanes] = slots[z, pl.ds(64 + 9, 1), :]
    count = GAINS + SHARED
    total = slots[0, pl.ds(OWNED, count), :] + slots[1, pl.ds(OWNED, count), :]
    total += slots[2, pl.ds(OWNED, count), :] + slots[3, pl.ds(OWNED, count), :]
    for b in range(PLANE):
        lanes = pl.ds(b * channels, channels)
        gain_one[:, lanes] = total[b : b + 1]
        gain_two[:, lanes] = total[PLANE + b : PLANE + b + 1]
    total = total[GAINS:]
    middle[...] = total[:, :inner]
    first[...] = total[:EMB, inner : 2 * inner]
    bias_one[...] = total[:1, 2 * inner : 3 * inner]
    bias_two[...] = total[:1, 3 * inner :]


def tick_kernel(count, *refs):
    refs[count][...] = jnp.zeros_like(refs[count])


def run(kernel, outs, *args, scratch=(), name, micros=2.0, limit=56, after=()):
    place = lambda a: pltpu.SMEM if a.dtype == jnp.int32 else pltpu.VMEM
    shapes = [jax.ShapeDtypeStruct(*o) for o in outs]
    count = len(args)

    def body(*refs):
        kernel(*refs[:count], *refs[count + len(after) :])

    return pl.pallas_call(
        body,
        out_shape=shapes,
        in_specs=[pl.BlockSpec(memory_space=place(a)) for a in args]
        + [pl.BlockSpec(memory_space=pl.ANY) for _ in after],
        out_specs=[pl.BlockSpec(memory_space=pltpu.VMEM)] * len(shapes),
        scratch_shapes=[pltpu.VMEM(*s) for s in scratch],
        compiler_params=pltpu.CompilerParams(vmem_limit_bytes=limit * 2**20),
        cost_estimate=pl.CostEstimate(
            flops=int(SCALE * micros * 1e9), bytes_accessed=int(SCALE * micros * 3e6), transcendentals=0
        ),
        name=name,
    )(*args, *after)


def on_device(
    block_input,
    cotangent,
    lengths,
    in_proj,
    out_proj,
    up_proj,
    down_proj,
    first_gain,
    second_gain,
    short_filter,
    skip_bias,
    filter_in,
    filter_in_bias,
    filter_mid,
    filter_mid_bias,
    filter_out,
):
    seq_size = lax.axis_size("seq")
    fold = seq_size // CUBE
    member = lax.axis_index("seq") // fold
    ring_place = lax.axis_index("pos")
    rows, width = block_input.shape
    channels = width // RING
    lane = width // CUBE
    hidden = up_proj.shape[1]
    seq_len = LSEQ
    members = [[i * fold + o for i in range(CUBE)] for o in range(fold)]
    bundles = [list(range(i * fold, (i + 1) * fold)) for i in range(CUBE)]

    def hop(value, bit):
        pairs = [(i, ((i // fold) ^ bit) * fold + i % fold) for i in range(seq_size)]
        return lax.ppermute(value, "seq", pairs)

    def ring(value, shift):
        return lax.ppermute(value, "pos", [(i, (i + shift) % RING) for i in range(RING)])

    def near_ring(value, bit):
        return lax.ppermute(value, "pos", [(i, i ^ bit) for i in range(RING)])

    def to_rows(value):
        return lax.all_to_all(value, "pos", 0, 0, tiled=True)

    def swap(value):
        return lax.all_to_all(value, "seq", 0, 0, axis_index_groups=members, tiled=True)

    def gather(value):
        return lax.all_gather(value, "seq", axis=0, axis_index_groups=members, tiled=True)

    def scatter(value):
        return lax.psum_scatter(value, "seq", scatter_dimension=0, axis_index_groups=members, tiled=True)

    def settle(value, axis):
        if fold == 1:
            return value
        return lax.psum_scatter(
            value, "seq", scatter_dimension=axis, axis_index_groups=bundles, tiled=True
        )

    def widen(value, axis):
        if fold == 1:
            return value
        return lax.all_gather(value, "seq", axis=axis, axis_index_groups=bundles, tiled=True)

    info = jnp.stack([member % 2, member, ring_place, lengths[0]]).astype(jnp.int32)
    waiting = []
    latest = []

    def now(*values):
        waiting.extend(values)
        return values

    def step(kernel, outs, *args, **options):
        after = [v for v in latest + waiting if not any(v is a for a in args)]
        results = run(kernel, outs, *args, after=after, **options)
        waiting.clear()
        latest[:] = results[:1]
        return results

    def phase(*values, after=()):
        after = [v for v in latest + waiting + list(after) if not any(v is a for a in values)]
        waiting.clear()
        count = len(values) + len(after)
        mark, *passed = pl.pallas_call(
            functools.partial(tick_kernel, count),
            out_shape=[jax.ShapeDtypeStruct((8, 128), f32)]
            + [jax.ShapeDtypeStruct(v.shape, v.dtype) for v in values],
            in_specs=[pl.BlockSpec(memory_space=pl.ANY)] * count,
            out_specs=[pl.BlockSpec(memory_space=pltpu.VMEM)]
            + [pl.BlockSpec(memory_space=pl.ANY)] * len(values),
            input_output_aliases={i: i + 1 for i in range(len(values))},
            name="phase",
        )(*values, *after)
        latest[:] = [mark]
        return passed

    gain_one, gain_two = first_gain.reshape(1, width), second_gain.reshape(1, width)
    in_turned = widen(in_proj.transpose(1, 0, 2), 1)
    out_shard, up_shard, down_shard = widen(out_proj, 1), widen(up_proj, 0), widen(down_proj, 1)
    normed, inputs, cot = step(
        rows_kernel, [((rows, width), bf16)] * 3, block_input, cotangent, gain_one, name="rows", micros=0.2
    )
    normed_slots = [normed, ring(normed, -1)]
    in_rows, layer_rows = step(
        weights_kernel,
        [((3 * channels, lane), bf16), ((2 * hidden, lane), bf16)],
        in_turned, up_shard, down_shard,
        name="weights", micros=0.2,
    )
    in_all = gather(in_rows)
    layer_got = swap(layer_rows)

    channel_start = ring_place * channels
    features, times = (jnp.asarray(v) for v in embedding(seq_len))
    last_layer = lax.dynamic_slice_in_dim(filter_out, channel_start, channels, 1)
    tables, turns = spectral_tables(seq_len)
    tables = [jnp.asarray(t) for t in tables]
    turns = jnp.asarray(turns)
    lags = lax.dynamic_slice_in_dim(
        short_filter.reshape(3, 3, width), channel_start, channels, 2
    ).reshape(3, 3 * channels)
    skip = lax.dynamic_slice_in_dim(skip_bias, channel_start, channels, 0)[None]
    pair = ((2, seq_len, channels), f32)
    inner = filter_mid.shape[0]

    def with_width(kernel):
        return lambda info, *refs: kernel(info, width, *refs)

    (filter_hidden,) = step(
        hidden_kernel,
        [((seq_len, 4 * inner), f32)],
        features, filter_in, filter_in_bias[None], filter_mid, filter_mid_bias[None],
        name="hidden", micros=5,
    )
    normed_slots[1], out_shard = phase(normed_slots[1], out_shard)
    normed_slots.append(ring(normed_slots[1], -1))
    out_shards = [out_shard] + [ring(out_shard, -j) for j in range(1, RING)]
    (layer_own,) = step(
        side_by_side, [((2 * hidden // CUBE, width), bf16)], layer_got, name="layer_own", micros=0.2
    )
    (spectrum,) = step(
        with_width(taps_kernel),
        [pair],
        info, filter_hidden, times, last_layer, turns, *tables,
        name="taps", micros=5,
    )
    normed_slots[2], out_shards[0], *out_shards[1:] = phase(normed_slots[2], *out_shards)
    normed_slots.append(ring(normed_slots[2], -1))
    cot_all = gather(cot)
    layer_own, *out_shards = phase(layer_own, *out_shards, after=[normed_slots[3]])
    layer_slots = [layer_own, ring(layer_own, -1)]
    out_all = gather(jnp.concatenate(out_shards, 0))

    projected, long_conv, driven_spectrum, gated, in_full = step(
        conv_kernel,
        [
            ((seq_len, 3 * channels), bf16),
            ((seq_len, channels), f32),
            pair,
            ((seq_len, channels), bf16),
            ((3 * channels, width), bf16),
        ],
        info, *normed_slots, in_all, lags, skip, spectrum, *tables,
        name="conv", micros=14,
    )
    gated, layer_slots[1] = phase(gated, layer_slots[1], after=[cot_all])
    gated = to_rows(gated)
    layer_slots[:2] = phase(*layer_slots[:2], after=[gated, out_all])
    layer_slots += [ring(layer_slots[1], -1), ring(layer_slots[0], 1)]
    residual, second = step(
        out_kernel,
        [((rows, width), f32), ((rows, width), bf16)],
        info, gated, out_all, inputs, gain_two,
        name="out", micros=0.2,
    )

    second_sib, across, along = (hop(second, bit) for bit in (1, 2, 4))
    half = rows // 2
    top, low = hop(along[:half], 2), hop(across[half:], 4)
    across_sib, along_sib, top_sib, low_sib = (hop(v, 1) for v in (across, along, top, low))
    wide = CUBE * rows // 2
    out_kept, out_given, back_kept, back_given, layer_grads = step(
        layer_kernel,
        [((wide, width), bf16)] * 4 + [((hidden, width), bf16)],
        info, second, second_sib, across, across_sib, along, along_sib, top, low, top_sib, low_sib,
        cot_all, *layer_slots,
        scratch=[((hidden // 2, width), f32)] * 2,
        name="layer", micros=22,
    )
    back_given, out_given, layer_grads = phase(back_given, out_given, layer_grads)
    layer_grads = lax.psum_scatter(layer_grads, "pos", scatter_dimension=0, tiled=True)

    block, part = ((rows, width), bf16), ((half, width), bf16)
    turned = []
    shares = [
        step(share_kernel, [block] * 3 + [part] * 2, kept, hop(given, 1), name="share", micros=0.1)
        for kept, given in ((back_kept, back_given), (out_kept, out_given))
    ]
    for own, across, along, top, low in shares:
        across, along = step(
            turn_kernel, [block] * 2, across, along, hop(top, 2), hop(low, 4), name="turn", micros=0.1
        )
        turned.append([own, hop(across, 2), hop(along, 4)])
    back_parts, out_parts = turned
    grad_res, branch, second_gain_grad, grad_gated = step(
        branch_kernel,
        [((rows, width), f32), ((rows, width), bf16), ((1, width), f32), ((seq_len, channels), bf16)],
        info, *back_parts, residual, gain_two, cot, out_all,
        name="branch", micros=0.2,
    )
    (grad_gated,) = phase(grad_gated, after=[layer_grads])
    grad_gated = to_rows(grad_gated)
    (out_grad,) = step(
        out_grad_kernel, [((CUBE * width, lane), bf16)], gated, branch, name="out_grad", micros=0.1
    )
    (layer_sums,) = step(below_kernel, [((2 * hidden, lane), bf16)], layer_grads, name="layer_sum", micros=0.1)
    (out_grad,) = phase(out_grad, after=[grad_gated])
    out_grad = swap(out_grad)

    grad_projected, grad_taps, small = step(
        back_kernel,
        [((seq_len, 3 * channels), bf16), ((seq_len, channels), f32), ((16, channels), f32)],
        info, grad_gated, projected, long_conv, driven_spectrum, lags, skip, spectrum, turns, *tables,
        name="back", micros=15,
    )
    partial, first_gain_grad = step(
        normed_kernel,
        [((seq_len, width), bf16), ((1, width), f32)],
        info, grad_projected, in_full, *normed_slots, gain_one,
        name="normed", micros=0.2,
    )
    partial, layer_sums = phase(partial, layer_sums, after=[out_grad, *out_parts[1:]])
    grad_normed = lax.psum_scatter(partial, "pos", scatter_dimension=0, tiled=True)
    layer_sums = swap(layer_sums)
    (packed,) = step(
        with_width(pack_kernel),
        [((PACKED, channels), f32)],
        info, grad_taps, filter_hidden, features, times, filter_mid, last_layer, small,
        first_gain_grad, second_gain_grad,
        name="pack", micros=0.1,
    )
    if fold > 1:
        packed = lax.psum(packed, "seq", axis_index_groups=bundles)
    (packed,) = phase(packed)
    (in_grad,) = step(
        in_grad_kernel,
        [((3 * CUBE * channels, lane), bf16)],
        info, grad_projected, *normed_slots,
        name="in_grad", micros=0.1,
    )
    out_slots = step(
        out_sum_kernel, [((channels, lane), t) for t in (f32, bf16, bf16, bf16)], info, out_grad,
        name="out_sum", micros=0.1,
    )
    (block_output,) = step(
        finish_kernel, [((rows, width), bf16)], residual, *out_parts, name="finish", micros=0.1
    )
    for bit in (1, 2, 4):
        packed = packed + hop(packed, bit)
    in_grad, packed, *sent = phase(in_grad, packed, *out_slots[1:], after=[layer_sums])
    in_grad = swap(in_grad)
    out_slots = [out_slots[0]] + [ring(v, j) for j, v in enumerate(sent, 1)]
    up_grad, down_grad = step(
        layer_end_kernel, [((lane, hidden), f32), ((hidden, lane), f32)], layer_sums, name="layer_end"
    )
    packed_slots = [packed, near_ring(packed, 1)]
    packed_slots += [near_ring(v, 2) for v in packed_slots]
    small_grads = step(
        unpack_kernel,
        [
            ((1, width), f32),
            ((1, width), f32),
            ((3, 3 * width), f32),
            ((1, width), f32),
            ((EMB, inner), f32),
            ((1, inner), f32),
            ((inner, inner), f32),
            ((1, inner), f32),
            ((inner, width), f32),
        ],
        info, *packed_slots,
        scratch=[((RING, PACKED, channels), f32)],
        name="unpack",
    )
    (input_grad,) = step(
        end_kernel, [((rows, width), bf16)], grad_normed, inputs, gain_one, grad_res, name="end", micros=4
    )
    (out_grad,) = step(out_end_kernel, [((channels, lane), f32)], *out_slots, name="out_end")
    (in_grad,) = step(in_end_kernel, [((3, lane, channels), f32)], in_grad, name="in_end")
    return (
        block_output,
        input_grad,
        settle(in_grad, 1).transpose(1, 0, 2),
        settle(out_grad, 1),
        settle(up_grad, 0),
        settle(down_grad, 1),
        small_grads[0].reshape(width),
        small_grads[1].reshape(width),
        small_grads[2],
        small_grads[3].reshape(width),
        small_grads[4],
        small_grads[5].reshape(inner),
        small_grads[6],
        small_grads[7].reshape(inner),
        small_grads[8],
    )


def solution(mesh):
    rows = P(("seq", "pos"), None)
    in_place, down_place, up_place = P("seq", None, "pos"), P("pos", "seq"), P("seq", "pos")
    return jax.shard_map(
        on_device,
        mesh=mesh,
        in_specs=(rows, rows, P("seq"), in_place, down_place, up_place, down_place) + (P(),) * 9,
        out_specs=(rows, rows, in_place, down_place, up_place, down_place) + (P(),) * 9,
        check_vma=False,
    )
```

profile of v0, /device:TPU:0, one launch (start us, length us, event | category | flops | bytes accessed | tf_op | source)
XLA Modules:
  0.0 367.5 jit_solution(4342869554916775759)
XLA Ops:
  7.2 1.5 copy.103.refs_1_
  8.7 2.8 rows.1
  11.5 2.1 weights.1
  14.4 5.1 %collective-permute-start = (bf16[256,1024]{1,0:T(8,128)(2,1)}, bf16[256,1024]{1,0:T(8,128)(2,1)S(1)}, u32[]{:S(2)}, u32[]{:S(2)}) collective-permute-start(bf16[256,1024]{1,0:T(8,128)(2,1)} %get-tuple-element.110.refs_3_.refs_1_.refs_2_), channel_id=1, source_target_pairs={{0,3},{1,0},{2,1},{3,2},{4,7},{5,4},{6,5},{7,6},{8,11},{9,8},{10,9... | collective-permute-start | bytes 1572872 | tf_op jit(solution)/shard_map/ppermute | solution.py:621
  19.5 3.7 %all-to-all-start = ((bf16[8,256,128]{2,1,0:T(8,128)(2,1)}), bf16[8,256,128]{2,1,0:T(8,128)(2,1)S(1)}, u32[]{:S(2)}, u32[]{:S(2)}) async-start(bf16[8,256,128]{2,1,0:T(8,128)(2,1)} %bitcast.45), calls=%async_computation | async-start | bytes 1048576 | tf_op jit(solution)/shard_map/all_to_all | solution.py:630
  24.6 5.2 %hidden.1.refs_2_.refs_1_ = f32[1024,256]{1,0:T(8,128)} custom-call(f32[1024,33]{1,0:T(8,128)} %constant.60.clone.refs_0_.refs_3_, f32[33,64]{1,0:T(8,128)} %refs_1_.6, f32[1,64]{1,0:T(1,128)} %bitcast.56, f32[64,64]{1,0:T(8,128)} %refs_5_.2, f32[1,64]{1,0:T(1,128)} %bitcast.57, bf16[768,128]{1,0:T(8,128)(2,1)} %get-tuple-element.111.refs_5_), custom_call_target="tpu_custom_call" | custom-call | flops 5000000000 | bytes 15000000 | tf_op jit(solution)/shard_map/hidden/pallas_call | solution.py:571
  32.4 4.2 %collective-permute-start.1 = (bf16[256,1024]{1,0:T(8,128)(2,1)}, bf16[256,1024]{1,0:T(8,128)(2,1)S(1)}, u32[]{:S(2)}, u32[]{:S(2)}) collective-permute-start(bf16[256,1024]{1,0:T(8,128)(2,1)} %get-tuple-element.112.refs_2_.refs_4_.refs_3_), channel_id=1, source_target_pairs={{0,3},{1,0},{2,1},{3,2},{4,7},{5,4},{6,5},{7,6},{8,11},{9,8},{10,9... | collective-permute-start | bytes 1572872 | tf_op jit(solution)/shard_map/ppermute | solution.py:621
  37.7 3.3 collective-permute-start.2
  41.8 2.0 layer_own.1.refs_13_.refs_0_
  43.7 8.3 %taps.1.refs_5_.refs_8_.refs_7_ = f32[2,1024,256]{2,1,0:T(8,128)} custom-call(s32[4]{0:T(128)} %pad_add_fusion.refs_0_, f32[1024,256]{1,0:T(8,128)} %hidden.1.refs_2_.refs_1_, f32[1024,1]{1,0:T(8,128)} %constant.61.clone.refs_2_.refs_4_, f32[64,256]{1,0:T(8,128)} %constant_dynamic-slice_fusion.refs_3_.refs_6_, f32[2,1024,1]{2,1,0:T(8,128)} %constant.70.clone.refs_4_.refs_8_, ...), custom_call_target="tpu_custom_call" | custom-call | flops 5000000000 | bytes 15000000 | tf_op jit(solution)/shard_map/taps/pallas_call | solution.py:571
  54.1 3.5 collective-permute-start.5
  57.6 10.3 %collective-permute-done.5.refs_6_.refs_4_.refs_5_ = bf16[256,1024]{1,0:T(8,128)(2,1)S(1)} collective-permute-done((bf16[256,1024]{1,0:T(8,128)(2,1)}, bf16[256,1024]{1,0:T(8,128)(2,1)S(1)}, u32[]{:S(2)}, u32[]{:S(2)}) %collective-permute-start.5) | collective-permute-done | bytes 524320 | tf_op jit(solution)/shard_map/ppermute | solution.py:621
  69.4 1.7 pad_maximum_fusion
  73.1 4.3 %collective-permute-start.6 = (bf16[256,1024]{1,0:T(8,128)(2,1)}, bf16[256,1024]{1,0:T(8,128)(2,1)S(1)}, u32[]{:S(2)}, u32[]{:S(2)}) collective-permute-start(bf16[256,1024]{1,0:T(8,128)(2,1)} %get-tuple-element.124.refs_0_), channel_id=1, source_target_pairs={{0,3},{1,0},{2,1},{3,2},{4,7},{5,4},{6,5},{7,6},{8,11},{9,8},{10,9... | collective-permute-start | bytes 1572872 | tf_op jit(solution)/shard_map/ppermute | solution.py:621
  77.4 13.9 %conv.1 = (bf16[1024,768]{1,0:T(8,128)(2,1)}, f32[1024,256]{1,0:T(8,128)}, f32[2,1024,256]{2,1,0:T(8,128)}, bf16[1024,256]{1,0:T(8,128)(2,1)}, bf16[768,1024]{1,0:T(8,128)(2,1)}) custom-call(s32[4]{0:T(128)} %pad_add_fusion.refs_0_, bf16[256,1024]{1,0:T(8,128)(2,1)} %get-tuple-element.110.refs_3_.refs_1_.refs_2_, ...), custom_call_target="tpu_custom_call" | custom-call | flops 14000000000 | bytes 42000000 | tf_op jit(solution)/shard_map/conv/pallas_call | solution.py:571
  92.7 3.5 all-to-all-start.1
  96.2 18.1 %all-gather.8.cloned.1.call-done.refs_4_.refs_2_.refs_7_ = bf16[8192,128]{1,0:T(8,128)(2,1)} async-done(((bf16[1024,128]{1,0:T(8,128)(2,1)}), bf16[8192,128]{1,0:T(8,128)(2,1)}) %all-gather.8.cloned.1.call-update) | async-done | bytes 2097168 | tf_op jit(solution)/shard_map/all_gather | solution.py:633
  115.7 4.3 %out.1 = (f32[256,1024]{1,0:T(8,128)}, bf16[256,1024]{1,0:T(8,128)(2,1)}) custom-call(s32[4]{0:T(128)} %pad_add_fusion.refs_0_, bf16[1024,256]{1,0:T(8,128)(2,1)} %bitcast.35, bf16[8192,128]{1,0:T(8,128)(2,1)} %all-gather.8.cloned.1.call-done.refs_4_.refs_2_.refs_7_, bf16[256,1024]{1,0:T(8,128)(2,1)} %get-tuple-element.132.refs_3_.refs_1_, ...), custom_call_target="tpu_custom_call" | custom-call | flops 200000000 | bytes 600000 | tf_op jit(solution)/shard_map/out/pallas_call | solution.py:571
  120.0 1.4 collective-permute-start.10
  122.0 1.5 collective-permute-start.17
  123.5 2.7 collective-permute-start.16
  126.3 8.1 %collective-permute-done.10.refs_5_ = bf16[256,1024]{1,0:T(8,128)(2,1)S(1)} collective-permute-done((bf16[256,1024]{1,0:T(8,128)(2,1)}, bf16[256,1024]{1,0:T(8,128)(2,1)S(1)}, u32[]{:S(2)}, u32[]{:S(2)}) %collective-permute-start.10) | collective-permute-done | bytes 524320 | tf_op jit(solution)/shard_map/ppermute | solution.py:618
  134.3 1.5 collective-permute-start.12
  136.5 2.2 collective-permute-done.17.refs_15_
  138.7 9.7 %collective-permute-done.16.refs_14_ = bf16[256,1024]{1,0:T(8,128)(2,1)S(1)} collective-permute-done((bf16[256,1024]{1,0:T(8,128)(2,1)S(1)}, bf16[256,1024]{1,0:T(8,128)(2,1)S(1)}, u32[]{:S(2)}, u32[]{:S(2)}) %collective-permute-start.16) | collective-permute-done | bytes 524320 | tf_op jit(solution)/shard_map/ppermute | solution.py:621
  149.0 1.7 collective-permute-done.14.refs_9_
  151.9 20.5 %layer.1 = (bf16[1024,1024]{1,0:T(8,128)(2,1)}, bf16[1024,1024]{1,0:T(8,128)(2,1)}, bf16[1024,1024]{1,0:T(8,128)(2,1)}, bf16[1024,1024]{1,0:T(8,128)(2,1)}, bf16[1024,1024]{1,0:T(8,128)(2,1)}) custom-call(s32[4]{0:T(128)} %pad_add_fusion.refs_0_, bf16[256,1024]{1,0:T(8,128)(2,1)} %get-tuple-element.137.refs_1_, bf16[256,1024]{1,0:T(8,128)(2,1)} %copy-done.37, ...), custom_call_target="tpu_custom_call" | custom-call | flops 22000001024 | bytes 66000000 | tf_op jit(solution)/shard_map/layer/pallas_call | solution.py:571
  174.7 2.7 collective-permute-done.19.refs_1_
  178.8 3.6 share.2
  185.8 3.7 %share.3 = (bf16[256,1024]{1,0:T(8,128)(2,1)}, bf16[256,1024]{1,0:T(8,128)(2,1)}, bf16[256,1024]{1,0:T(8,128)(2,1)}, bf16[128,1024]{1,0:T(8,128)(2,1)}, bf16[128,1024]{1,0:T(8,128)(2,1)}) custom-call(bf16[1024,1024]{1,0:T(8,128)(2,1)} %get-tuple-element.140.refs_3_.refs_0_, bf16[1024,1024]{1,0:T(8,128)(2,1)} %copy-done.9, ...), custom_call_target="tpu_custom_call" | custom-call | flops 100000000 | bytes 300000 | tf_op jit(solution)/shard_map/share/pallas_call | solution.py:571
  189.5 1.5 collective-permute-done.22.refs_2_
  192.8 2.4 turn.2
  199.3 15.2 %collective-permute-done.20.refs_2_ = bf16[128,1024]{1,0:T(8,128)(2,1)S(1)} collective-permute-done((bf16[128,1024]{1,0:T(8,128)(2,1)S(1)}, bf16[128,1024]{1,0:T(8,128)(2,1)S(1)}, u32[]{:S(2)}, u32[]{:S(2)}) %collective-permute-start.20) | collective-permute-done | bytes 262176 | tf_op jit(solution)/shard_map/ppermute | solution.py:618
  215.2 2.4 turn.3
  218.6 5.4 %branch.1 = (f32[256,1024]{1,0:T(8,128)}, bf16[256,1024]{1,0:T(8,128)(2,1)}, f32[1,1024]{1,0:T(1,128)}, bf16[1024,256]{1,0:T(8,128)(2,1)}) custom-call(s32[4]{0:T(128)} %pad_add_fusion.refs_0_, bf16[256,1024]{1,0:T(8,128)(2,1)} %get-tuple-element.148.refs_2_.refs_1_, bf16[256,1024]{1,0:T(8,128)(2,1)} %copy-done.24, bf16[256,1024]{1,0:T(8,128)(2,1)} %copy-done.23, ...), custom_call_target="tpu_custom_call" | custom-call | flops 200000000 | bytes 600000 | tf_op jit(solution)/shard_map/branch/pallas_call | solution.py:571
  224.7 3.5 all-to-all-start.2
  228.1 3.2 out_grad.1.refs_1_.refs_0_
  231.4 1.9 layer_sum.1.refs_1_
  233.3 7.7 %all-to-all-done.2 = bf16[4,256,256]{2,1,0:T(8,128)(2,1)S(1)} async-done(((bf16[4,256,256]{2,1,0:T(8,128)(2,1)}), bf16[4,256,256]{2,1,0:T(8,128)(2,1)S(1)}, u32[]{:S(2)}, u32[]{:S(2)}) %all-to-all-start.2) | async-done | bytes 524320 | tf_op jit(solution)/shard_map/all_to_all | solution.py:627
  242.4 3.6 all-to-all-start.3
  246.0 1.9 collective-permute-start.24
  247.9 1.5 collective-permute-start.25
  249.4 15.4 %back.1 = (bf16[1024,768]{1,0:T(8,128)(2,1)}, f32[1024,256]{1,0:T(8,128)}, f32[16,256]{1,0:T(8,128)}) custom-call(s32[4]{0:T(128)} %pad_add_fusion.refs_0_, bf16[1024,256]{1,0:T(8,128)(2,1)} %bitcast.41, bf16[1024,768]{1,0:T(8,128)(2,1)} %get-tuple-element.125.refs_2_, f32[1024,256]{1,0:T(8,128)} %get-tuple-element.169.refs_3_, ...), custom_call_target="tpu_custom_call" | custom-call | flops 15000000512 | bytes 45000000 | tf_op jit(solution)/shard_map/back/pallas_call | solution.py:571
  264.8 5.6 %normed.1 = (bf16[1024,1024]{1,0:T(8,128)(2,1)}, f32[1,1024]{1,0:T(1,128)}) custom-call(s32[4]{0:T(128)} %pad_add_fusion.refs_0_, bf16[1024,768]{1,0:T(8,128)(2,1)} %get-tuple-element.172.refs_1_, bf16[768,1024]{1,0:T(8,128)(2,1)} %get-tuple-element.175.refs_2_, bf16[256,1024]{1,0:T(8,128)(2,1)} %get-tuple-element.110.refs_3_.refs_1_.refs_2_, ...), custom_call_target="tpu_custom_call" | custom-call | flops 200000000 | bytes 600000 | tf_op jit(solution)/shard_map/normed/pallas_call | solution.py:571
  270.4 12.4 %collective-permute-done.25.refs_4_.refs_3_ = bf16[256,1024]{1,0:T(8,128)(2,1)S(1)} collective-permute-done((bf16[256,1024]{1,0:T(8,128)(2,1)}, bf16[256,1024]{1,0:T(8,128)(2,1)S(1)}, u32[]{:S(2)}, u32[]{:S(2)}) %collective-permute-start.25) | collective-permute-done | bytes 524320 | tf_op jit(solution)/shard_map/ppermute | solution.py:618
  285.1 6.2 %pack.1.refs_0_ = f32[152,256]{1,0:T(8,128)} custom-call(s32[4]{0:T(128)} %pad_add_fusion.refs_0_, f32[1024,256]{1,0:T(8,128)} %get-tuple-element.173.refs_1_, f32[1024,256]{1,0:T(8,128)} %hidden.1.refs_2_.refs_1_, f32[1024,33]{1,0:T(8,128)} %constant.60.clone.refs_0_.refs_3_, f32[1024,1]{1,0:T(8,128)} %constant.61.clone.refs_2_.refs_4_, f32[64,64]{1,0:T(8,128)} %refs_5_.2, ...), custom_call_target="tpu_custom_call" | custom-call | flops 100000000 | bytes 300000 | tf_op jit(solution)/shard_map/pack/pallas_call | solution.py:571
  291.9 3.5 all-to-all-start.4
  296.3 2.0 collective-permute-start.29
  298.3 9.1 %collective-permute-done.29 = f32[152,256]{1,0:T(8,128)S(1)} collective-permute-done((f32[152,256]{1,0:T(8,128)S(1)}, f32[152,256]{1,0:T(8,128)S(1)}, u32[]{:S(2)}, u32[]{:S(2)}) %collective-permute-start.29) | collective-permute-done | bytes 155680 | tf_op jit(solution)/shard_map/ppermute | solution.py:618
  307.5 1.6 collective-permute-start.30
  309.0 5.0 %in_grad.1.refs_2_.refs_0_ = bf16[6144,128]{1,0:T(8,128)(2,1)} custom-call(s32[4]{0:T(128)} %pad_add_fusion.refs_0_, bf16[1024,768]{1,0:T(8,128)(2,1)} %get-tuple-element.172.refs_1_, bf16[256,1024]{1,0:T(8,128)(2,1)} %get-tuple-element.110.refs_3_.refs_1_.refs_2_, bf16[256,1024]{1,0:T(8,128)(2,1)} %get-tuple-element.112.refs_2_.refs_4_.refs_3_, ...), custom_call_target="tpu_custom_call" | custom-call | flops 100000000 | bytes 300000 | tf_op jit(solution)/shard_map/in_grad/pallas_call | solution.py:571
  314.1 2.5 out_sum.1
  316.6 3.0 finish.1.refs_5_
  321.6 3.7 %all-to-all-start.5 = ((bf16[8,768,128]{2,1,0:T(8,128)(2,1)}), bf16[8,768,128]{2,1,0:T(8,128)(2,1)S(1)}, u32[]{:S(2)}, u32[]{:S(2)}) async-start(bf16[8,768,128]{2,1,0:T(8,128)(2,1)} %bitcast.31), calls=%async_computation.7 | async-start | bytes 3145728 | tf_op jit(solution)/shard_map/all_to_all | solution.py:630
  325.4 2.0 collective-permute-start.32
  327.5 2.9 collective-permute-start.35
  331.4 3.0 collective-permute-done.31.refs_2_
  334.7 2.1 layer_end.1
  336.8 5.9 %collective-permute-done.32.refs_3_ = f32[152,256]{1,0:T(8,128)S(1)} collective-permute-done((f32[152,256]{1,0:T(8,128)S(1)}, f32[152,256]{1,0:T(8,128)S(1)}, u32[]{:S(2)}, u32[]{:S(2)}) %collective-permute-start.32) | collective-permute-done | bytes 155680 | tf_op jit(solution)/shard_map/ppermute | solution.py:624
  342.8 5.5 %collective-permute-done.33.refs_4_ = f32[152,256]{1,0:T(8,128)S(1)} collective-permute-done((f32[152,256]{1,0:T(8,128)S(1)}, f32[152,256]{1,0:T(8,128)S(1)}, u32[]{:S(2)}, u32[]{:S(2)}) %collective-permute-start.33) | collective-permute-done | bytes 155680 | tf_op jit(solution)/shard_map/ppermute | solution.py:624
  349.0 2.0 unpack.1
  350.9 3.3 end.1.refs_4_
  355.6 1.6 out_end.1.refs_1_
  358.4 2.4 in_end.1
  (191 shorter events, 44.4 us)
Async XLA Ops:
  7.2 16.1 %copy-start = (f32[64,1024]{1,0:T(8,128)S(1)}, f32[64,1024]{1,0:T(8,128)}, u32[]{:S(2)}) copy-start(f32[64,1024]{1,0:T(8,128)} %param.42) | copy-start | bytes 786436
  7.2 70.2 %all-gather.4.cloned.1.call-start = ((), (), s32[]{:S(2)}) async-start(), calls=%async_computation.8 | async-start | bytes 1769472 | tf_op jit(solution)/shard_map/all_gather | solution.py:633
  13.6 77.7 %all-gather.6.cloned.1.call-start = ((), (), s32[]{:S(2)}) async-start(), calls=%async_computation.9 | async-start | bytes 4718592 | tf_op jit(solution)/shard_map/all_gather | solution.py:633
  14.4 16.6 %collective-permute-start = (bf16[256,1024]{1,0:T(8,128)(2,1)}, bf16[256,1024]{1,0:T(8,128)(2,1)S(1)}, u32[]{:S(2)}, u32[]{:S(2)}) collective-permute-start(bf16[256,1024]{1,0:T(8,128)(2,1)} %get-tuple-element.110.refs_3_.refs_1_.refs_2_), channel_id=1, source_target_pairs={{0,3},{1,0},{2,1},{3,2},{4,7},{5,4},{6,5},{7,6},{8,11},{9,8},{10,9... | collective-permute-start | bytes 1572872 | tf_op jit(solution)/shard_map/ppermute | solution.py:621
  19.5 21.5 %all-to-all-start = ((bf16[8,256,128]{2,1,0:T(8,128)(2,1)}), bf16[8,256,128]{2,1,0:T(8,128)(2,1)S(1)}, u32[]{:S(2)}, u32[]{:S(2)}) async-start(bf16[8,256,128]{2,1,0:T(8,128)(2,1)} %bitcast.45), calls=%async_computation | async-start | bytes 1048576 | tf_op jit(solution)/shard_map/all_to_all | solution.py:630
  23.2 91.1 %all-gather.8.cloned.1.call-start = ((), (), s32[]{:S(2)}) async-start(), calls=%async_computation.10 | async-start | bytes 2359296 | tf_op jit(solution)/shard_map/all_gather | solution.py:633
  32.4 19.8 %collective-permute-start.1 = (bf16[256,1024]{1,0:T(8,128)(2,1)}, bf16[256,1024]{1,0:T(8,128)(2,1)S(1)}, u32[]{:S(2)}, u32[]{:S(2)}) collective-permute-start(bf16[256,1024]{1,0:T(8,128)(2,1)} %get-tuple-element.112.refs_2_.refs_4_.refs_3_), channel_id=1, source_target_pairs={{0,3},{1,0},{2,1},{3,2},{4,7},{5,4},{6,5},{7,6},{8,11},{9,8},{10,9... | collective-permute-start | bytes 1572872 | tf_op jit(solution)/shard_map/ppermute | solution.py:621
  37.1 14.9 %collective-permute-start.4 = (bf16[256,128]{1,0:T(8,128)(2,1)}, bf16[256,128]{1,0:T(8,128)(2,1)S(1)}, u32[]{:S(2)}, u32[]{:S(2)}) collective-permute-start(bf16[256,128]{1,0:T(8,128)(2,1)} %get-tuple-element.113.refs_1_), channel_id=1, source_target_pairs={{0,1},{1,2},{2,3},{3,0},{4,5},{5,6},{6,7},{7,4},{8,9},{9,10},{10,1... | collective-permute-start | bytes 196616 | tf_op jit(solution)/shard_map/ppermute | solution.py:621
  37.1 15.0 %collective-permute-start.3 = (bf16[256,128]{1,0:T(8,128)(2,1)}, bf16[256,128]{1,0:T(8,128)(2,1)S(1)}, u32[]{:S(2)}, u32[]{:S(2)}) collective-permute-start(bf16[256,128]{1,0:T(8,128)(2,1)} %get-tuple-element.113.refs_1_), channel_id=1, source_target_pairs={{0,2},{1,3},{2,0},{3,1},{4,6},{5,7},{6,4},{7,5},{8,10},{9,11},{10,... | collective-permute-start | bytes 196616 | tf_op jit(solution)/shard_map/ppermute | solution.py:621
  37.7 14.4 %collective-permute-start.2 = (bf16[256,128]{1,0:T(8,128)(2,1)}, bf16[256,128]{1,0:T(8,128)(2,1)S(1)}, u32[]{:S(2)}, u32[]{:S(2)}) collective-permute-start(bf16[256,128]{1,0:T(8,128)(2,1)} %get-tuple-element.113.refs_1_), channel_id=1, source_target_pairs={{0,3},{1,0},{2,1},{3,2},{4,7},{5,4},{6,5},{7,6},{8,11},{9,8},{10,9... | collective-permute-start | bytes 196616 | tf_op jit(solution)/shard_map/ppermute | solution.py:621
  52.1 20.3 %copy-start.34 = (f32[3,3072]{1,0:T(4,128)S(1)}, f32[3,3072]{1,0:T(4,128)}, u32[]{:S(2)}) copy-start(f32[3,3072]{1,0:T(4,128)} %param.36) | copy-start | bytes 110596
  54.1 13.8 %collective-permute-start.5 = (bf16[256,1024]{1,0:T(8,128)(2,1)}, bf16[256,1024]{1,0:T(8,128)(2,1)S(1)}, u32[]{:S(2)}, u32[]{:S(2)}) collective-permute-start(bf16[256,1024]{1,0:T(8,128)(2,1)} %get-tuple-element.116.refs_3_.refs_5_.refs_4_), channel_id=1, source_target_pairs={{0,3},{1,0},{2,1},{3,2},{4,7},{5,4},{6,5},{7,6},{8,11},{9,8},{10,9... | collective-permute-start | bytes 1572872 | tf_op jit(solution)/shard_map/ppermute | solution.py:621
  73.1 18.2 %collective-permute-start.6 = (bf16[256,1024]{1,0:T(8,128)(2,1)}, bf16[256,1024]{1,0:T(8,128)(2,1)S(1)}, u32[]{:S(2)}, u32[]{:S(2)}) collective-permute-start(bf16[256,1024]{1,0:T(8,128)(2,1)} %get-tuple-element.124.refs_0_), channel_id=1, source_target_pairs={{0,3},{1,0},{2,1},{3,2},{4,7},{5,4},{6,5},{7,6},{8,11},{9,8},{10,9... | collective-permute-start | bytes 1572872 | tf_op jit(solution)/shard_map/ppermute | solution.py:621
  92.7 21.6 %all-to-all-start.1 = ((bf16[4,256,256]{2,1,0:T(8,128)(2,1)}), bf16[4,256,256]{2,1,0:T(8,128)(2,1)S(1)}, u32[]{:S(2)}, u32[]{:S(2)}) async-start(bf16[4,256,256]{2,1,0:T(8,128)(2,1)} %bitcast.43), calls=%async_computation.1 | async-start | bytes 1048576 | tf_op jit(solution)/shard_map/all_to_all | solution.py:627
  96.2 127.9 %reduce-scatter.3.cloned.1.call-start = ((), (), s32[]{:S(2)}) async-start(), calls=%async_computation.11 | async-start | bytes 2621440 | tf_op jit(solution)/shard_map/reduce_scatter | solution.py:776
  115.7 6.3 %copy-start.7 = (bf16[256,1024]{1,0:T(8,128)(2,1)S(1)}, bf16[256,1024]{1,0:T(8,128)(2,1)}, u32[]{:S(2)}) copy-start(bf16[256,1024]{1,0:T(8,128)(2,1)} %get-tuple-element.138.refs_12_) | copy-start | bytes 1572868
  115.7 7.8 %copy-start.17 = (bf16[256,1024]{1,0:T(8,128)(2,1)S(1)}, bf16[256,1024]{1,0:T(8,128)(2,1)}, u32[]{:S(2)}) copy-start(bf16[256,1024]{1,0:T(8,128)(2,1)} %get-tuple-element.139.refs_13_) | copy-start | bytes 1572868
  120.0 14.3 %collective-permute-start.10 = (bf16[256,1024]{1,0:T(8,128)(2,1)}, bf16[256,1024]{1,0:T(8,128)(2,1)S(1)}, u32[]{:S(2)}, u32[]{:S(2)}) collective-permute-start(bf16[256,1024]{1,0:T(8,128)(2,1)} %get-tuple-element.137.refs_1_), channel_id=1, source_target_pairs={{0,16},{4,20},{8,24},{12,28},{16,0},{20,4},{24,8},{28,12},{1,17},{... | collective-permute-start | bytes 1572872 | tf_op jit(solution)/shard_map/ppermute | solution.py:618
  121.4 14.5 %collective-permute-start.8 = (bf16[256,1024]{1,0:T(8,128)(2,1)}, bf16[256,1024]{1,0:T(8,128)(2,1)S(1)}, u32[]{:S(2)}, u32[]{:S(2)}) collective-permute-start(bf16[256,1024]{1,0:T(8,128)(2,1)} %get-tuple-element.137.refs_1_), channel_id=1, source_target_pairs={{0,8},{4,12},{8,0},{12,4},{16,24},{20,28},{24,16},{28,20},{1,9},{5... | collective-permute-start | bytes 1572872 | tf_op jit(solution)/shard_map/ppermute | solution.py:618
  122.0 16.7 %collective-permute-start.17 = (bf16[256,1024]{1,0:T(8,128)(2,1)S(1)}, bf16[256,1024]{1,0:T(8,128)(2,1)S(1)}, u32[]{:S(2)}, u32[]{:S(2)}) collective-permute-start(bf16[256,1024]{1,0:T(8,128)(2,1)S(1)} %copy-done.7), channel_id=1, source_target_pairs={{0,1},{1,2},{2,3},{3,0},{4,5},{5,6},{6,7},{7,4},{8,9},{9,10},{10,1... | collective-permute-start | bytes 1572872 | tf_op jit(solution)/shard_map/ppermute | solution.py:621
  123.5 24.9 %collective-permute-start.16 = (bf16[256,1024]{1,0:T(8,128)(2,1)S(1)}, bf16[256,1024]{1,0:T(8,128)(2,1)S(1)}, u32[]{:S(2)}, u32[]{:S(2)}) collective-permute-start(bf16[256,1024]{1,0:T(8,128)(2,1)S(1)} %copy-done.17), channel_id=1, source_target_pairs={{0,3},{1,0},{2,1},{3,2},{4,7},{5,4},{6,5},{7,6},{8,11},{9,8},{10,9... | collective-permute-start | bytes 1572872 | tf_op jit(solution)/shard_map/ppermute | solution.py:621
  126.2 22.8 %collective-permute-start.7 = (bf16[256,1024]{1,0:T(8,128)(2,1)}, bf16[256,1024]{1,0:T(8,128)(2,1)S(1)}, u32[]{:S(2)}, u32[]{:S(2)}) collective-permute-start(bf16[256,1024]{1,0:T(8,128)(2,1)} %get-tuple-element.137.refs_1_), channel_id=1, source_target_pairs={{0,4},{4,0},{8,12},{12,8},{16,20},{20,16},{24,28},{28,24},{1,5},{5... | collective-permute-start | bytes 1572872 | tf_op jit(solution)/shard_map/ppermute | solution.py:618
  134.3 16.8 %copy-start.29 = (bf16[256,1024]{1,0:T(8,128)(2,1)}, bf16[256,1024]{1,0:T(8,128)(2,1)S(1)}, u32[]{:S(2)}) copy-start(bf16[256,1024]{1,0:T(8,128)(2,1)S(1)} %collective-permute-done.10.refs_5_) | copy-start | bytes 1572868
  134.3 14.1 %collective-permute-start.12 = (bf16[128,1024]{1,0:T(8,128)(2,1)S(1)}, bf16[128,1024]{1,0:T(8,128)(2,1)S(1)}, u32[]{:S(2)}, u32[]{:S(2)}) collective-permute-start(bf16[128,1024]{1,0:T(8,128)(2,1)S(1)} %slice.8), channel_id=1, source_target_pairs={{0,8},{4,12},{8,0},{12,4},{16,24},{20,28},{24,16},{28,20},{1,9},{5... | collective-permute-start | bytes 786440 | tf_op jit(solution)/shard_map/ppermute | solution.py:618
  135.9 15.2 %copy-start.30 = (bf16[256,1024]{1,0:T(8,128)(2,1)}, bf16[256,1024]{1,0:T(8,128)(2,1)S(1)}, u32[]{:S(2)}) copy-start(bf16[256,1024]{1,0:T(8,128)(2,1)S(1)} %collective-permute-done.8.refs_3_) | copy-start | bytes 1572868
  135.9 13.0 %collective-permute-start.13 = (bf16[128,1024]{1,0:T(8,128)(2,1)S(1)}, bf16[128,1024]{1,0:T(8,128)(2,1)S(1)}, u32[]{:S(2)}, u32[]{:S(2)}) collective-permute-start(bf16[128,1024]{1,0:T(8,128)(2,1)S(1)} %slice.9), channel_id=1, source_target_pairs={{0,16},{4,20},{8,24},{12,28},{16,0},{20,4},{24,8},{28,12},{1,17},{... | collective-permute-start | bytes 786440 | tf_op jit(solution)/shard_map/ppermute | solution.py:618
  138.7 12.4 %copy-start.35 = (bf16[256,1024]{1,0:T(8,128)(2,1)}, bf16[256,1024]{1,0:T(8,128)(2,1)S(1)}, u32[]{:S(2)}) copy-start(bf16[256,1024]{1,0:T(8,128)(2,1)S(1)} %collective-permute-done.17.refs_15_) | copy-start | bytes 1572868
  138.7 12.0 %collective-permute-start.11 = (bf16[256,1024]{1,0:T(8,128)(2,1)S(1)}, bf16[256,1024]{1,0:T(8,128)(2,1)S(1)}, u32[]{:S(2)}, u32[]{:S(2)}) collective-permute-start(bf16[256,1024]{1,0:T(8,128)(2,1)S(1)} %collective-permute-done.10.refs_5_), channel_id=1, source_target_pairs={{0,4},{4,0},{8,12},{12,8},{16,20},{20,16},{24,28},{28,24},{1,5},{5... | collective-permute-start | bytes 1572872 | tf_op jit(solution)/shard_map/ppermute | solution.py:618
  148.4 2.7 copy-start.36
  148.4 2.7 collective-permute-start.9
  148.4 2.3 collective-permute-start.14
  148.9 2.1 collective-permute-start.15
  173.0 4.4 %collective-permute-start.19 = (bf16[1024,1024]{1,0:T(8,128)(2,1)}, bf16[1024,1024]{1,0:T(8,128)(2,1)S(1)}, u32[]{:S(2)}, u32[]{:S(2)}) collective-permute-start(bf16[1024,1024]{1,0:T(8,128)(2,1)} %get-tuple-element.146), channel_id=1, source_target_pairs={{0,4},{4,0},{8,12},{12,8},{16,20},{20,16},{24,28},{28,24},{1,5},{5... | collective-permute-start | bytes 6291464 | tf_op jit(solution)/shard_map/ppermute | solution.py:618
  174.6 9.9 %collective-permute-start.18 = (bf16[1024,1024]{1,0:T(8,128)(2,1)S(1)}, bf16[1024,1024]{1,0:T(8,128)(2,1)S(1)}, u32[]{:S(2)}, u32[]{:S(2)}) collective-permute-start(bf16[1024,1024]{1,0:T(8,128)(2,1)S(1)} %copy-done.13), channel_id=1, source_target_pairs={{0,4},{4,0},{8,12},{12,8},{16,20},{20,16},{24,28},{28,24},{1,5},{5... | collective-permute-start | bytes 6291464 | tf_op jit(solution)/shard_map/ppermute | solution.py:618
  182.4 8.6 %collective-permute-start.22 = (bf16[128,1024]{1,0:T(8,128)(2,1)}, bf16[128,1024]{1,0:T(8,128)(2,1)S(1)}, u32[]{:S(2)}, u32[]{:S(2)}) collective-permute-start(bf16[128,1024]{1,0:T(8,128)(2,1)} %get-tuple-element.156), channel_id=1, source_target_pairs={{0,8},{4,12},{8,0},{12,4},{16,24},{20,28},{24,16},{28,20},{1,9},{5... | collective-permute-start | bytes 786440 | tf_op jit(solution)/shard_map/ppermute | solution.py:618
  183.8 8.3 %collective-permute-start.23 = (bf16[128,1024]{1,0:T(8,128)(2,1)}, bf16[128,1024]{1,0:T(8,128)(2,1)S(1)}, u32[]{:S(2)}, u32[]{:S(2)}) collective-permute-start(bf16[128,1024]{1,0:T(8,128)(2,1)} %get-tuple-element.157), channel_id=1, source_target_pairs={{0,16},{4,20},{8,24},{12,28},{16,0},{20,4},{24,8},{28,12},{1,17},{... | collective-permute-start | bytes 786440 | tf_op jit(solution)/shard_map/ppermute | solution.py:618
  189.5 7.8 %copy-start.44 = (bf16[128,1024]{1,0:T(8,128)(2,1)S(1)}, bf16[128,1024]{1,0:T(8,128)(2,1)}, u32[]{:S(2)}) copy-start(bf16[128,1024]{1,0:T(8,128)(2,1)} %get-tuple-element.152) | copy-start | bytes 786436
  189.5 8.5 %copy-start.43 = (bf16[128,1024]{1,0:T(8,128)(2,1)S(1)}, bf16[128,1024]{1,0:T(8,128)(2,1)}, u32[]{:S(2)}) copy-start(bf16[128,1024]{1,0:T(8,128)(2,1)} %get-tuple-element.153) | copy-start | bytes 786436
  195.2 22.4 %collective-permute-start.27 = (bf16[256,1024]{1,0:T(8,128)(2,1)}, bf16[256,1024]{1,0:T(8,128)(2,1)S(1)}, u32[]{:S(2)}, u32[]{:S(2)}) collective-permute-start(bf16[256,1024]{1,0:T(8,128)(2,1)} %get-tuple-element.161), channel_id=1, source_target_pairs={{0,16},{4,20},{8,24},{12,28},{16,0},{20,4},{24,8},{28,12},{1,17},{... | collective-permute-start | bytes 1572872 | tf_op jit(solution)/shard_map/ppermute | solution.py:618
  195.9 21.7 %collective-permute-start.26 = (bf16[256,1024]{1,0:T(8,128)(2,1)}, bf16[256,1024]{1,0:T(8,128)(2,1)S(1)}, u32[]{:S(2)}, u32[]{:S(2)}) collective-permute-start(bf16[256,1024]{1,0:T(8,128)(2,1)} %get-tuple-element.158.refs_4_), channel_id=1, source_target_pairs={{0,8},{4,12},{8,0},{12,4},{16,24},{20,28},{24,16},{28,20},{1,9},{5... | collective-permute-start | bytes 1572872 | tf_op jit(solution)/shard_map/ppermute | solution.py:618
  197.3 17.1 %collective-permute-start.20 = (bf16[128,1024]{1,0:T(8,128)(2,1)S(1)}, bf16[128,1024]{1,0:T(8,128)(2,1)S(1)}, u32[]{:S(2)}, u32[]{:S(2)}) collective-permute-start(bf16[128,1024]{1,0:T(8,128)(2,1)S(1)} %copy-done.44), channel_id=1, source_target_pairs={{0,8},{4,12},{8,0},{12,4},{16,24},{20,28},{24,16},{28,20},{1,9},{5... | collective-permute-start | bytes 786440 | tf_op jit(solution)/shard_map/ppermute | solution.py:618
  198.0 16.5 %collective-permute-start.21 = (bf16[128,1024]{1,0:T(8,128)(2,1)S(1)}, bf16[128,1024]{1,0:T(8,128)(2,1)S(1)}, u32[]{:S(2)}, u32[]{:S(2)}) collective-permute-start(bf16[128,1024]{1,0:T(8,128)(2,1)S(1)} %copy-done.43), channel_id=1, source_target_pairs={{0,16},{4,20},{8,24},{12,28},{16,0},{20,4},{24,8},{28,12},{1,17},{... | collective-permute-start | bytes 786440 | tf_op jit(solution)/shard_map/ppermute | solution.py:618
  224.7 16.3 %all-to-all-start.2 = ((bf16[4,256,256]{2,1,0:T(8,128)(2,1)}), bf16[4,256,256]{2,1,0:T(8,128)(2,1)S(1)}, u32[]{:S(2)}, u32[]{:S(2)}) async-start(bf16[4,256,256]{2,1,0:T(8,128)(2,1)} %bitcast.42), calls=%async_computation.3 | async-start | bytes 1048576 | tf_op jit(solution)/shard_map/all_to_all | solution.py:627
  242.4 40.5 %all-to-all-start.3 = ((bf16[8,1024,128]{2,1,0:T(8,128)(2,1)}), bf16[8,1024,128]{2,1,0:T(8,128)(2,1)S(1)}, u32[]{:S(2)}, u32[]{:S(2)}) async-start(bf16[8,1024,128]{2,1,0:T(8,128)(2,1)} %bitcast.30), calls=%async_computation.4 | async-start | bytes 4194304 | tf_op jit(solution)/shard_map/all_to_all | solution.py:630
  246.0 105.0 %reduce-scatter.5.cloned.1.call-start = ((), (), s32[]{:S(2)}) async-start(), calls=%async_computation.12 | async-start | bytes 2621440 | tf_op jit(solution)/shard_map/reduce_scatter | solution.py:818
  246.0 36.9 %collective-permute-start.24 = (bf16[256,1024]{1,0:T(8,128)(2,1)}, bf16[256,1024]{1,0:T(8,128)(2,1)S(1)}, u32[]{:S(2)}, u32[]{:S(2)}) collective-permute-start(bf16[256,1024]{1,0:T(8,128)(2,1)} %get-tuple-element.159.refs_8_), channel_id=1, source_target_pairs={{0,8},{4,12},{8,0},{12,4},{16,24},{20,28},{24,16},{28,20},{1,9},{5... | collective-permute-start | bytes 1572872 | tf_op jit(solution)/shard_map/ppermute | solution.py:618
  247.9 34.9 %collective-permute-start.25 = (bf16[256,1024]{1,0:T(8,128)(2,1)}, bf16[256,1024]{1,0:T(8,128)(2,1)S(1)}, u32[]{:S(2)}, u32[]{:S(2)}) collective-permute-start(bf16[256,1024]{1,0:T(8,128)(2,1)} %get-tuple-element.160), channel_id=1, source_target_pairs={{0,16},{4,20},{8,24},{12,28},{16,0},{20,4},{24,8},{28,12},{1,17},{... | collective-permute-start | bytes 1572872 | tf_op jit(solution)/shard_map/ppermute | solution.py:618
  291.9 3.5 collective-permute-start.28
  291.9 28.3 %all-to-all-start.4 = ((bf16[8,256,128]{2,1,0:T(8,128)(2,1)}), bf16[8,256,128]{2,1,0:T(8,128)(2,1)S(1)}, u32[]{:S(2)}, u32[]{:S(2)}) async-start(bf16[8,256,128]{2,1,0:T(8,128)(2,1)} %bitcast.17), calls=%async_computation.6 | async-start | bytes 1048576 | tf_op jit(solution)/shard_map/all_to_all | solution.py:630
  296.3 11.1 %collective-permute-start.29 = (f32[152,256]{1,0:T(8,128)S(1)}, f32[152,256]{1,0:T(8,128)S(1)}, u32[]{:S(2)}, u32[]{:S(2)}) collective-permute-start(f32[152,256]{1,0:T(8,128)S(1)} %add.25), channel_id=1, source_target_pairs={{0,8},{4,12},{8,0},{12,4},{16,24},{20,28},{24,16},{28,20},{1,9},{5... | collective-permute-start | bytes 466952 | tf_op jit(solution)/shard_map/ppermute | solution.py:618
  307.5 12.0 %collective-permute-start.30 = (f32[152,256]{1,0:T(8,128)S(1)}, f32[152,256]{1,0:T(8,128)S(1)}, u32[]{:S(2)}, u32[]{:S(2)}) collective-permute-start(f32[152,256]{1,0:T(8,128)S(1)} %add.26), channel_id=1, source_target_pairs={{0,16},{4,20},{8,24},{12,28},{16,0},{20,4},{24,8},{28,12},{1,17},{... | collective-permute-start | bytes 466952 | tf_op jit(solution)/shard_map/ppermute | solution.py:618
  321.6 3.8 %copy-start.19 = (f32[152,256]{1,0:T(8,128)S(1)}, f32[152,256]{1,0:T(8,128)}, u32[]{:S(2)}) copy-start(f32[152,256]{1,0:T(8,128)} %get-tuple-element.188.refs_1_) | copy-start | bytes 466948
  321.6 5.8 %copy-start.31 = (bf16[256,128]{1,0:T(8,128)(2,1)S(1)}, bf16[256,128]{1,0:T(8,128)(2,1)}, u32[]{:S(2)}) copy-start(bf16[256,128]{1,0:T(8,128)(2,1)} %get-tuple-element.193) | copy-start | bytes 196612
  321.6 5.9 %copy-start.32 = (bf16[256,128]{1,0:T(8,128)(2,1)S(1)}, bf16[256,128]{1,0:T(8,128)(2,1)}, u32[]{:S(2)}) copy-start(bf16[256,128]{1,0:T(8,128)(2,1)} %get-tuple-element.194) | copy-start | bytes 196612
  321.6 8.8 %copy-start.33 = (bf16[256,128]{1,0:T(8,128)(2,1)S(1)}, bf16[256,128]{1,0:T(8,128)(2,1)}, u32[]{:S(2)}) copy-start(bf16[256,128]{1,0:T(8,128)(2,1)} %get-tuple-element.195) | copy-start | bytes 196612
  321.6 35.6 %all-to-all-start.5 = ((bf16[8,768,128]{2,1,0:T(8,128)(2,1)}), bf16[8,768,128]{2,1,0:T(8,128)(2,1)S(1)}, u32[]{:S(2)}, u32[]{:S(2)}) async-start(bf16[8,768,128]{2,1,0:T(8,128)(2,1)} %bitcast.31), calls=%async_computation.7 | async-start | bytes 3145728 | tf_op jit(solution)/shard_map/all_to_all | solution.py:630
  325.4 9.0 %collective-permute-start.31 = (f32[152,256]{1,0:T(8,128)S(1)}, f32[152,256]{1,0:T(8,128)S(1)}, u32[]{:S(2)}, u32[]{:S(2)}) collective-permute-start(f32[152,256]{1,0:T(8,128)S(1)} %copy-done.19), channel_id=1, source_target_pairs={{0,1},{1,0},{2,3},{3,2},{4,5},{5,4},{6,7},{7,6},{8,9},{9,8},{10,11... | collective-permute-start | bytes 466952 | tf_op jit(solution)/shard_map/ppermute | solution.py:624
  325.4 17.3 %collective-permute-start.32 = (f32[152,256]{1,0:T(8,128)S(1)}, f32[152,256]{1,0:T(8,128)S(1)}, u32[]{:S(2)}, u32[]{:S(2)}) collective-permute-start(f32[152,256]{1,0:T(8,128)S(1)} %copy-done.19), channel_id=1, source_target_pairs={{0,2},{1,3},{2,0},{3,1},{4,6},{5,7},{6,4},{7,5},{8,10},{9,11},{10,... | collective-permute-start | bytes 466952 | tf_op jit(solution)/shard_map/ppermute | solution.py:624
  327.4 26.8 %collective-permute-start.34 = (bf16[256,128]{1,0:T(8,128)(2,1)S(1)}, bf16[256,128]{1,0:T(8,128)(2,1)S(1)}, u32[]{:S(2)}, u32[]{:S(2)}) collective-permute-start(bf16[256,128]{1,0:T(8,128)(2,1)S(1)} %copy-done.31), channel_id=1, source_target_pairs={{0,1},{1,2},{2,3},{3,0},{4,5},{5,6},{6,7},{7,4},{8,9},{9,10},{10,1... | collective-permute-start | bytes 196616 | tf_op jit(solution)/shard_map/ppermute | solution.py:621
  327.5 26.8 %collective-permute-start.35 = (bf16[256,128]{1,0:T(8,128)(2,1)S(1)}, bf16[256,128]{1,0:T(8,128)(2,1)S(1)}, u32[]{:S(2)}, u32[]{:S(2)}) collective-permute-start(bf16[256,128]{1,0:T(8,128)(2,1)S(1)} %copy-done.32), channel_id=1, source_target_pairs={{0,2},{1,3},{2,0},{3,1},{4,6},{5,7},{6,4},{7,5},{8,10},{9,11},{10,... | collective-permute-start | bytes 196616 | tf_op jit(solution)/shard_map/ppermute | solution.py:621
  330.4 23.9 %collective-permute-start.36 = (bf16[256,128]{1,0:T(8,128)(2,1)S(1)}, bf16[256,128]{1,0:T(8,128)(2,1)S(1)}, u32[]{:S(2)}, u32[]{:S(2)}) collective-permute-start(bf16[256,128]{1,0:T(8,128)(2,1)S(1)} %copy-done.33), channel_id=1, source_target_pairs={{0,3},{1,0},{2,1},{3,2},{4,7},{5,4},{6,5},{7,6},{8,11},{9,8},{10,9... | collective-permute-start | bytes 196616 | tf_op jit(solution)/shard_map/ppermute | solution.py:621
  334.4 13.9 %collective-permute-start.33 = (f32[152,256]{1,0:T(8,128)S(1)}, f32[152,256]{1,0:T(8,128)S(1)}, u32[]{:S(2)}, u32[]{:S(2)}) collective-permute-start(f32[152,256]{1,0:T(8,128)S(1)} %collective-permute-done.31.refs_2_), channel_id=1, source_target_pairs={{0,2},{1,3},{2,0},{3,1},{4,6},{5,7},{6,4},{7,5},{8,10},{9,11},{10,... | collective-permute-start | bytes 466952 | tf_op jit(solution)/shard_map/ppermute | solution.py:624
  342.8 5.6 %copy-start.47 = (f32[152,256]{1,0:T(8,128)}, f32[152,256]{1,0:T(8,128)S(1)}, u32[]{:S(2)}) copy-start(f32[152,256]{1,0:T(8,128)S(1)} %collective-permute-done.32.refs_3_) | copy-start | bytes 466948
  357.2 3.6 copy-start.1
  (36 other events, 37.1 us)
Sparse Core Ops, SparseCore 0:
  13.7 30.9 all-gather.3
  47.2 36.7 all-gather.5
  86.4 27.8 all-gather.7
  173.1 42.2 reduce-scatter.2
  285.2 41.9 reduce-scatter.4
where the time goes:
time: 374 us; the launch traced here: 368 us
  Pallas kernels  137 us (37%)
  waiting for transfers between devices  117 us (31%)
  starting transfers between devices  71.2 us (19%)
  local copies, waits for them, and re-layouts  23.1 us (6%)
  between operations  15.1 us (4%)
  other arithmetic  3.89 us (1%)
    pallas_call x26, Pallas kernels, run(): pl.pallas_call(body, out_shape=shapes, in_specs=[pl.BlockSpec(memory_spac...  131 us
    ppermute x22, waiting for transfers between devices, hop(): return lax.ppermute(value, 'seq', pairs)  52.3 us
    ppermute x12, starting transfers between devices, ring(): lax.ppermute(value, 'pos', [(i, (i + shift) % RING) for i in range(RING)])  29 us
    ppermute x12, waiting for transfers between devices, ring(): lax.ppermute(value, 'pos', [(i, (i + shift) % RING) for i in range(RING)])  23.4 us
    unnamed x107, local copies, waits for them, and re-layouts  21 us
    ppermute x22, starting transfers between devices, hop(): return lax.ppermute(value, 'seq', pairs)  18.1 us
    all_gather x3, waiting for transfers between devices, gather(): lax.all_gather(value, 'seq', axis=0, axis_index_groups=members, tiled=True)  18.1 us
    all_to_all x4, starting transfers between devices, swap(): lax.all_to_all(value, 'seq', 0, 0, axis_index_groups=members, tiled=True)  14.5 us
  transfers between devices with their start and end apart: 48, of which 19 were waited for; matrix products, arithmetic and copies ran while one was open for 2% of the time, Pallas kernels for 28%

commit v1 on v0

--- a/solution.py
+++ b/solution.py
@@ -157,10 +157,12 @@
     normed[...] = (unit * gains[...]).astype(bf16)
 
 
-def weights_kernel(in_w, up_w, down_w, in_rows, layer_rows):
+def weights_kernel(in_w, up_w, down_w, o0, o1, o2, o3, in_rows, layer_rows, out_rows):
     streams, channels = in_w.shape[0], in_w.shape[2]
     for k in range(streams):
         in_rows[pl.ds(k * channels, channels), :] = in_w[k].T
+    for j, slot in enumerate((o0, o1, o2, o3)):
+        out_rows[pl.ds(j * channels, channels), :] = slot[...]
     turned = up_w[...].T
     part = turned.shape[0] // CUBE
     for m in range(CUBE):
@@ -442,7 +444,7 @@
     grad_taps[pl.ds(half, half), :] = taps_odd
 
 
-def normed_kernel(info, grad_projected, in_full, n0, n1, n2, n3, gains, partial, gain_grad):
+def normed_kernel(info, grad_projected, in_full, n0, n1, n2, n3, gains, small, partial, packed):
     rows = n0.shape[0]
     total_gain = None
     for j, (slot, block) in enumerate(zip((n0, n1, n2, n3), ring_blocks(info, rows))):
@@ -450,7 +452,11 @@
         partial[block, :] = total.astype(bf16)
         part = jnp.sum(total * slot[...].astype(f32), axis=0, keepdims=True)
         total_gain = part if j == 0 else total_gain + part
-    gain_grad[...] = total_gain / gains[...]
+    total_gain = total_gain / gains[...]
+    packed[...] = small[...]
+    span = packed.shape[1]
+    for r in range(PLANE):
+        packed[pl.ds(OWNED + r, 1), :] = total_gain[:, r * span : (r + 1) * span]
 
 
 def in_grad_kernel(info, grad_projected, n0, n1, n2, n3, in_grad):
@@ -474,21 +480,8 @@
         down_grad[here, :] = parts[pl.ds((2 * m + 1) * part, part), :].astype(f32)
 
 
-def out_sum_kernel(info, parts, own, p1, p2, p3):
-    rows = parts.shape[0] // CUBE
-    count = own.shape[0]
-    for j, ref in enumerate((own, p1, p2, p3)):
-        place = ((info[2] + j) & (RING - 1)) * count
-        total = None
-        for m in range(CUBE):
-            here = pl.ds(pl.multiple_of(m * rows + place, count), count)
-            part = parts[here, :].astype(f32)
-            total = part if m == 0 else total + part
-        ref[...] = total.astype(ref.dtype)
-
-
 def out_end_kernel(own, p1, p2, p3, total):
-    total[...] = own[...] + p1[...].astype(f32) + p2[...].astype(f32) + p3[...].astype(f32)
+    total[...] = own[...].astype(f32) + p1[...].astype(f32) + p2[...].astype(f32) + p3[...].astype(f32)
 
 
 def in_end_kernel(parts, in_grad):
@@ -503,7 +496,7 @@
 
 
 def pack_kernel(
-    info, width, grad_taps, hidden, features, times, middle, last, small, gain_one, gain_two, packed
+    info, width, grad_taps, hidden, features, times, middle, last, small, gain_two, packed
 ):
     inner = middle.shape[0]
     span = packed.shape[1]
@@ -516,7 +509,7 @@
     packed[pl.ds(64, 16), :] = small[...]
     for r in range(PLANE):
         lanes = pl.ds(r * span, span)
-        packed[pl.ds(OWNED + r, 1), :] = gain_one[:, lanes]
+        packed[pl.ds(OWNED + r, 1), :] = jnp.zeros((1, span), f32)
         packed[pl.ds(OWNED + PLANE + r, 1), :] = gain_two[:, lanes]
     start = OWNED + GAINS
     packed[pl.ds(start, SHARED), :] = jnp.zeros((SHARED, span), f32)
@@ -679,20 +672,22 @@
         latest[:] = [mark]
         return passed
 
-    gain_one, gain_two = first_gain.reshape(1, width), second_gain.reshape(1, width)
+    gain_one, gain_two = first_gain, second_gain
     in_turned = widen(in_proj.transpose(1, 0, 2), 1)
     out_shard, up_shard, down_shard = widen(out_proj, 1), widen(up_proj, 0), widen(down_proj, 1)
+    out_shards = [out_shard] + [ring(out_shard, -j) for j in range(1, RING)]
     normed, inputs, cot = step(
         rows_kernel, [((rows, width), bf16)] * 3, block_input, cotangent, gain_one, name="rows", micros=0.2
     )
     normed_slots = [normed, ring(normed, -1)]
-    in_rows, layer_rows = step(
+    in_rows, layer_rows, out_rows = step(
         weights_kernel,
-        [((3 * channels, lane), bf16), ((2 * hidden, lane), bf16)],
-        in_turned, up_shard, down_shard,
+        [((3 * channels, lane), bf16), ((2 * hidden, lane), bf16), ((width, lane), bf16)],
+        in_turned, up_shard, down_shard, *out_shards,
         name="weights", micros=0.2,
     )
     in_all = gather(in_rows)
+    out_all = gather(out_rows)
     layer_got = swap(layer_rows)
 
     channel_start = ring_place * channels
@@ -717,24 +712,22 @@
         features, filter_in, filter_in_bias[None], filter_mid, filter_mid_bias[None],
         name="hidden", micros=5,
     )
-    normed_slots[1], out_shard = phase(normed_slots[1], out_shard)
+    (normed_slots[1],) = phase(normed_slots[1], after=[layer_got])
     normed_slots.append(ring(normed_slots[1], -1))
-    out_shards = [out_shard] + [ring(out_shard, -j) for j in range(1, RING)]
     (layer_own,) = step(
         side_by_side, [((2 * hidden // CUBE, width), bf16)], layer_got, name="layer_own", micros=0.2
     )
+    (normed_slots[2],) = phase(normed_slots[2], after=[lags, skip])
+    normed_slots.append(ring(normed_slots[2], -1))
     (spectrum,) = step(
         with_width(taps_kernel),
         [pair],
         info, filter_hidden, times, last_layer, turns, *tables,
         name="taps", micros=5,
     )
-    normed_slots[2], out_shards[0], *out_shards[1:] = phase(normed_slots[2], *out_shards)
-    normed_slots.append(ring(normed_slots[2], -1))
+    layer_own, cot = phase(layer_own, cot, after=[normed_slots[3]])
+    layer_slots = [layer_own, ring(layer_own, -1)]
     cot_all = gather(cot)
-    layer_own, *out_shards = phase(layer_own, *out_shards, after=[normed_slots[3]])
-    layer_slots = [layer_own, ring(layer_own, -1)]
-    out_all = gather(jnp.concatenate(out_shards, 0))
 
     projected, long_conv, driven_spectrum, gated, in_full = step(
         conv_kernel,
@@ -748,9 +741,9 @@
         info, *normed_slots, in_all, lags, skip, spectrum, *tables,
         name="conv", micros=14,
     )
-    gated, layer_slots[1] = phase(gated, layer_slots[1], after=[cot_all])
+    gated, layer_slots[1] = phase(gated, layer_slots[1])
     gated = to_rows(gated)
-    layer_slots[:2] = phase(*layer_slots[:2], after=[gated, out_all])
+    layer_slots = phase(*layer_slots, after=[gated, out_all])
     layer_slots += [ring(layer_slots[1], -1), ring(layer_slots[0], 1)]
     residual, second = step(
         out_kernel,
@@ -776,17 +769,18 @@
     layer_grads = lax.psum_scatter(layer_grads, "pos", scatter_dimension=0, tiled=True)
 
     block, part = ((rows, width), bf16), ((half, width), bf16)
-    turned = []
     shares = [
         step(share_kernel, [block] * 3 + [part] * 2, kept, hop(given, 1), name="share", micros=0.1)
         for kept, given in ((back_kept, back_given), (out_kept, out_given))
     ]
-    for own, across, along, top, low in shares:
+
+    def turn(own, across, along, top, low):
         across, along = step(
             turn_kernel, [block] * 2, across, along, hop(top, 2), hop(low, 4), name="turn", micros=0.1
         )
-        turned.append([own, hop(across, 2), hop(along, 4)])
-    back_parts, out_parts = turned
+        return own, hop(across, 2), hop(along, 4)
+
+    back_parts = turn(*shares[0])
     grad_res, branch, second_gain_grad, grad_gated = step(
         branch_kernel,
         [((rows, width), f32), ((rows, width), bf16), ((1, width), f32), ((seq_len, channels), bf16)],
@@ -798,9 +792,9 @@
     (out_grad,) = step(
         out_grad_kernel, [((CUBE * width, lane), bf16)], gated, branch, name="out_grad", micros=0.1
     )
+    out_parts = turn(*shares[1])
+    out_grad = scatter(out_grad)
     (layer_sums,) = step(below_kernel, [((2 * hidden, lane), bf16)], layer_grads, name="layer_sum", micros=0.1)
-    (out_grad,) = phase(out_grad, after=[grad_gated])
-    out_grad = swap(out_grad)
 
     grad_projected, grad_taps, small = step(
         back_kernel,
@@ -808,48 +802,46 @@
         info, grad_gated, projected, long_conv, driven_spectrum, lags, skip, spectrum, turns, *tables,
         name="back", micros=15,
     )
-    partial, first_gain_grad = step(
-        normed_kernel,
-        [((seq_len, width), bf16), ((1, width), f32)],
-        info, grad_projected, in_full, *normed_slots, gain_one,
-        name="normed", micros=0.2,
-    )
-    partial, layer_sums = phase(partial, layer_sums, after=[out_grad, *out_parts[1:]])
-    grad_normed = lax.psum_scatter(partial, "pos", scatter_dimension=0, tiled=True)
-    layer_sums = swap(layer_sums)
     (packed,) = step(
         with_width(pack_kernel),
         [((PACKED, channels), f32)],
-        info, grad_taps, filter_hidden, features, times, filter_mid, last_layer, small,
-        first_gain_grad, second_gain_grad,
+        info, grad_taps, filter_hidden, features, times, filter_mid, last_layer, small, second_gain_grad,
         name="pack", micros=0.1,
     )
+    partial, packed = step(
+        normed_kernel,
+        [((seq_len, width), bf16), ((PACKED, channels), f32)],
+        info, grad_projected, in_full, *normed_slots, gain_one, packed,
+        name="normed", micros=0.2,
+    )
+    partial, packed, layer_sums = phase(partial, packed, layer_sums, after=[out_grad])
+    grad_normed = lax.psum_scatter(partial, "pos", scatter_dimension=0, tiled=True)
+    layer_sums = swap(layer_sums)
     if fold > 1:
         packed = lax.psum(packed, "seq", axis_index_groups=bundles)
-    (packed,) = phase(packed)
     (in_grad,) = step(
         in_grad_kernel,
         [((3 * CUBE * channels, lane), bf16)],
         info, grad_projected, *normed_slots,
         name="in_grad", micros=0.1,
     )
-    out_slots = step(
-        out_sum_kernel, [((channels, lane), t) for t in (f32, bf16, bf16, bf16)], info, out_grad,
-        name="out_sum", micros=0.1,
+    for bit in (1, 2, 4):
+        packed = packed + hop(packed, bit)
+    in_grad, packed, out_grad = phase(in_grad, packed, out_grad, after=[layer_sums, *out_parts[1:]])
+    in_grad = swap(in_grad)
+    out_slots = [
+        lax.dynamic_slice_in_dim(out_grad, (ring_place + j) % RING * channels, channels) for j in range(RING)
+    ]
+    out_slots = [out_slots[0]] + [ring(out_slots[j], j) for j in range(1, RING)]
+    packed_slots = [packed, near_ring(packed, 1)]
+    packed_slots += [near_ring(v, 2) for v in packed_slots]
+    up_grad, down_grad = step(
+        layer_end_kernel, [((lane, hidden), f32), ((hidden, lane), f32)], layer_sums, name="layer_end"
     )
     (block_output,) = step(
         finish_kernel, [((rows, width), bf16)], residual, *out_parts, name="finish", micros=0.1
     )
-    for bit in (1, 2, 4):
-        packed = packed + hop(packed, bit)
-    in_grad, packed, *sent = phase(in_grad, packed, *out_slots[1:], after=[layer_sums])
-    in_grad = swap(in_grad)
-    out_slots = [out_slots[0]] + [ring(v, j) for j, v in enumerate(sent, 1)]
-    up_grad, down_grad = step(
-        layer_end_kernel, [((lane, hidden), f32), ((hidden, lane), f32)], layer_sums, name="layer_end"
-    )
-    packed_slots = [packed, near_ring(packed, 1)]
-    packed_slots += [near_ring(v, 2) for v in packed_slots]
+    (out_grad,) = step(out_end_kernel, [((channels, lane), f32)], *out_slots, name="out_end")
     small_grads = step(
         unpack_kernel,
         [
@@ -867,11 +859,10 @@
         scratch=[((RING, PACKED, channels), f32)],
         name="unpack",
     )
+    (in_grad,) = step(in_end_kernel, [((3, lane, channels), f32)], in_grad, name="in_end")
     (input_grad,) = step(
-        end_kernel, [((rows, width), bf16)], grad_normed, inputs, gain_one, grad_res, name="end", micros=4
-    )
-    (out_grad,) = step(out_end_kernel, [((channels, lane), f32)], *out_slots, name="out_end")
-    (in_grad,) = step(in_end_kernel, [((3, lane, channels), f32)], in_grad, name="in_end")
+        end_kernel, [((rows, width), bf16)], grad_normed, inputs, gain_one, grad_res, name="end", micros=1
+    )
     return (
         block_output,
         input_grad,

time: 374 us -> 348 us (0.930)
  waiting for transfers between devices: 117 us -> 86.5 us
  blocking collectives: 0 us -> 14.5 us
  local copies, waits for them, and re-layouts: 23.1 us -> 18.8 us
    all_gather x3, waiting for transfers between devices: 18.1 us -> 0.01 us  [gather(): lax.all_gather(value, 'seq', axis=0, axis_index_groups=members, tiled=True)]
    all_to_all x0 -> x1, blocking collectives: none -> 14.5 us  [to_rows(): return lax.all_to_all(value, 'pos', 0, 0, tiled=True)]
    ppermute x22, starting transfers between devices: 18.1 us -> 31.8 us  [hop(): return lax.ppermute(value, 'seq', pairs)]
    ppermute x12, starting transfers between devices: 29 us -> 21.7 us  [ring(): lax.ppermute(value, 'pos', [(i, (i + shift) % RING) for i in range(RING)])]
    all_to_all x2 -> x1, waiting for transfers between devices: 7.68 us -> 0.55 us  [to_rows(): return lax.all_to_all(value, 'pos', 0, 0, tiled=True)]
    all_to_all x4 -> x3, waiting for transfers between devices: 0.01 us -> 6.55 us  [swap(): lax.all_to_all(value, 'seq', 0, 0, axis_index_groups=members, tiled=True)]
    ppermute x3, waiting for transfers between devices: 14.5 us -> 8.69 us  [near_ring(): return lax.ppermute(value, 'pos', [(i, i ^ bit) for i in range(RING)])]
    unnamed x107 -> x102, local copies, waits for them, and re-layouts: 21 us -> 16.1 us
  transfers between devices with their start and end apart: 48 -> 47, of which waited for: 19 -> 20; matrix products, arithmetic and copies ran while one was open for 2% -> 1% of each run, Pallas kernels for 28% -> 30%
where the time goes in v1:
time: 348 us; the launch traced here: 342 us
  Pallas kernels  135 us (39%)
  waiting for transfers between devices  86.5 us (25%)
  starting transfers between devices  70.1 us (20%)
  local copies, waits for them, and re-layouts  18.8 us (5%)
  between operations  15.4 us (4%)
  blocking collectives  14.5 us (4%)
    pallas_call x25, Pallas kernels, run(): pl.pallas_call(body, out_shape=shapes, in_specs=[pl.BlockSpec(memory_spac...  130 us
    ppermute x22, waiting for transfers between devices, hop(): return lax.ppermute(value, 'seq', pairs)  49.2 us
    ppermute x22, starting transfers between devices, hop(): return lax.ppermute(value, 'seq', pairs)  31.8 us
    ppermute x12, starting transfers between devices, ring(): lax.ppermute(value, 'pos', [(i, (i + shift) % RING) for i in range(RING)])  21.7 us
    ppermute x12, waiting for transfers between devices, ring(): lax.ppermute(value, 'pos', [(i, (i + shift) % RING) for i in range(RING)])  20.5 us
    unnamed x102, local copies, waits for them, and re-layouts  16.1 us
    all_to_all x1, blocking collectives, to_rows(): return lax.all_to_all(value, 'pos', 0, 0, tiled=True)  14.5 us
    all_to_all x3, starting transfers between devices, swap(): lax.all_to_all(value, 'seq', 0, 0, axis_index_groups=members, tiled=True)  10.9 us
  transfers between devices with their start and end apart: 47, of which 20 were waited for; matrix products, arithmetic and copies ran while one was open for 1% of the time, Pallas kernels for 30%

profile of v1, /device:TPU:0, one launch (start us, length us, event | category | flops | bytes accessed | tf_op | source)
XLA Modules:
  0.0 341.7 jit_solution(17894998223583487892)
XLA Ops:
  7.2 5.1 %collective-permute-start.1 = (bf16[256,128]{1,0:T(8,128)(2,1)}, bf16[256,128]{1,0:T(8,128)(2,1)S(1)}, u32[]{:S(2)}, u32[]{:S(2)}) collective-permute-start(bf16[256,128]{1,0:T(8,128)(2,1)} %refs_3_.3), channel_id=1, source_target_pairs={{0,3},{1,0},{2,1},{3,2},{4,7},{5,4},{6,5},{7,6},{8,11},{9,8},{10,9... | collective-permute-start | bytes 196616 | tf_op jit(solution)/shard_map/ppermute | solution.py:614
  13.4 2.8 rows.1
  16.1 2.9 collective-permute-done.2.refs_5_
  19.7 2.2 weights.1
  22.7 1.9 collective-permute-start
  24.6 3.7 %all-to-all-start = ((bf16[8,256,128]{2,1,0:T(8,128)(2,1)}), bf16[8,256,128]{2,1,0:T(8,128)(2,1)S(1)}, u32[]{:S(2)}, u32[]{:S(2)}) async-start(bf16[8,256,128]{2,1,0:T(8,128)(2,1)} %bitcast.37), calls=%async_computation | async-start | bytes 1048576 | tf_op jit(solution)/shard_map/all_to_all | solution.py:623
  28.4 5.3 %hidden.1.refs_1_.refs_2_ = f32[1024,256]{1,0:T(8,128)} custom-call(f32[1024,33]{1,0:T(8,128)} %constant.83.clone.refs_0_.refs_3_, f32[33,64]{1,0:T(8,128)} %refs_1_.5, f32[1,64]{1,0:T(1,128)} %bitcast.45, f32[64,64]{1,0:T(8,128)} %refs_5_.4, f32[1,64]{1,0:T(1,128)} %bitcast.46, bf16[768,128]{1,0:T(8,128)(2,1)} %get-tuple-element.95.refs_5_), custom_call_target="tpu_custom_call" | custom-call | flops 5000000000 | bytes 15000000 | tf_op jit(solution)/shard_map/hidden/pallas_call | solution.py:564
  33.7 6.5 %all-to-all-done = bf16[8,256,128]{2,1,0:T(8,128)(2,1)S(1)} async-done(((bf16[8,256,128]{2,1,0:T(8,128)(2,1)}), bf16[8,256,128]{2,1,0:T(8,128)(2,1)S(1)}, u32[]{:S(2)}, u32[]{:S(2)}) %all-to-all-start) | async-done | bytes 524320 | tf_op jit(solution)/shard_map/all_to_all | solution.py:623
  41.8 1.3 collective-permute-start.4
  46.4 2.0 layer_own.1.refs_1_.refs_0_
  48.4 5.0 %collective-permute-done.4.refs_0_ = bf16[256,1024]{1,0:T(8,128)(2,1)S(1)} collective-permute-done((bf16[256,1024]{1,0:T(8,128)(2,1)}, bf16[256,1024]{1,0:T(8,128)(2,1)S(1)}, u32[]{:S(2)}, u32[]{:S(2)}) %collective-permute-start.4) | collective-permute-done | bytes 524320 | tf_op jit(solution)/shard_map/ppermute | solution.py:614
  54.8 2.5 collective-permute-start.5
  57.9 8.6 %taps.1.refs_2_.refs_8_.refs_7_ = f32[2,1024,256]{2,1,0:T(8,128)} custom-call(s32[4]{0:T(128)} %pad_add_fusion.refs_0_, f32[1024,256]{1,0:T(8,128)} %hidden.1.refs_1_.refs_2_, f32[1024,1]{1,0:T(8,128)} %constant.84.clone.refs_2_.refs_4_, f32[64,256]{1,0:T(8,128)} %constant_dynamic-slice_fusion.4.refs_3_.refs_6_, ...), custom_call_target="tpu_custom_call" | custom-call | flops 5000000000 | bytes 15000000 | tf_op jit(solution)/shard_map/taps/pallas_call | solution.py:564
  68.0 3.1 collective-permute-start.6
  71.1 14.1 %conv.1 = (bf16[1024,768]{1,0:T(8,128)(2,1)}, f32[1024,256]{1,0:T(8,128)}, f32[2,1024,256]{2,1,0:T(8,128)}, bf16[1024,256]{1,0:T(8,128)(2,1)}, bf16[768,1024]{1,0:T(8,128)(2,1)}) custom-call(s32[4]{0:T(128)} %pad_add_fusion.refs_0_, bf16[256,1024]{1,0:T(8,128)(2,1)} %get-tuple-element.94.refs_7_.refs_1_.refs_3_.refs_2_, ...), custom_call_target="tpu_custom_call" | custom-call | flops 14000000000 | bytes 42000000 | tf_op jit(solution)/shard_map/conv/pallas_call | solution.py:564
  86.6 14.5 %all_to_all.55 = bf16[4,256,256]{2,1,0:T(8,128)(2,1)} all-to-all(bf16[4,256,256]{2,1,0:T(8,128)(2,1)} %bitcast.34), channel_id=1, replica_groups=mesh['seq'=8,'pos'=4] {'pos'}, dimensions={0} | all-to-all | bytes 1048576 | tf_op jit(solution)/shard_map/all_to_all | solution.py:620
  101.7 4.3 %out.1 = (f32[256,1024]{1,0:T(8,128)}, bf16[256,1024]{1,0:T(8,128)(2,1)}) custom-call(s32[4]{0:T(128)} %pad_add_fusion.refs_0_, bf16[1024,256]{1,0:T(8,128)(2,1)} %bitcast.28, bf16[8192,128]{1,0:T(8,128)(2,1)} %all-gather.6.cloned.1.call-done.refs_4_.refs_2_.refs_7_, bf16[256,1024]{1,0:T(8,128)(2,1)} %get-tuple-element.108.refs_3_.refs_1_, f32[1024]{0:T(1024)} %refs_5_.3, ...), custom_call_target="tpu_custom_call" | custom-call | flops 200000000 | bytes 600000 | tf_op jit(solution)/shard_map/out/pallas_call | solution.py:564
  106.0 2.4 collective-permute-start.10
  108.4 6.8 %collective-permute-start.8 = (bf16[256,1024]{1,0:T(8,128)(2,1)}, bf16[256,1024]{1,0:T(8,128)(2,1)S(1)}, u32[]{:S(2)}, u32[]{:S(2)}) collective-permute-start(bf16[256,1024]{1,0:T(8,128)(2,1)} %get-tuple-element.113.refs_1_), channel_id=1, source_target_pairs={{0,8},{4,12},{8,0},{12,4},{16,24},{20,28},{24,16},{28,20},{1,9},{5... | collective-permute-start | bytes 1572872 | tf_op jit(solution)/shard_map/ppermute | solution.py:611
  115.1 1.5 collective-permute-start.16
  117.7 8.7 %collective-permute-done.10.refs_5_ = bf16[256,1024]{1,0:T(8,128)(2,1)S(1)} collective-permute-done((bf16[256,1024]{1,0:T(8,128)(2,1)}, bf16[256,1024]{1,0:T(8,128)(2,1)S(1)}, u32[]{:S(2)}, u32[]{:S(2)}) %collective-permute-start.10) | collective-permute-done | bytes 524320 | tf_op jit(solution)/shard_map/ppermute | solution.py:611
  126.4 5.0 %collective-permute-start.12 = (bf16[128,1024]{1,0:T(8,128)(2,1)S(1)}, bf16[128,1024]{1,0:T(8,128)(2,1)S(1)}, u32[]{:S(2)}, u32[]{:S(2)}) collective-permute-start(bf16[128,1024]{1,0:T(8,128)(2,1)S(1)} %slice.8), channel_id=1, source_target_pairs={{0,8},{4,12},{8,0},{12,4},{16,24},{20,28},{24,16},{28,20},{1,9},{5... | collective-permute-start | bytes 786440 | tf_op jit(solution)/shard_map/ppermute | solution.py:611
  132.0 8.7 %collective-permute-done.16.refs_14_ = bf16[256,1024]{1,0:T(8,128)(2,1)S(1)} collective-permute-done((bf16[256,1024]{1,0:T(8,128)(2,1)S(1)}, bf16[256,1024]{1,0:T(8,128)(2,1)S(1)}, u32[]{:S(2)}, u32[]{:S(2)}) %collective-permute-start.16) | collective-permute-done | bytes 524320 | tf_op jit(solution)/shard_map/ppermute | solution.py:614
  140.7 2.0 collective-permute-start.13
  142.8 4.3 %collective-permute-done.13.refs_8_ = bf16[128,1024]{1,0:T(8,128)(2,1)S(1)} collective-permute-done((bf16[128,1024]{1,0:T(8,128)(2,1)S(1)}, bf16[128,1024]{1,0:T(8,128)(2,1)S(1)}, u32[]{:S(2)}, u32[]{:S(2)}) %collective-permute-start.13) | collective-permute-done | bytes 262176 | tf_op jit(solution)/shard_map/ppermute | solution.py:611
  148.8 20.6 %layer.1 = (bf16[1024,1024]{1,0:T(8,128)(2,1)}, bf16[1024,1024]{1,0:T(8,128)(2,1)}, bf16[1024,1024]{1,0:T(8,128)(2,1)}, bf16[1024,1024]{1,0:T(8,128)(2,1)}, bf16[1024,1024]{1,0:T(8,128)(2,1)}) custom-call(s32[4]{0:T(128)} %pad_add_fusion.refs_0_, bf16[256,1024]{1,0:T(8,128)(2,1)} %get-tuple-element.113.refs_1_, bf16[256,1024]{1,0:T(8,128)(2,1)} %copy-done.34, ...), custom_call_target="tpu_custom_call" | custom-call | flops 22000001024 | bytes 66000000 | tf_op jit(solution)/shard_map/layer/pallas_call | solution.py:564
  171.9 2.7 collective-permute-done.19.refs_1_
  176.0 3.6 %share.2 = (bf16[256,1024]{1,0:T(8,128)(2,1)}, bf16[256,1024]{1,0:T(8,128)(2,1)}, bf16[256,1024]{1,0:T(8,128)(2,1)}, bf16[128,1024]{1,0:T(8,128)(2,1)}, bf16[128,1024]{1,0:T(8,128)(2,1)}) custom-call(bf16[1024,1024]{1,0:T(8,128)(2,1)} %get-tuple-element.122.refs_0_, bf16[1024,1024]{1,0:T(8,128)(2,1)} %copy-done.10, f32[8,128]{1,0:T(8,128)} %get-tuple-element.124.refs_2_), custom_call_target="tpu_custom_call" | custom-call | flops 100000000 | bytes 300000 | tf_op jit(solution)/shard_map/share/pallas_call | solution.py:564
  179.7 1.9 collective-permute-start.23
  183.0 3.8 %share.3 = (bf16[256,1024]{1,0:T(8,128)(2,1)}, bf16[256,1024]{1,0:T(8,128)(2,1)}, bf16[256,1024]{1,0:T(8,128)(2,1)}, bf16[128,1024]{1,0:T(8,128)(2,1)}, bf16[128,1024]{1,0:T(8,128)(2,1)}) custom-call(bf16[1024,1024]{1,0:T(8,128)(2,1)} %get-tuple-element.117.refs_3_.refs_0_, bf16[1024,1024]{1,0:T(8,128)(2,1)} %copy-done.12, ...), custom_call_target="tpu_custom_call" | custom-call | flops 100000000 | bytes 300000 | tf_op jit(solution)/shard_map/share/pallas_call | solution.py:564
  186.8 1.6 collective-permute-done.22.refs_2_
  189.4 2.4 turn.2
  191.8 1.7 collective-permute-start.24
  193.6 1.7 collective-permute-start.25
  195.3 10.4 %collective-permute-done.24.refs_2_ = bf16[256,1024]{1,0:T(8,128)(2,1)S(1)} collective-permute-done((bf16[256,1024]{1,0:T(8,128)(2,1)}, bf16[256,1024]{1,0:T(8,128)(2,1)S(1)}, u32[]{:S(2)}, u32[]{:S(2)}) %collective-permute-start.24) | collective-permute-done | bytes 524320 | tf_op jit(solution)/shard_map/ppermute | solution.py:611
  207.8 5.5 %branch.1 = (f32[256,1024]{1,0:T(8,128)}, bf16[256,1024]{1,0:T(8,128)(2,1)}, f32[1,1024]{1,0:T(1,128)}, bf16[1024,256]{1,0:T(8,128)(2,1)}) custom-call(s32[4]{0:T(128)} %pad_add_fusion.refs_0_, bf16[256,1024]{1,0:T(8,128)(2,1)} %get-tuple-element.125.refs_2_.refs_1_, bf16[256,1024]{1,0:T(8,128)(2,1)} %copy-done.21, bf16[256,1024]{1,0:T(8,128)(2,1)} %copy-done.22, ...), custom_call_target="tpu_custom_call" | custom-call | flops 200000000 | bytes 600000 | tf_op jit(solution)/shard_map/branch/pallas_call | solution.py:564
  213.9 3.2 out_grad.1.refs_4_
  217.2 3.6 %all-to-all-start.2 = ((bf16[4,256,256]{2,1,0:T(8,128)(2,1)}), bf16[4,256,256]{2,1,0:T(8,128)(2,1)S(1)}, u32[]{:S(2)}, u32[]{:S(2)}) async-start(bf16[4,256,256]{2,1,0:T(8,128)(2,1)} %bitcast.11), calls=%async_computation.3 | async-start | bytes 1048576 | tf_op jit(solution)/shard_map/all_to_all | solution.py:620
  222.0 1.4 collective-permute-start.21
  223.4 4.3 %collective-permute-done.20.refs_2_ = bf16[128,1024]{1,0:T(8,128)(2,1)S(1)} collective-permute-done((bf16[128,1024]{1,0:T(8,128)(2,1)S(1)}, bf16[128,1024]{1,0:T(8,128)(2,1)S(1)}, u32[]{:S(2)}, u32[]{:S(2)}) %collective-permute-start.20) | collective-permute-done | bytes 262176 | tf_op jit(solution)/shard_map/ppermute | solution.py:611
  229.5 2.4 turn.3
  231.9 1.9 layer_sum.1.refs_17_.refs_2_
  235.1 15.7 %back.1 = (bf16[1024,768]{1,0:T(8,128)(2,1)}, f32[1024,256]{1,0:T(8,128)}, f32[16,256]{1,0:T(8,128)}) custom-call(s32[4]{0:T(128)} %pad_add_fusion.refs_0_, bf16[1024,256]{1,0:T(8,128)(2,1)} %bitcast.36, bf16[1024,768]{1,0:T(8,128)(2,1)} %get-tuple-element.105.refs_2_, f32[1024,256]{1,0:T(8,128)} %get-tuple-element.145.refs_3_, ...), custom_call_target="tpu_custom_call" | custom-call | flops 15000000512 | bytes 45000000 | tf_op jit(solution)/shard_map/back/pallas_call | solution.py:564
  250.8 6.0 %pack.1.refs_8_ = f32[152,256]{1,0:T(8,128)} custom-call(s32[4]{0:T(128)} %pad_add_fusion.refs_0_, f32[1024,256]{1,0:T(8,128)} %get-tuple-element.149.refs_1_, f32[1024,256]{1,0:T(8,128)} %hidden.1.refs_1_.refs_2_, f32[1024,33]{1,0:T(8,128)} %constant.83.clone.refs_0_.refs_3_, f32[1024,1]{1,0:T(8,128)} %constant.84.clone.refs_2_.refs_4_, f32[64,64]{1,0:T(8,128)} %refs_5_.4, ...), custom_call_target="tpu_custom_call" | custom-call | flops 100000000 | bytes 300000 | tf_op jit(solution)/shard_map/pack/pallas_call | solution.py:564
  256.8 5.9 %normed.1 = (bf16[1024,1024]{1,0:T(8,128)(2,1)}, f32[152,256]{1,0:T(8,128)}) custom-call(s32[4]{0:T(128)} %pad_add_fusion.refs_0_, bf16[1024,768]{1,0:T(8,128)(2,1)} %get-tuple-element.147.refs_9_.refs_1_, bf16[768,1024]{1,0:T(8,128)(2,1)} %get-tuple-element.148.refs_2_, bf16[256,1024]{1,0:T(8,128)(2,1)} %get-tuple-element.94.refs_7_.refs_1_.refs_3_.refs_2_, ...), custom_call_target="tpu_custom_call" | custom-call | flops 200000000 | bytes 600000 | tf_op jit(solution)/shard_map/normed/pallas_call | solution.py:564
  265.1 1.5 collective-permute-start.27
  266.5 3.5 %all-to-all-start.3 = ((bf16[8,256,128]{2,1,0:T(8,128)(2,1)}), bf16[8,256,128]{2,1,0:T(8,128)(2,1)S(1)}, u32[]{:S(2)}, u32[]{:S(2)}) async-start(bf16[8,256,128]{2,1,0:T(8,128)(2,1)} %bitcast.13), calls=%async_computation.5 | async-start | bytes 1048576 | tf_op jit(solution)/shard_map/all_to_all | solution.py:623
  270.1 2.0 collective-permute-start.29
  272.1 13.7 %collective-permute-done.29 = f32[152,256]{1,0:T(8,128)S(1)} collective-permute-done((f32[152,256]{1,0:T(8,128)S(1)}, f32[152,256]{1,0:T(8,128)S(1)}, u32[]{:S(2)}, u32[]{:S(2)}) %collective-permute-start.29) | collective-permute-done | bytes 155680 | tf_op jit(solution)/shard_map/ppermute | solution.py:611
  285.8 1.4 collective-permute-start.30
  287.2 5.0 %in_grad.1.refs_0_ = bf16[6144,128]{1,0:T(8,128)(2,1)} custom-call(s32[4]{0:T(128)} %pad_add_fusion.refs_0_, bf16[1024,768]{1,0:T(8,128)(2,1)} %get-tuple-element.147.refs_9_.refs_1_, bf16[256,1024]{1,0:T(8,128)(2,1)} %get-tuple-element.94.refs_7_.refs_1_.refs_3_.refs_2_, bf16[256,1024]{1,0:T(8,128)(2,1)} %get-tuple-element.97.refs_2_.refs_4_.refs_3_, ...), custom_call_target="tpu_custom_call" | custom-call | flops 100000000 | bytes 300000 | tf_op jit(solution)/shard_map/in_grad/pallas_call | solution.py:564
  294.6 3.7 %all-to-all-start.4 = ((bf16[8,768,128]{2,1,0:T(8,128)(2,1)}), bf16[8,768,128]{2,1,0:T(8,128)(2,1)S(1)}, u32[]{:S(2)}, u32[]{:S(2)}) async-start(bf16[8,768,128]{2,1,0:T(8,128)(2,1)} %bitcast.26), calls=%async_computation.7 | async-start | bytes 3145728 | tf_op jit(solution)/shard_map/all_to_all | solution.py:623
  298.5 1.7 collective-permute-start.32
  301.4 2.7 collective-permute-start.35
  305.1 2.1 layer_end.1
  307.2 2.9 finish.1.refs_4_
  310.1 3.0 collective-permute-done.31.refs_2_
  313.1 2.5 collective-permute-done.34.refs_1_
  315.6 1.4 collective-permute-done.35.refs_2_
  317.6 1.6 out_end.1.refs_5_
  319.3 5.7 %collective-permute-done.33.refs_4_ = f32[152,256]{1,0:T(8,128)S(1)} collective-permute-done((f32[152,256]{1,0:T(8,128)S(1)}, f32[152,256]{1,0:T(8,128)S(1)}, u32[]{:S(2)}, u32[]{:S(2)}) %collective-permute-start.33) | collective-permute-done | bytes 155680 | tf_op jit(solution)/shard_map/ppermute | solution.py:617
  325.7 2.0 unpack.1
  328.8 2.5 in_end.1.refs_4_
  331.2 3.3 end.1
  (183 shorter events, 38.1 us)
Async XLA Ops:
  7.2 38.6 %copy-start = (f32[64,1024]{1,0:T(8,128)S(1)}, f32[64,1024]{1,0:T(8,128)}, u32[]{:S(2)}) copy-start(f32[64,1024]{1,0:T(8,128)} %param.42) | copy-start | bytes 786436
  7.2 63.9 %all-gather.4.cloned.1.call-start = ((), (), s32[]{:S(2)}) async-start(), calls=%async_computation.8 | async-start | bytes 1769472 | tf_op jit(solution)/shard_map/all_gather | solution.py:626
  7.2 8.9 %collective-permute-start.1 = (bf16[256,128]{1,0:T(8,128)(2,1)}, bf16[256,128]{1,0:T(8,128)(2,1)S(1)}, u32[]{:S(2)}, u32[]{:S(2)}) collective-permute-start(bf16[256,128]{1,0:T(8,128)(2,1)} %refs_3_.3), channel_id=1, source_target_pairs={{0,3},{1,0},{2,1},{3,2},{4,7},{5,4},{6,5},{7,6},{8,11},{9,8},{10,9... | collective-permute-start | bytes 196616 | tf_op jit(solution)/shard_map/ppermute | solution.py:614
  12.3 6.7 %collective-permute-start.2 = (bf16[256,128]{1,0:T(8,128)(2,1)}, bf16[256,128]{1,0:T(8,128)(2,1)S(1)}, u32[]{:S(2)}, u32[]{:S(2)}) collective-permute-start(bf16[256,128]{1,0:T(8,128)(2,1)} %refs_3_.3), channel_id=1, source_target_pairs={{0,2},{1,3},{2,0},{3,1},{4,6},{5,7},{6,4},{7,5},{8,10},{9,11},{10,... | collective-permute-start | bytes 196616 | tf_op jit(solution)/shard_map/ppermute | solution.py:614
  12.3 6.7 %collective-permute-start.3 = (bf16[256,128]{1,0:T(8,128)(2,1)}, bf16[256,128]{1,0:T(8,128)(2,1)S(1)}, u32[]{:S(2)}, u32[]{:S(2)}) collective-permute-start(bf16[256,128]{1,0:T(8,128)(2,1)} %refs_3_.3), channel_id=1, source_target_pairs={{0,1},{1,2},{2,3},{3,0},{4,5},{5,6},{6,7},{7,4},{8,9},{9,10},{10,1... | collective-permute-start | bytes 196616 | tf_op jit(solution)/shard_map/ppermute | solution.py:614
  21.9 79.1 %all-gather.6.cloned.1.call-start = ((), (), s32[]{:S(2)}) async-start(), calls=%async_computation.9 | async-start | bytes 2359296 | tf_op jit(solution)/shard_map/all_gather | solution.py:626
  22.7 17.5 %collective-permute-start = (bf16[256,1024]{1,0:T(8,128)(2,1)}, bf16[256,1024]{1,0:T(8,128)(2,1)S(1)}, u32[]{:S(2)}, u32[]{:S(2)}) collective-permute-start(bf16[256,1024]{1,0:T(8,128)(2,1)} %get-tuple-element.94.refs_7_.refs_1_.refs_3_.refs_2_), channel_id=1, source_target_pairs={{0,3},{1,0},{2,1},{3,2},{4,7},{5,4},{6,5},{7,6},{8,11},{9,8},{10,9... | collective-permute-start | bytes 1572872 | tf_op jit(solution)/shard_map/ppermute | solution.py:614
  24.6 15.6 %all-to-all-start = ((bf16[8,256,128]{2,1,0:T(8,128)(2,1)}), bf16[8,256,128]{2,1,0:T(8,128)(2,1)S(1)}, u32[]{:S(2)}, u32[]{:S(2)}) async-start(bf16[8,256,128]{2,1,0:T(8,128)(2,1)} %bitcast.37), calls=%async_computation | async-start | bytes 1048576 | tf_op jit(solution)/shard_map/all_to_all | solution.py:623
  28.4 120.4 %all-gather.8.cloned.1.call-start = ((), (), s32[]{:S(2)}) async-start(), calls=%async_computation.10 | async-start | bytes 4718592 | tf_op jit(solution)/shard_map/all_gather | solution.py:626
  33.7 10.1 %copy-start.32 = (f32[3,3072]{1,0:T(4,128)S(1)}, f32[3,3072]{1,0:T(4,128)}, u32[]{:S(2)}) copy-start(f32[3,3072]{1,0:T(4,128)} %param.36) | copy-start | bytes 110596
  41.8 11.6 %collective-permute-start.4 = (bf16[256,1024]{1,0:T(8,128)(2,1)}, bf16[256,1024]{1,0:T(8,128)(2,1)S(1)}, u32[]{:S(2)}, u32[]{:S(2)}) collective-permute-start(bf16[256,1024]{1,0:T(8,128)(2,1)} %get-tuple-element.97.refs_2_.refs_4_.refs_3_), channel_id=1, source_target_pairs={{0,3},{1,0},{2,1},{3,2},{4,7},{5,4},{6,5},{7,6},{8,11},{9,8},{10,9... | collective-permute-start | bytes 1572872 | tf_op jit(solution)/shard_map/ppermute | solution.py:614
  54.8 11.7 %collective-permute-start.5 = (bf16[256,1024]{1,0:T(8,128)(2,1)}, bf16[256,1024]{1,0:T(8,128)(2,1)S(1)}, u32[]{:S(2)}, u32[]{:S(2)}) collective-permute-start(bf16[256,1024]{1,0:T(8,128)(2,1)} %get-tuple-element.99.refs_3_.refs_5_.refs_4_), channel_id=1, source_target_pairs={{0,3},{1,0},{2,1},{3,2},{4,7},{5,4},{6,5},{7,6},{8,11},{9,8},{10,9... | collective-permute-start | bytes 1572872 | tf_op jit(solution)/shard_map/ppermute | solution.py:614
  68.0 145.4 %reduce-scatter.4.cloned.1.call-start = ((), (), s32[]{:S(2)}) async-start(), calls=%async_computation.11 | async-start | bytes 2621440 | tf_op jit(solution)/shard_map/reduce_scatter | solution.py:769
  68.0 17.2 %collective-permute-start.6 = (bf16[256,1024]{1,0:T(8,128)(2,1)}, bf16[256,1024]{1,0:T(8,128)(2,1)S(1)}, u32[]{:S(2)}, u32[]{:S(2)}) collective-permute-start(bf16[256,1024]{1,0:T(8,128)(2,1)} %get-tuple-element.104.refs_0_), channel_id=1, source_target_pairs={{0,3},{1,0},{2,1},{3,2},{4,7},{5,4},{6,5},{7,6},{8,11},{9,8},{10,9... | collective-permute-start | bytes 1572872 | tf_op jit(solution)/shard_map/ppermute | solution.py:614
  101.7 13.5 %copy-start.14 = (bf16[256,1024]{1,0:T(8,128)(2,1)S(1)}, bf16[256,1024]{1,0:T(8,128)(2,1)}, u32[]{:S(2)}) copy-start(bf16[256,1024]{1,0:T(8,128)(2,1)} %get-tuple-element.116.refs_13_) | copy-start | bytes 1572868
  101.7 14.9 %copy-start.2 = (bf16[256,1024]{1,0:T(8,128)(2,1)S(1)}, bf16[256,1024]{1,0:T(8,128)(2,1)}, u32[]{:S(2)}) copy-start(bf16[256,1024]{1,0:T(8,128)(2,1)} %get-tuple-element.115.refs_12_) | copy-start | bytes 1572868
  106.0 20.4 %collective-permute-start.10 = (bf16[256,1024]{1,0:T(8,128)(2,1)}, bf16[256,1024]{1,0:T(8,128)(2,1)S(1)}, u32[]{:S(2)}, u32[]{:S(2)}) collective-permute-start(bf16[256,1024]{1,0:T(8,128)(2,1)} %get-tuple-element.113.refs_1_), channel_id=1, source_target_pairs={{0,16},{4,20},{8,24},{12,28},{16,0},{20,4},{24,8},{28,12},{1,17},{... | collective-permute-start | bytes 1572872 | tf_op jit(solution)/shard_map/ppermute | solution.py:611
  108.4 23.0 %collective-permute-start.8 = (bf16[256,1024]{1,0:T(8,128)(2,1)}, bf16[256,1024]{1,0:T(8,128)(2,1)S(1)}, u32[]{:S(2)}, u32[]{:S(2)}) collective-permute-start(bf16[256,1024]{1,0:T(8,128)(2,1)} %get-tuple-element.113.refs_1_), channel_id=1, source_target_pairs={{0,8},{4,12},{8,0},{12,4},{16,24},{20,28},{24,16},{28,20},{1,9},{5... | collective-permute-start | bytes 1572872 | tf_op jit(solution)/shard_map/ppermute | solution.py:611
  115.1 16.3 %collective-permute-start.7 = (bf16[256,1024]{1,0:T(8,128)(2,1)}, bf16[256,1024]{1,0:T(8,128)(2,1)S(1)}, u32[]{:S(2)}, u32[]{:S(2)}) collective-permute-start(bf16[256,1024]{1,0:T(8,128)(2,1)} %get-tuple-element.113.refs_1_), channel_id=1, source_target_pairs={{0,4},{4,0},{8,12},{12,8},{16,20},{20,16},{24,28},{28,24},{1,5},{5... | collective-permute-start | bytes 1572872 | tf_op jit(solution)/shard_map/ppermute | solution.py:611
  115.1 25.6 %collective-permute-start.16 = (bf16[256,1024]{1,0:T(8,128)(2,1)S(1)}, bf16[256,1024]{1,0:T(8,128)(2,1)S(1)}, u32[]{:S(2)}, u32[]{:S(2)}) collective-permute-start(bf16[256,1024]{1,0:T(8,128)(2,1)S(1)} %copy-done.14), channel_id=1, source_target_pairs={{0,3},{1,0},{2,1},{3,2},{4,7},{5,4},{6,5},{7,6},{8,11},{9,8},{10,9... | collective-permute-start | bytes 1572872 | tf_op jit(solution)/shard_map/ppermute | solution.py:614
  116.6 30.5 %collective-permute-start.17 = (bf16[256,1024]{1,0:T(8,128)(2,1)S(1)}, bf16[256,1024]{1,0:T(8,128)(2,1)S(1)}, u32[]{:S(2)}, u32[]{:S(2)}) collective-permute-start(bf16[256,1024]{1,0:T(8,128)(2,1)S(1)} %copy-done.2), channel_id=1, source_target_pairs={{0,1},{1,2},{2,3},{3,0},{4,5},{5,6},{6,7},{7,4},{8,9},{9,10},{10,1... | collective-permute-start | bytes 1572872 | tf_op jit(solution)/shard_map/ppermute | solution.py:614
  126.4 22.4 %copy-start.27 = (bf16[256,1024]{1,0:T(8,128)(2,1)}, bf16[256,1024]{1,0:T(8,128)(2,1)S(1)}, u32[]{:S(2)}) copy-start(bf16[256,1024]{1,0:T(8,128)(2,1)S(1)} %collective-permute-done.10.refs_5_) | copy-start | bytes 1572868
  126.4 16.3 %collective-permute-start.12 = (bf16[128,1024]{1,0:T(8,128)(2,1)S(1)}, bf16[128,1024]{1,0:T(8,128)(2,1)S(1)}, u32[]{:S(2)}, u32[]{:S(2)}) collective-permute-start(bf16[128,1024]{1,0:T(8,128)(2,1)S(1)} %slice.8), channel_id=1, source_target_pairs={{0,8},{4,12},{8,0},{12,4},{16,24},{20,28},{24,16},{28,20},{1,9},{5... | collective-permute-start | bytes 786440 | tf_op jit(solution)/shard_map/ppermute | solution.py:611
  131.4 17.4 %copy-start.28 = (bf16[256,1024]{1,0:T(8,128)(2,1)}, bf16[256,1024]{1,0:T(8,128)(2,1)S(1)}, u32[]{:S(2)}) copy-start(bf16[256,1024]{1,0:T(8,128)(2,1)S(1)} %collective-permute-done.8.refs_3_) | copy-start | bytes 1572868
  131.4 15.7 %collective-permute-start.11 = (bf16[256,1024]{1,0:T(8,128)(2,1)S(1)}, bf16[256,1024]{1,0:T(8,128)(2,1)S(1)}, u32[]{:S(2)}, u32[]{:S(2)}) collective-permute-start(bf16[256,1024]{1,0:T(8,128)(2,1)S(1)} %collective-permute-done.10.refs_5_), channel_id=1, source_target_pairs={{0,4},{4,0},{8,12},{12,8},{16,20},{20,16},{24,28},{28,24},{1,5},{5... | collective-permute-start | bytes 1572872 | tf_op jit(solution)/shard_map/ppermute | solution.py:611
  131.5 17.3 %copy-start.34 = (bf16[256,1024]{1,0:T(8,128)(2,1)}, bf16[256,1024]{1,0:T(8,128)(2,1)S(1)}, u32[]{:S(2)}) copy-start(bf16[256,1024]{1,0:T(8,128)(2,1)S(1)} %collective-permute-done.7.refs_2_) | copy-start | bytes 1572868
  131.5 15.7 %collective-permute-start.9 = (bf16[256,1024]{1,0:T(8,128)(2,1)S(1)}, bf16[256,1024]{1,0:T(8,128)(2,1)S(1)}, u32[]{:S(2)}, u32[]{:S(2)}) collective-permute-start(bf16[256,1024]{1,0:T(8,128)(2,1)S(1)} %collective-permute-done.8.refs_3_), channel_id=1, source_target_pairs={{0,4},{4,0},{8,12},{12,8},{16,20},{20,16},{24,28},{28,24},{1,5},{5... | collective-permute-start | bytes 1572872 | tf_op jit(solution)/shard_map/ppermute | solution.py:611
  140.7 8.1 %copy-start.35 = (bf16[256,1024]{1,0:T(8,128)(2,1)}, bf16[256,1024]{1,0:T(8,128)(2,1)S(1)}, u32[]{:S(2)}) copy-start(bf16[256,1024]{1,0:T(8,128)(2,1)S(1)} %collective-permute-done.16.refs_14_) | copy-start | bytes 1572868
  140.7 6.4 %collective-permute-start.13 = (bf16[128,1024]{1,0:T(8,128)(2,1)S(1)}, bf16[128,1024]{1,0:T(8,128)(2,1)S(1)}, u32[]{:S(2)}, u32[]{:S(2)}) collective-permute-start(bf16[128,1024]{1,0:T(8,128)(2,1)S(1)} %slice.9), channel_id=1, source_target_pairs={{0,16},{4,20},{8,24},{12,28},{16,0},{20,4},{24,8},{28,12},{1,17},{... | collective-permute-start | bytes 786440 | tf_op jit(solution)/shard_map/ppermute | solution.py:611
  142.7 5.3 %copy-start.41 = (bf16[128,1024]{1,0:T(8,128)(2,1)}, bf16[128,1024]{1,0:T(8,128)(2,1)S(1)}, u32[]{:S(2)}) copy-start(bf16[128,1024]{1,0:T(8,128)(2,1)S(1)} %collective-permute-done.12.refs_7_) | copy-start | bytes 786436
  142.7 5.3 %collective-permute-start.14 = (bf16[128,1024]{1,0:T(8,128)(2,1)S(1)}, bf16[128,1024]{1,0:T(8,128)(2,1)S(1)}, u32[]{:S(2)}, u32[]{:S(2)}) collective-permute-start(bf16[128,1024]{1,0:T(8,128)(2,1)S(1)} %collective-permute-done.12.refs_7_), channel_id=1, source_target_pairs={{0,4},{4,0},{8,12},{12,8},{16,20},{20,16},{24,28},{28,24},{1,5},{5... | collective-permute-start | bytes 786440 | tf_op jit(solution)/shard_map/ppermute | solution.py:611
  147.1 1.7 collective-permute-start.15
  170.2 92.5 %reduce-scatter.6.cloned.1.call-start = ((), (), s32[]{:S(2)}) async-start(), calls=%async_computation.12 | async-start | bytes 2359296 | tf_op jit(solution)/shard_map/reduce_scatter | solution.py:629
  170.2 4.4 %collective-permute-start.19 = (bf16[1024,1024]{1,0:T(8,128)(2,1)}, bf16[1024,1024]{1,0:T(8,128)(2,1)S(1)}, u32[]{:S(2)}, u32[]{:S(2)}) collective-permute-start(bf16[1024,1024]{1,0:T(8,128)(2,1)} %get-tuple-element.123), channel_id=1, source_target_pairs={{0,4},{4,0},{8,12},{12,8},{16,20},{20,16},{24,28},{28,24},{1,5},{5... | collective-permute-start | bytes 6291464 | tf_op jit(solution)/shard_map/ppermute | solution.py:611
  171.6 10.1 %collective-permute-start.18 = (bf16[1024,1024]{1,0:T(8,128)(2,1)S(1)}, bf16[1024,1024]{1,0:T(8,128)(2,1)S(1)}, u32[]{:S(2)}, u32[]{:S(2)}) collective-permute-start(bf16[1024,1024]{1,0:T(8,128)(2,1)S(1)} %copy-done.15), channel_id=1, source_target_pairs={{0,4},{4,0},{8,12},{12,8},{16,20},{20,16},{24,28},{28,24},{1,5},{5... | collective-permute-start | bytes 6291464 | tf_op jit(solution)/shard_map/ppermute | solution.py:611
  179.6 8.8 %collective-permute-start.22 = (bf16[128,1024]{1,0:T(8,128)(2,1)}, bf16[128,1024]{1,0:T(8,128)(2,1)S(1)}, u32[]{:S(2)}, u32[]{:S(2)}) collective-permute-start(bf16[128,1024]{1,0:T(8,128)(2,1)} %get-tuple-element.133), channel_id=1, source_target_pairs={{0,8},{4,12},{8,0},{12,4},{16,24},{20,28},{24,16},{28,20},{1,9},{5... | collective-permute-start | bytes 786440 | tf_op jit(solution)/shard_map/ppermute | solution.py:611
  179.7 9.0 %collective-permute-start.23 = (bf16[128,1024]{1,0:T(8,128)(2,1)}, bf16[128,1024]{1,0:T(8,128)(2,1)S(1)}, u32[]{:S(2)}, u32[]{:S(2)}) collective-permute-start(bf16[128,1024]{1,0:T(8,128)(2,1)} %get-tuple-element.134), channel_id=1, source_target_pairs={{0,16},{4,20},{8,24},{12,28},{16,0},{20,4},{24,8},{28,12},{1,17},{... | collective-permute-start | bytes 786440 | tf_op jit(solution)/shard_map/ppermute | solution.py:611
  191.8 13.9 %collective-permute-start.24 = (bf16[256,1024]{1,0:T(8,128)(2,1)}, bf16[256,1024]{1,0:T(8,128)(2,1)S(1)}, u32[]{:S(2)}, u32[]{:S(2)}) collective-permute-start(bf16[256,1024]{1,0:T(8,128)(2,1)} %get-tuple-element.135.refs_8_), channel_id=1, source_target_pairs={{0,8},{4,12},{8,0},{12,4},{16,24},{20,28},{24,16},{28,20},{1,9},{5... | collective-permute-start | bytes 1572872 | tf_op jit(solution)/shard_map/ppermute | solution.py:611
  193.6 13.4 %collective-permute-start.25 = (bf16[256,1024]{1,0:T(8,128)(2,1)}, bf16[256,1024]{1,0:T(8,128)(2,1)S(1)}, u32[]{:S(2)}, u32[]{:S(2)}) collective-permute-start(bf16[256,1024]{1,0:T(8,128)(2,1)} %get-tuple-element.136), channel_id=1, source_target_pairs={{0,16},{4,20},{8,24},{12,28},{16,0},{20,4},{24,8},{28,12},{1,17},{... | collective-permute-start | bytes 1572872 | tf_op jit(solution)/shard_map/ppermute | solution.py:611
  217.2 3.7 %copy-start.40 = (bf16[128,1024]{1,0:T(8,128)(2,1)S(1)}, bf16[128,1024]{1,0:T(8,128)(2,1)}, u32[]{:S(2)}) copy-start(bf16[128,1024]{1,0:T(8,128)(2,1)} %get-tuple-element.129) | copy-start | bytes 786436
  217.2 4.8 %copy-start.39 = (bf16[128,1024]{1,0:T(8,128)(2,1)S(1)}, bf16[128,1024]{1,0:T(8,128)(2,1)}, u32[]{:S(2)}) copy-start(bf16[128,1024]{1,0:T(8,128)(2,1)} %get-tuple-element.130) | copy-start | bytes 786436
  217.2 17.1 %all-to-all-start.2 = ((bf16[4,256,256]{2,1,0:T(8,128)(2,1)}), bf16[4,256,256]{2,1,0:T(8,128)(2,1)S(1)}, u32[]{:S(2)}, u32[]{:S(2)}) async-start(bf16[4,256,256]{2,1,0:T(8,128)(2,1)} %bitcast.11), calls=%async_computation.3 | async-start | bytes 1048576 | tf_op jit(solution)/shard_map/all_to_all | solution.py:620
  220.8 110.4 %reduce-scatter.8.cloned.1.call-start = ((), (), s32[]{:S(2)}) async-start(), calls=%async_computation.13 | async-start | bytes 2621440 | tf_op jit(solution)/shard_map/reduce_scatter | solution.py:818
  220.9 6.9 %collective-permute-start.20 = (bf16[128,1024]{1,0:T(8,128)(2,1)S(1)}, bf16[128,1024]{1,0:T(8,128)(2,1)S(1)}, u32[]{:S(2)}, u32[]{:S(2)}) collective-permute-start(bf16[128,1024]{1,0:T(8,128)(2,1)S(1)} %copy-done.40), channel_id=1, source_target_pairs={{0,8},{4,12},{8,0},{12,4},{16,24},{20,28},{24,16},{28,20},{1,9},{5... | collective-permute-start | bytes 786440 | tf_op jit(solution)/shard_map/ppermute | solution.py:611
  222.0 6.8 %collective-permute-start.21 = (bf16[128,1024]{1,0:T(8,128)(2,1)S(1)}, bf16[128,1024]{1,0:T(8,128)(2,1)S(1)}, u32[]{:S(2)}, u32[]{:S(2)}) collective-permute-start(bf16[128,1024]{1,0:T(8,128)(2,1)S(1)} %copy-done.39), channel_id=1, source_target_pairs={{0,16},{4,20},{8,24},{12,28},{16,0},{20,4},{24,8},{28,12},{1,17},{... | collective-permute-start | bytes 786440 | tf_op jit(solution)/shard_map/ppermute | solution.py:611
  263.3 3.2 copy-start.18
  263.8 29.1 %collective-permute-start.26 = (bf16[256,1024]{1,0:T(8,128)(2,1)S(1)}, bf16[256,1024]{1,0:T(8,128)(2,1)S(1)}, u32[]{:S(2)}, u32[]{:S(2)}) collective-permute-start(bf16[256,1024]{1,0:T(8,128)(2,1)S(1)} %copy-done.19), channel_id=1, source_target_pairs={{0,8},{4,12},{8,0},{12,4},{16,24},{20,28},{24,16},{28,20},{1,9},{5... | collective-permute-start | bytes 1572872 | tf_op jit(solution)/shard_map/ppermute | solution.py:611
  265.1 27.8 %collective-permute-start.27 = (bf16[256,1024]{1,0:T(8,128)(2,1)S(1)}, bf16[256,1024]{1,0:T(8,128)(2,1)S(1)}, u32[]{:S(2)}, u32[]{:S(2)}) collective-permute-start(bf16[256,1024]{1,0:T(8,128)(2,1)S(1)} %copy-done.33), channel_id=1, source_target_pairs={{0,16},{4,20},{8,24},{12,28},{16,0},{20,4},{24,8},{28,12},{1,17},{... | collective-permute-start | bytes 1572872 | tf_op jit(solution)/shard_map/ppermute | solution.py:611
  266.5 3.5 %collective-permute-start.28 = (f32[152,256]{1,0:T(8,128)S(1)}, f32[152,256]{1,0:T(8,128)S(1)}, u32[]{:S(2)}, u32[]{:S(2)}) collective-permute-start(f32[152,256]{1,0:T(8,128)S(1)} %copy-done.18), channel_id=1, source_target_pairs={{0,4},{4,0},{8,12},{12,8},{16,20},{20,16},{24,28},{28,24},{1,5},{5... | collective-permute-start | bytes 466952 | tf_op jit(solution)/shard_map/ppermute | solution.py:611
  266.5 26.4 %all-to-all-start.3 = ((bf16[8,256,128]{2,1,0:T(8,128)(2,1)}), bf16[8,256,128]{2,1,0:T(8,128)(2,1)S(1)}, u32[]{:S(2)}, u32[]{:S(2)}) async-start(bf16[8,256,128]{2,1,0:T(8,128)(2,1)} %bitcast.13), calls=%async_computation.5 | async-start | bytes 1048576 | tf_op jit(solution)/shard_map/all_to_all | solution.py:623
  270.1 15.7 %collective-permute-start.29 = (f32[152,256]{1,0:T(8,128)S(1)}, f32[152,256]{1,0:T(8,128)S(1)}, u32[]{:S(2)}, u32[]{:S(2)}) collective-permute-start(f32[152,256]{1,0:T(8,128)S(1)} %add.60), channel_id=1, source_target_pairs={{0,8},{4,12},{8,0},{12,4},{16,24},{20,28},{24,16},{28,20},{1,9},{5... | collective-permute-start | bytes 466952 | tf_op jit(solution)/shard_map/ppermute | solution.py:611
  285.8 6.4 %collective-permute-start.30 = (f32[152,256]{1,0:T(8,128)S(1)}, f32[152,256]{1,0:T(8,128)S(1)}, u32[]{:S(2)}, u32[]{:S(2)}) collective-permute-start(f32[152,256]{1,0:T(8,128)S(1)} %add.61), channel_id=1, source_target_pairs={{0,16},{4,20},{8,24},{12,28},{16,0},{20,4},{24,8},{28,12},{1,17},{... | collective-permute-start | bytes 466952 | tf_op jit(solution)/shard_map/ppermute | solution.py:611
  294.6 3.8 %copy-start.17 = (f32[152,256]{1,0:T(8,128)S(1)}, f32[152,256]{1,0:T(8,128)}, u32[]{:S(2)}) copy-start(f32[152,256]{1,0:T(8,128)} %get-tuple-element.161.refs_1_) | copy-start | bytes 466948
  294.6 5.6 %copy-start.7 = (bf16[1024,128]{1,0:T(8,128)(2,1)S(1)}, bf16[1024,128]{1,0:T(8,128)(2,1)}, u32[]{:S(2)}) copy-start(bf16[1024,128]{1,0:T(8,128)(2,1)} %get-tuple-element.162) | copy-start | bytes 786436
  294.6 33.0 %all-to-all-start.4 = ((bf16[8,768,128]{2,1,0:T(8,128)(2,1)}), bf16[8,768,128]{2,1,0:T(8,128)(2,1)S(1)}, u32[]{:S(2)}, u32[]{:S(2)}) async-start(bf16[8,768,128]{2,1,0:T(8,128)(2,1)} %bitcast.26), calls=%async_computation.7 | async-start | bytes 3145728 | tf_op jit(solution)/shard_map/all_to_all | solution.py:623
  298.4 14.7 %collective-permute-start.31 = (f32[152,256]{1,0:T(8,128)S(1)}, f32[152,256]{1,0:T(8,128)S(1)}, u32[]{:S(2)}, u32[]{:S(2)}) collective-permute-start(f32[152,256]{1,0:T(8,128)S(1)} %copy-done.17), channel_id=1, source_target_pairs={{0,1},{1,0},{2,3},{3,2},{4,5},{5,4},{6,7},{7,6},{8,9},{9,8},{10,11... | collective-permute-start | bytes 466952 | tf_op jit(solution)/shard_map/ppermute | solution.py:617
  298.5 20.8 %collective-permute-start.32 = (f32[152,256]{1,0:T(8,128)S(1)}, f32[152,256]{1,0:T(8,128)S(1)}, u32[]{:S(2)}, u32[]{:S(2)}) collective-permute-start(f32[152,256]{1,0:T(8,128)S(1)} %copy-done.17), channel_id=1, source_target_pairs={{0,2},{1,3},{2,0},{3,1},{4,6},{5,7},{6,4},{7,5},{8,10},{9,11},{10,... | collective-permute-start | bytes 466952 | tf_op jit(solution)/shard_map/ppermute | solution.py:617
  300.9 14.7 %collective-permute-start.34 = (bf16[256,128]{1,0:T(8,128)(2,1)S(1)}, bf16[256,128]{1,0:T(8,128)(2,1)S(1)}, u32[]{:S(2)}, u32[]{:S(2)}) collective-permute-start(bf16[256,128]{1,0:T(8,128)(2,1)S(1)} %get-tuple-element.175), channel_id=1, source_target_pairs={{0,1},{1,2},{2,3},{3,0},{4,5},{5,6},{6,7},{7,4},{8,9},{9,10},{10,1... | collective-permute-start | bytes 196616 | tf_op jit(solution)/shard_map/ppermute | solution.py:614
  301.4 15.6 %collective-permute-start.35 = (bf16[256,128]{1,0:T(8,128)(2,1)S(1)}, bf16[256,128]{1,0:T(8,128)(2,1)S(1)}, u32[]{:S(2)}, u32[]{:S(2)}) collective-permute-start(bf16[256,128]{1,0:T(8,128)(2,1)S(1)} %get-tuple-element.174), channel_id=1, source_target_pairs={{0,2},{1,3},{2,0},{3,1},{4,6},{5,7},{6,4},{7,5},{8,10},{9,11},{10,... | collective-permute-start | bytes 196616 | tf_op jit(solution)/shard_map/ppermute | solution.py:614
  304.1 12.9 %collective-permute-start.36 = (bf16[256,128]{1,0:T(8,128)(2,1)S(1)}, bf16[256,128]{1,0:T(8,128)(2,1)S(1)}, u32[]{:S(2)}, u32[]{:S(2)}) collective-permute-start(bf16[256,128]{1,0:T(8,128)(2,1)S(1)} %get-tuple-element.173), channel_id=1, source_target_pairs={{0,3},{1,0},{2,1},{3,2},{4,7},{5,4},{6,5},{7,6},{8,11},{9,8},{10,9... | collective-permute-start | bytes 196616 | tf_op jit(solution)/shard_map/ppermute | solution.py:614
  313.1 6.2 %copy-start.44 = (f32[152,256]{1,0:T(8,128)}, f32[152,256]{1,0:T(8,128)S(1)}, u32[]{:S(2)}) copy-start(f32[152,256]{1,0:T(8,128)S(1)} %collective-permute-done.31.refs_2_) | copy-start | bytes 466948
  313.1 11.9 %collective-permute-start.33 = (f32[152,256]{1,0:T(8,128)S(1)}, f32[152,256]{1,0:T(8,128)S(1)}, u32[]{:S(2)}, u32[]{:S(2)}) collective-permute-start(f32[152,256]{1,0:T(8,128)S(1)} %collective-permute-done.31.refs_2_), channel_id=1, source_target_pairs={{0,2},{1,3},{2,0},{3,1},{4,6},{5,7},{6,4},{7,5},{8,10},{9,11},{10,... | collective-permute-start | bytes 466952 | tf_op jit(solution)/shard_map/ppermute | solution.py:617
  319.3 5.7 %copy-start.45 = (f32[152,256]{1,0:T(8,128)}, f32[152,256]{1,0:T(8,128)S(1)}, u32[]{:S(2)}) copy-start(f32[152,256]{1,0:T(8,128)S(1)} %collective-permute-done.32.refs_3_) | copy-start | bytes 466948
  328.8 5.8 %copy-start.1 = (f32[64,1024]{1,0:T(8,128)S(1)}, f32[64,1024]{1,0:T(8,128)}, u32[]{:S(2)}) copy-start(f32[64,1024]{1,0:T(8,128)} %param.42) | copy-start | bytes 786436
  (33 other events, 35.2 us)
Sparse Core Ops, SparseCore 0:
  22.1 28.6 all-gather.3
  53.2 27.8 all-gather.5
  83.6 43.6 all-gather.7
  170.3 41.6 reduce-scatter.3
  217.3 39.2 reduce-scatter.5
  263.5 48.5 reduce-scatter.7

commit v2 on v1

--- a/solution.py
+++ b/solution.py
@@ -26,6 +26,8 @@
 GAINS = 8
 SHARED = 64
 PACKED = OWNED + GAINS + SHARED
+
+SPARE = 16
 
 
 def nt_dot(left, right):
@@ -173,7 +175,9 @@
 def side_by_side(ref, out):
     count, lane = ref.shape[0] // CUBE, ref.shape[1]
     for m in range(CUBE):
-        out[:, pl.ds(m * lane, lane)] = ref[pl.ds(m * count, count), :]
+        out[pl.ds(0, count), pl.ds(m * lane, lane)] = ref[pl.ds(m * count, count), :]
+    if out.shape[0] > count:
+        out[pl.ds(count, out.shape[0] - count), :] = jnp.zeros((out.shape[0] - count, out.shape[1]), out.dtype)
 
 
 def decay_of(info, times, channels, width):
@@ -281,7 +285,7 @@
     out_kept, out_given, back_kept, back_given, grads, up_sum, down_sum = refs
     own, sib, across, across_sib, along, along_sib, top, low, top_sib, low_sib = rows_in
     rows = own.shape[0]
-    part = slots[0].shape[0] // 2
+    part = (slots[0].shape[0] - SPARE) // 2
     ups = jnp.concatenate([slot[pl.ds(0, part), :] for slot in slots], 0)
     downs = jnp.concatenate([slot[pl.ds(part, part), :] for slot in slots], 0)
     chips = ((own, sib), (across, across_sib), (along, along_sib), (top, low, top_sib, low_sib))
@@ -524,7 +528,7 @@
 ):
     place = info[2]
     for j, ref in enumerate((s0, s1, s2, s3)):
-        slots[place ^ j] = ref[...]
+        slots[place ^ j] = ref[...].astype(f32)
     channels = s0.shape[1]
     inner = middle.shape[0]
     for z in range(RING):
@@ -553,7 +557,7 @@
     refs[count][...] = jnp.zeros_like(refs[count])
 
 
-def run(kernel, outs, *args, scratch=(), name, micros=2.0, limit=56, after=()):
+def run(kernel, outs, *args, scratch=(), name, micros=2.0, limit=62, after=()):
     place = lambda a: pltpu.SMEM if a.dtype == jnp.int32 else pltpu.VMEM
     shapes = [jax.ShapeDtypeStruct(*o) for o in outs]
     count = len(args)
@@ -667,6 +671,7 @@
             out_specs=[pl.BlockSpec(memory_space=pltpu.VMEM)]
             + [pl.BlockSpec(memory_space=pl.ANY)] * len(values),
             input_output_aliases={i: i + 1 for i in range(len(values))},
+            compiler_params=pltpu.CompilerParams(vmem_limit_bytes=62 * 2**20),
             name="phase",
         )(*values, *after)
         latest[:] = [mark]
@@ -715,7 +720,7 @@
     (normed_slots[1],) = phase(normed_slots[1], after=[layer_got])
     normed_slots.append(ring(normed_slots[1], -1))
     (layer_own,) = step(
-        side_by_side, [((2 * hidden // CUBE, width), bf16)], layer_got, name="layer_own", micros=0.2
+        side_by_side, [((2 * hidden // CUBE + SPARE, width), bf16)], layer_got, name="layer_own", micros=0.2
     )
     (normed_slots[2],) = phase(normed_slots[2], after=[lags, skip])
     normed_slots.append(ring(normed_slots[2], -1))
@@ -754,6 +759,7 @@
 
     second_sib, across, along = (hop(second, bit) for bit in (1, 2, 4))
     half = rows // 2
+    across, along = phase(across, along, after=[second_sib, *layer_slots[2:]])
     top, low = hop(along[:half], 2), hop(across[half:], 4)
     across_sib, along_sib, top_sib, low_sib = (hop(v, 1) for v in (across, along, top, low))
     wide = CUBE * rows // 2
@@ -833,6 +839,7 @@
         lax.dynamic_slice_in_dim(out_grad, (ring_place + j) % RING * channels, channels) for j in range(RING)
     ]
     out_slots = [out_slots[0]] + [ring(out_slots[j], j) for j in range(1, RING)]
+    packed = packed.astype(bf16)
     packed_slots = [packed, near_ring(packed, 1)]
     packed_slots += [near_ring(v, 2) for v in packed_slots]
     up_grad, down_grad = step(
@@ -841,7 +848,11 @@
     (block_output,) = step(
         finish_kernel, [((rows, width), bf16)], residual, *out_parts, name="finish", micros=0.1
     )
+    (input_grad,) = step(
+        end_kernel, [((rows, width), bf16)], grad_normed, inputs, gain_one, grad_res, name="end", micros=1
+    )
     (out_grad,) = step(out_end_kernel, [((channels, lane), f32)], *out_slots, name="out_end")
+    (in_grad,) = step(in_end_kernel, [((3, lane, channels), f32)], in_grad, name="in_end")
     small_grads = step(
         unpack_kernel,
         [
@@ -859,10 +870,6 @@
         scratch=[((RING, PACKED, channels), f32)],
         name="unpack",
     )
-    (in_grad,) = step(in_end_kernel, [((3, lane, channels), f32)], in_grad, name="in_end")
-    (input_grad,) = step(
-        end_kernel, [((rows, width), bf16)], grad_normed, inputs, gain_one, grad_res, name="end", micros=1
-    )
     return (
         block_output,
         input_grad,

time: 348 us -> 339 us (0.974)
  starting transfers between devices: 70.1 us -> 64 us
  waiting for transfers between devices: 86.5 us -> 81.5 us
    ppermute x22, waiting for transfers between devices: 49.2 us -> 65 us  [hop(): return lax.ppermute(value, 'seq', pairs)]
    ppermute x22, starting transfers between devices: 31.8 us -> 17.5 us  [hop(): return lax.ppermute(value, 'seq', pairs)]
    ppermute x12, waiting for transfers between devices: 20.5 us -> 7.99 us  [ring(): lax.ppermute(value, 'pos', [(i, (i + shift) % RING) for i in range(RING)])]
    ppermute x3, waiting for transfers between devices: 8.69 us -> 0.01 us  [near_ring(): return lax.ppermute(value, 'pos', [(i, i ^ bit) for i in range(RING)])]
    ppermute x12, starting transfers between devices: 21.7 us -> 26.8 us  [ring(): lax.ppermute(value, 'pos', [(i, (i + shift) % RING) for i in range(RING)])]
    unnamed x102 -> x86, local copies, waits for them, and re-layouts: 16.1 us -> 14.6 us
  transfers between devices with their start and end apart: 47 -> 47, of which waited for: 20 -> 18; matrix products, arithmetic and copies ran while one was open for 1% -> 2% of each run, Pallas kernels for 30% -> 32%
where the time goes in v2:
time: 339 us; the launch traced here: 333 us
  Pallas kernels  136 us (40%)
  waiting for transfers between devices  81.5 us (24%)
  starting transfers between devices  64 us (19%)
  local copies, waits for them, and re-layouts  19.2 us (6%)
  blocking collectives  15.4 us (5%)
  between operations  15.4 us (5%)
    pallas_call x25, Pallas kernels, run(): pl.pallas_call(body, out_shape=shapes, in_specs=[pl.BlockSpec(memory_spac...  130 us
    ppermute x22, waiting for transfers between devices, hop(): return lax.ppermute(value, 'seq', pairs)  65 us
    ppermute x12, starting transfers between devices, ring(): lax.ppermute(value, 'pos', [(i, (i + shift) % RING) for i in range(RING)])  26.8 us
    ppermute x22, starting transfers between devices, hop(): return lax.ppermute(value, 'seq', pairs)  17.5 us
    all_to_all x1, blocking collectives, to_rows(): return lax.all_to_all(value, 'pos', 0, 0, tiled=True)  15.4 us
    unnamed x86, local copies, waits for them, and re-layouts  14.6 us
    all_to_all x3, starting transfers between devices, swap(): lax.all_to_all(value, 'seq', 0, 0, axis_index_groups=members, tiled=True)  10.9 us
    ppermute x12, waiting for transfers between devices, ring(): lax.ppermute(value, 'pos', [(i, (i + shift) % RING) for i in range(RING)])  7.99 us
  transfers between devices with their start and end apart: 47, of which 18 were waited for; matrix products, arithmetic and copies ran while one was open for 2% of the time, Pallas kernels for 32%

profile of v2, /device:TPU:0, one launch (start us, length us, event | category | flops | bytes accessed | tf_op | source)
XLA Modules:
  0.0 332.6 jit_solution(10181289512717816792)
XLA Ops:
  7.2 5.1 %collective-permute-start.1 = (bf16[256,128]{1,0:T(8,128)(2,1)}, bf16[256,128]{1,0:T(8,128)(2,1)S(1)}, u32[]{:S(2)}, u32[]{:S(2)}) collective-permute-start(bf16[256,128]{1,0:T(8,128)(2,1)} %refs_3_.3), channel_id=1, source_target_pairs={{0,3},{1,0},{2,1},{3,2},{4,7},{5,4},{6,5},{7,6},{8,11},{9,8},{10,9... | collective-permute-start | bytes 196616 | tf_op jit(solution)/shard_map/ppermute | solution.py:618
  13.4 2.8 rows.1
  16.1 2.9 collective-permute-done.2.refs_5_
  19.7 2.2 weights.1
  22.7 1.9 collective-permute-start
  24.6 3.7 %all-to-all-start = ((bf16[8,256,128]{2,1,0:T(8,128)(2,1)}), bf16[8,256,128]{2,1,0:T(8,128)(2,1)S(1)}, u32[]{:S(2)}, u32[]{:S(2)}) async-start(bf16[8,256,128]{2,1,0:T(8,128)(2,1)} %bitcast.37), calls=%async_computation | async-start | bytes 1048576 | tf_op jit(solution)/shard_map/all_to_all | solution.py:627
  28.4 5.2 %hidden.1.refs_1_.refs_2_ = f32[1024,256]{1,0:T(8,128)} custom-call(f32[1024,33]{1,0:T(8,128)} %constant.83.clone.refs_0_.refs_3_, f32[33,64]{1,0:T(8,128)} %refs_1_.5, f32[1,64]{1,0:T(1,128)} %bitcast.45, f32[64,64]{1,0:T(8,128)} %refs_5_.4, f32[1,64]{1,0:T(1,128)} %bitcast.46, bf16[768,128]{1,0:T(8,128)(2,1)} %get-tuple-element.98.refs_5_), custom_call_target="tpu_custom_call" | custom-call | flops 5000000000 | bytes 15000000 | tf_op jit(solution)/shard_map/hidden/pallas_call | solution.py:568
  33.6 6.6 %all-to-all-done = bf16[8,256,128]{2,1,0:T(8,128)(2,1)S(1)} async-done(((bf16[8,256,128]{2,1,0:T(8,128)(2,1)}), bf16[8,256,128]{2,1,0:T(8,128)(2,1)S(1)}, u32[]{:S(2)}, u32[]{:S(2)}) %all-to-all-start) | async-done | bytes 524320 | tf_op jit(solution)/shard_map/all_to_all | solution.py:627
  41.8 1.3 collective-permute-start.4
  44.4 1.3 dynamic_slice.22
  46.4 2.0 layer_own.1.refs_1_.refs_0_
  48.4 5.1 %collective-permute-done.4.refs_0_ = bf16[256,1024]{1,0:T(8,128)(2,1)S(1)} collective-permute-done((bf16[256,1024]{1,0:T(8,128)(2,1)}, bf16[256,1024]{1,0:T(8,128)(2,1)S(1)}, u32[]{:S(2)}, u32[]{:S(2)}) %collective-permute-start.4) | collective-permute-done | bytes 524320 | tf_op jit(solution)/shard_map/ppermute | solution.py:618
  54.8 2.5 collective-permute-start.5
  57.9 8.6 %taps.1.refs_2_.refs_8_.refs_7_ = f32[2,1024,256]{2,1,0:T(8,128)} custom-call(s32[4]{0:T(128)} %pad_add_fusion.refs_0_, f32[1024,256]{1,0:T(8,128)} %hidden.1.refs_1_.refs_2_, f32[1024,1]{1,0:T(8,128)} %constant.84.clone.refs_2_.refs_4_, f32[64,256]{1,0:T(8,128)} %constant_dynamic-slice_fusion.4.refs_3_.refs_6_, ...), custom_call_target="tpu_custom_call" | custom-call | flops 5000000000 | bytes 15000000 | tf_op jit(solution)/shard_map/taps/pallas_call | solution.py:568
  68.0 3.1 collective-permute-start.6
  71.1 14.1 %conv.1 = (bf16[1024,768]{1,0:T(8,128)(2,1)}, f32[1024,256]{1,0:T(8,128)}, f32[2,1024,256]{2,1,0:T(8,128)}, bf16[1024,256]{1,0:T(8,128)(2,1)}, bf16[768,1024]{1,0:T(8,128)(2,1)}) custom-call(s32[4]{0:T(128)} %pad_add_fusion.refs_0_, bf16[256,1024]{1,0:T(8,128)(2,1)} %get-tuple-element.97.refs_7_.refs_1_.refs_3_.refs_2_, ...), custom_call_target="tpu_custom_call" | custom-call | flops 14000000000 | bytes 42000000 | tf_op jit(solution)/shard_map/conv/pallas_call | solution.py:568
  86.6 15.4 %all_to_all.55 = bf16[4,256,256]{2,1,0:T(8,128)(2,1)} all-to-all(bf16[4,256,256]{2,1,0:T(8,128)(2,1)} %bitcast.34), channel_id=1, replica_groups=mesh['seq'=8,'pos'=4] {'pos'}, dimensions={0} | all-to-all | bytes 1048576 | tf_op jit(solution)/shard_map/all_to_all | solution.py:624
  102.6 7.5 %collective-permute-start.10 = (bf16[272,1024]{1,0:T(8,128)(2,1)}, bf16[272,1024]{1,0:T(8,128)(2,1)S(1)}, u32[]{:S(2)}, u32[]{:S(2)}) collective-permute-start(bf16[272,1024]{1,0:T(8,128)(2,1)} %get-tuple-element.117.refs_13_), channel_id=1, source_target_pairs={{0,3},{1,0},{2,1},{3,2},{4,7},{5,4},{6,5},{7,6},{8,11},{9,8},{10,9... | collective-permute-start | bytes 1671176 | tf_op jit(solution)/shard_map/ppermute | solution.py:618
  110.6 4.3 %out.1 = (f32[256,1024]{1,0:T(8,128)}, bf16[256,1024]{1,0:T(8,128)(2,1)}) custom-call(s32[4]{0:T(128)} %pad_add_fusion.refs_0_, bf16[1024,256]{1,0:T(8,128)(2,1)} %bitcast.28, bf16[8192,128]{1,0:T(8,128)(2,1)} %all-gather.6.cloned.1.call-done.refs_4_.refs_2_.refs_7_, bf16[256,1024]{1,0:T(8,128)(2,1)} %get-tuple-element.111.refs_3_.refs_1_, f32[1024]{0:T(1024)} %refs_5_.3, ...), custom_call_target="tpu_custom_call" | custom-call | flops 200000000 | bytes 600000 | tf_op jit(solution)/shard_map/out/pallas_call | solution.py:568
  114.9 2.7 collective-permute-start.8
  117.6 12.8 %collective-permute-done.8.refs_0_ = bf16[256,1024]{1,0:T(8,128)(2,1)S(1)} collective-permute-done((bf16[256,1024]{1,0:T(8,128)(2,1)}, bf16[256,1024]{1,0:T(8,128)(2,1)S(1)}, u32[]{:S(2)}, u32[]{:S(2)}) %collective-permute-start.8) | collective-permute-done | bytes 524320 | tf_op jit(solution)/shard_map/ppermute | solution.py:615
  130.4 1.5 collective-permute-done.9.refs_1_
  135.5 3.2 collective-permute-start.14
  138.9 6.7 %collective-permute-done.14.refs_7_ = bf16[128,1024]{1,0:T(8,128)(2,1)S(1)} collective-permute-done((bf16[128,1024]{1,0:T(8,128)(2,1)S(1)}, bf16[128,1024]{1,0:T(8,128)(2,1)S(1)}, u32[]{:S(2)}, u32[]{:S(2)}) %collective-permute-start.14) | collective-permute-done | bytes 262176 | tf_op jit(solution)/shard_map/ppermute | solution.py:615
  145.7 1.7 collective-permute-done.15.refs_8_
  149.7 20.6 %layer.1 = (bf16[1024,1024]{1,0:T(8,128)(2,1)}, bf16[1024,1024]{1,0:T(8,128)(2,1)}, bf16[1024,1024]{1,0:T(8,128)(2,1)}, bf16[1024,1024]{1,0:T(8,128)(2,1)}, bf16[1024,1024]{1,0:T(8,128)(2,1)}) custom-call(s32[4]{0:T(128)} %pad_add_fusion.refs_0_, bf16[256,1024]{1,0:T(8,128)(2,1)} %get-tuple-element.116.refs_1_, bf16[256,1024]{1,0:T(8,128)(2,1)} %copy-done.18, ...), custom_call_target="tpu_custom_call" | custom-call | flops 22000001024 | bytes 66000000 | tf_op jit(solution)/shard_map/layer/pallas_call | solution.py:568
  171.0 1.5 copy-done.11
  173.0 5.3 %collective-permute-done.19.refs_1_ = bf16[1024,1024]{1,0:T(8,128)(2,1)} collective-permute-done((bf16[1024,1024]{1,0:T(8,128)(2,1)S(1)}, bf16[1024,1024]{1,0:T(8,128)(2,1)}, u32[]{:S(2)}, u32[]{:S(2)}) %collective-permute-start.19) | collective-permute-done | bytes 2097184 | tf_op jit(solution)/shard_map/ppermute | solution.py:615
  178.3 3.6 %share.2 = (bf16[256,1024]{1,0:T(8,128)(2,1)}, bf16[256,1024]{1,0:T(8,128)(2,1)}, bf16[256,1024]{1,0:T(8,128)(2,1)}, bf16[128,1024]{1,0:T(8,128)(2,1)}, bf16[128,1024]{1,0:T(8,128)(2,1)}) custom-call(bf16[1024,1024]{1,0:T(8,128)(2,1)} %get-tuple-element.128.refs_0_, bf16[1024,1024]{1,0:T(8,128)(2,1)} %collective-permute-done.19.refs_1_, ...), custom_call_target="tpu_custom_call" | custom-call | flops 100000000 | bytes 300000 | tf_op jit(solution)/shard_map/share/pallas_call | solution.py:568
  182.7 3.7 %share.3 = (bf16[256,1024]{1,0:T(8,128)(2,1)}, bf16[256,1024]{1,0:T(8,128)(2,1)}, bf16[256,1024]{1,0:T(8,128)(2,1)}, bf16[128,1024]{1,0:T(8,128)(2,1)}, bf16[128,1024]{1,0:T(8,128)(2,1)}) custom-call(bf16[1024,1024]{1,0:T(8,128)(2,1)} %get-tuple-element.123.refs_3_.refs_0_, bf16[1024,1024]{1,0:T(8,128)(2,1)} %collective-permute-done.18.refs_1_, ...), custom_call_target="tpu_custom_call" | custom-call | flops 100000000 | bytes 300000 | tf_op jit(solution)/shard_map/share/pallas_call | solution.py:568
  186.4 4.2 %collective-permute-done.22.refs_2_ = bf16[128,1024]{1,0:T(8,128)(2,1)S(1)} collective-permute-done((bf16[128,1024]{1,0:T(8,128)(2,1)}, bf16[128,1024]{1,0:T(8,128)(2,1)S(1)}, u32[]{:S(2)}, u32[]{:S(2)}) %collective-permute-start.22) | collective-permute-done | bytes 262176 | tf_op jit(solution)/shard_map/ppermute | solution.py:615
  191.7 2.4 turn.2
  194.1 1.3 collective-permute-start.24
  195.8 11.4 %collective-permute-done.24.refs_2_ = bf16[256,1024]{1,0:T(8,128)(2,1)S(1)} collective-permute-done((bf16[256,1024]{1,0:T(8,128)(2,1)}, bf16[256,1024]{1,0:T(8,128)(2,1)S(1)}, u32[]{:S(2)}, u32[]{:S(2)}) %collective-permute-start.24) | collective-permute-done | bytes 524320 | tf_op jit(solution)/shard_map/ppermute | solution.py:615
  209.0 5.5 %branch.1 = (f32[256,1024]{1,0:T(8,128)}, bf16[256,1024]{1,0:T(8,128)(2,1)}, f32[1,1024]{1,0:T(1,128)}, bf16[1024,256]{1,0:T(8,128)(2,1)}) custom-call(s32[4]{0:T(128)} %pad_add_fusion.refs_0_, bf16[256,1024]{1,0:T(8,128)(2,1)} %get-tuple-element.131.refs_2_.refs_1_, bf16[256,1024]{1,0:T(8,128)(2,1)} %copy-done.20, bf16[256,1024]{1,0:T(8,128)(2,1)} %copy-done.21, ...), custom_call_target="tpu_custom_call" | custom-call | flops 200000000 | bytes 600000 | tf_op jit(solution)/shard_map/branch/pallas_call | solution.py:568
  215.1 3.2 out_grad.1.refs_4_
  218.4 3.8 %all-to-all-start.2 = ((bf16[4,256,256]{2,1,0:T(8,128)(2,1)}), bf16[4,256,256]{2,1,0:T(8,128)(2,1)S(1)}, u32[]{:S(2)}, u32[]{:S(2)}) async-start(bf16[4,256,256]{2,1,0:T(8,128)(2,1)} %bitcast.11), calls=%async_computation.3 | async-start | bytes 1048576 | tf_op jit(solution)/shard_map/all_to_all | solution.py:624
  222.2 1.2 collective-permute-start.20
  223.6 5.0 %collective-permute-done.20.refs_2_ = bf16[128,1024]{1,0:T(8,128)(2,1)S(1)} collective-permute-done((bf16[128,1024]{1,0:T(8,128)(2,1)S(1)}, bf16[128,1024]{1,0:T(8,128)(2,1)S(1)}, u32[]{:S(2)}, u32[]{:S(2)}) %collective-permute-start.20) | collective-permute-done | bytes 262176 | tf_op jit(solution)/shard_map/ppermute | solution.py:615
  228.6 1.2 collective-permute-done.21.refs_3_
  230.5 2.4 turn.3
  232.9 1.9 layer_sum.1.refs_17_.refs_2_
  236.0 15.7 %back.1 = (bf16[1024,768]{1,0:T(8,128)(2,1)}, f32[1024,256]{1,0:T(8,128)}, f32[16,256]{1,0:T(8,128)}) custom-call(s32[4]{0:T(128)} %pad_add_fusion.refs_0_, bf16[1024,256]{1,0:T(8,128)(2,1)} %bitcast.36, bf16[1024,768]{1,0:T(8,128)(2,1)} %get-tuple-element.108.refs_2_, f32[1024,256]{1,0:T(8,128)} %get-tuple-element.151.refs_3_, ...), custom_call_target="tpu_custom_call" | custom-call | flops 15000000512 | bytes 45000000 | tf_op jit(solution)/shard_map/back/pallas_call | solution.py:568
  251.7 6.1 %pack.1.refs_8_ = f32[152,256]{1,0:T(8,128)} custom-call(s32[4]{0:T(128)} %pad_add_fusion.refs_0_, f32[1024,256]{1,0:T(8,128)} %get-tuple-element.155.refs_1_, f32[1024,256]{1,0:T(8,128)} %hidden.1.refs_1_.refs_2_, f32[1024,33]{1,0:T(8,128)} %constant.83.clone.refs_0_.refs_3_, f32[1024,1]{1,0:T(8,128)} %constant.84.clone.refs_2_.refs_4_, f32[64,64]{1,0:T(8,128)} %refs_5_.4, ...), custom_call_target="tpu_custom_call" | custom-call | flops 100000000 | bytes 300000 | tf_op jit(solution)/shard_map/pack/pallas_call | solution.py:568
  257.8 5.9 %normed.1 = (bf16[1024,1024]{1,0:T(8,128)(2,1)}, f32[152,256]{1,0:T(8,128)}) custom-call(s32[4]{0:T(128)} %pad_add_fusion.refs_0_, bf16[1024,768]{1,0:T(8,128)(2,1)} %get-tuple-element.153.refs_9_.refs_1_, bf16[768,1024]{1,0:T(8,128)(2,1)} %get-tuple-element.154.refs_2_, bf16[256,1024]{1,0:T(8,128)(2,1)} %get-tuple-element.97.refs_7_.refs_1_.refs_3_.refs_2_, ...), custom_call_target="tpu_custom_call" | custom-call | flops 200000000 | bytes 600000 | tf_op jit(solution)/shard_map/normed/pallas_call | solution.py:568
  264.4 1.5 collective-permute-start.26
  265.9 1.5 collective-permute-start.27
  267.4 3.5 %all-to-all-start.3 = ((bf16[8,256,128]{2,1,0:T(8,128)(2,1)}), bf16[8,256,128]{2,1,0:T(8,128)(2,1)S(1)}, u32[]{:S(2)}, u32[]{:S(2)}) async-start(bf16[8,256,128]{2,1,0:T(8,128)(2,1)} %bitcast.13), calls=%async_computation.5 | async-start | bytes 1048576 | tf_op jit(solution)/shard_map/all_to_all | solution.py:627
  270.9 2.0 collective-permute-start.29
  272.9 13.0 %collective-permute-done.29 = f32[152,256]{1,0:T(8,128)S(1)} collective-permute-done((f32[152,256]{1,0:T(8,128)S(1)}, f32[152,256]{1,0:T(8,128)S(1)}, u32[]{:S(2)}, u32[]{:S(2)}) %collective-permute-start.29) | collective-permute-done | bytes 155680 | tf_op jit(solution)/shard_map/ppermute | solution.py:615
  286.0 2.0 collective-permute-start.30
  287.9 5.0 %in_grad.1.refs_0_ = bf16[6144,128]{1,0:T(8,128)(2,1)} custom-call(s32[4]{0:T(128)} %pad_add_fusion.refs_0_, bf16[1024,768]{1,0:T(8,128)(2,1)} %get-tuple-element.153.refs_9_.refs_1_, bf16[256,1024]{1,0:T(8,128)(2,1)} %get-tuple-element.97.refs_7_.refs_1_.refs_3_.refs_2_, bf16[256,1024]{1,0:T(8,128)(2,1)} %get-tuple-element.100.refs_2_.refs_4_.refs_3_, ...), custom_call_target="tpu_custom_call" | custom-call | flops 100000000 | bytes 300000 | tf_op jit(solution)/shard_map/in_grad/pallas_call | solution.py:568
  295.4 3.7 %all-to-all-start.4 = ((bf16[8,768,128]{2,1,0:T(8,128)(2,1)}), bf16[8,768,128]{2,1,0:T(8,128)(2,1)S(1)}, u32[]{:S(2)}, u32[]{:S(2)}) async-start(bf16[8,768,128]{2,1,0:T(8,128)(2,1)} %bitcast.26), calls=%async_computation.7 | async-start | bytes 3145728 | tf_op jit(solution)/shard_map/all_to_all | solution.py:627
  299.6 2.3 collective-permute-start.35
  302.0 2.2 layer_end.1
  305.4 1.6 collective-permute-start.32
  307.1 1.6 collective-permute-start.33
  308.6 2.9 finish.1.refs_4_
  311.6 2.0 collective-permute-start.36
  313.6 3.3 %end.1.refs_4_ = bf16[256,1024]{1,0:T(8,128)(2,1)} custom-call(bf16[256,1024]{1,0:T(8,128)(2,1)} %reduce-scatter.8.cloned.1.call-done.refs_0_, bf16[256,1024]{1,0:T(8,128)(2,1)} %get-tuple-element.111.refs_3_.refs_1_, f32[1024]{0:T(1024)} %refs_2_.6, f32[256,1024]{1,0:T(8,128)} %get-tuple-element.145.refs_1_.refs_3_, bf16[256,1024]{1,0:T(8,128)(2,1)} %finish.1.refs_4_), custom_call_target="tpu_custom_call" | custom-call | flops 1000000000 | bytes 3000000 | tf_op jit(solution)/shard_map/end/pallas_call | solution.py:568
  317.6 1.6 out_end.1.refs_1_
  320.0 1.1 copy-done.12
  321.2 2.5 in_end.1.refs_5_
  323.6 1.8 unpack.1
  (169 shorter events, 31.6 us)
Async XLA Ops:
  7.2 38.6 %copy-start = (f32[64,1024]{1,0:T(8,128)S(1)}, f32[64,1024]{1,0:T(8,128)}, u32[]{:S(2)}) copy-start(f32[64,1024]{1,0:T(8,128)} %param.42) | copy-start | bytes 786436
  7.2 63.9 %all-gather.4.cloned.1.call-start = ((), (), s32[]{:S(2)}) async-start(), calls=%async_computation.8 | async-start | bytes 1769472 | tf_op jit(solution)/shard_map/all_gather | solution.py:630
  7.2 8.9 %collective-permute-start.1 = (bf16[256,128]{1,0:T(8,128)(2,1)}, bf16[256,128]{1,0:T(8,128)(2,1)S(1)}, u32[]{:S(2)}, u32[]{:S(2)}) collective-permute-start(bf16[256,128]{1,0:T(8,128)(2,1)} %refs_3_.3), channel_id=1, source_target_pairs={{0,3},{1,0},{2,1},{3,2},{4,7},{5,4},{6,5},{7,6},{8,11},{9,8},{10,9... | collective-permute-start | bytes 196616 | tf_op jit(solution)/shard_map/ppermute | solution.py:618
  12.3 6.7 %collective-permute-start.2 = (bf16[256,128]{1,0:T(8,128)(2,1)}, bf16[256,128]{1,0:T(8,128)(2,1)S(1)}, u32[]{:S(2)}, u32[]{:S(2)}) collective-permute-start(bf16[256,128]{1,0:T(8,128)(2,1)} %refs_3_.3), channel_id=1, source_target_pairs={{0,2},{1,3},{2,0},{3,1},{4,6},{5,7},{6,4},{7,5},{8,10},{9,11},{10,... | collective-permute-start | bytes 196616 | tf_op jit(solution)/shard_map/ppermute | solution.py:618
  12.3 6.7 %collective-permute-start.3 = (bf16[256,128]{1,0:T(8,128)(2,1)}, bf16[256,128]{1,0:T(8,128)(2,1)S(1)}, u32[]{:S(2)}, u32[]{:S(2)}) collective-permute-start(bf16[256,128]{1,0:T(8,128)(2,1)} %refs_3_.3), channel_id=1, source_target_pairs={{0,1},{1,2},{2,3},{3,0},{4,5},{5,6},{6,7},{7,4},{8,9},{9,10},{10,1... | collective-permute-start | bytes 196616 | tf_op jit(solution)/shard_map/ppermute | solution.py:618
  16.1 2.9 copy-start.27
  21.9 80.1 %all-gather.6.cloned.1.call-start = ((), (), s32[]{:S(2)}) async-start(), calls=%async_computation.9 | async-start | bytes 2359296 | tf_op jit(solution)/shard_map/all_gather | solution.py:630
  22.7 17.5 %collective-permute-start = (bf16[256,1024]{1,0:T(8,128)(2,1)}, bf16[256,1024]{1,0:T(8,128)(2,1)S(1)}, u32[]{:S(2)}, u32[]{:S(2)}) collective-permute-start(bf16[256,1024]{1,0:T(8,128)(2,1)} %get-tuple-element.97.refs_7_.refs_1_.refs_3_.refs_2_), channel_id=1, source_target_pairs={{0,3},{1,0},{2,1},{3,2},{4,7},{5,4},{6,5},{7,6},{8,11},{9,8},{10,9... | collective-permute-start | bytes 1572872 | tf_op jit(solution)/shard_map/ppermute | solution.py:618
  24.6 15.6 %all-to-all-start = ((bf16[8,256,128]{2,1,0:T(8,128)(2,1)}), bf16[8,256,128]{2,1,0:T(8,128)(2,1)S(1)}, u32[]{:S(2)}, u32[]{:S(2)}) async-start(bf16[8,256,128]{2,1,0:T(8,128)(2,1)} %bitcast.37), calls=%async_computation | async-start | bytes 1048576 | tf_op jit(solution)/shard_map/all_to_all | solution.py:627
  28.4 120.6 %all-gather.8.cloned.1.call-start = ((), (), s32[]{:S(2)}) async-start(), calls=%async_computation.10 | async-start | bytes 4718592 | tf_op jit(solution)/shard_map/all_gather | solution.py:630
  33.6 10.1 %copy-start.30 = (f32[3,3072]{1,0:T(4,128)S(1)}, f32[3,3072]{1,0:T(4,128)}, u32[]{:S(2)}) copy-start(f32[3,3072]{1,0:T(4,128)} %param.36) | copy-start | bytes 110596
  41.8 11.6 %collective-permute-start.4 = (bf16[256,1024]{1,0:T(8,128)(2,1)}, bf16[256,1024]{1,0:T(8,128)(2,1)S(1)}, u32[]{:S(2)}, u32[]{:S(2)}) collective-permute-start(bf16[256,1024]{1,0:T(8,128)(2,1)} %get-tuple-element.100.refs_2_.refs_4_.refs_3_), channel_id=1, source_target_pairs={{0,3},{1,0},{2,1},{3,2},{4,7},{5,4},{6,5},{7,6},{8,11},{9,8},{10,9... | collective-permute-start | bytes 1572872 | tf_op jit(solution)/shard_map/ppermute | solution.py:618
  54.8 11.7 %collective-permute-start.5 = (bf16[256,1024]{1,0:T(8,128)(2,1)}, bf16[256,1024]{1,0:T(8,128)(2,1)S(1)}, u32[]{:S(2)}, u32[]{:S(2)}) collective-permute-start(bf16[256,1024]{1,0:T(8,128)(2,1)} %get-tuple-element.102.refs_3_.refs_5_.refs_4_), channel_id=1, source_target_pairs={{0,3},{1,0},{2,1},{3,2},{4,7},{5,4},{6,5},{7,6},{8,11},{9,8},{10,9... | collective-permute-start | bytes 1572872 | tf_op jit(solution)/shard_map/ppermute | solution.py:618
  68.0 146.6 %reduce-scatter.4.cloned.1.call-start = ((), (), s32[]{:S(2)}) async-start(), calls=%async_computation.11 | async-start | bytes 2621440 | tf_op jit(solution)/shard_map/reduce_scatter | solution.py:775
  68.0 17.2 %collective-permute-start.6 = (bf16[272,1024]{1,0:T(8,128)(2,1)}, bf16[272,1024]{1,0:T(8,128)(2,1)S(1)}, u32[]{:S(2)}, u32[]{:S(2)}) collective-permute-start(bf16[272,1024]{1,0:T(8,128)(2,1)} %get-tuple-element.107.refs_0_), channel_id=1, source_target_pairs={{0,3},{1,0},{2,1},{3,2},{4,7},{5,4},{6,5},{7,6},{8,11},{9,8},{10,9... | collective-permute-start | bytes 1671176 | tf_op jit(solution)/shard_map/ppermute | solution.py:618
  102.6 29.3 %collective-permute-start.10 = (bf16[272,1024]{1,0:T(8,128)(2,1)}, bf16[272,1024]{1,0:T(8,128)(2,1)S(1)}, u32[]{:S(2)}, u32[]{:S(2)}) collective-permute-start(bf16[272,1024]{1,0:T(8,128)(2,1)} %get-tuple-element.117.refs_13_), channel_id=1, source_target_pairs={{0,3},{1,0},{2,1},{3,2},{4,7},{5,4},{6,5},{7,6},{8,11},{9,8},{10,9... | collective-permute-start | bytes 1671176 | tf_op jit(solution)/shard_map/ppermute | solution.py:618
  110.1 21.8 %collective-permute-start.11 = (bf16[272,1024]{1,0:T(8,128)(2,1)}, bf16[272,1024]{1,0:T(8,128)(2,1)}, u32[]{:S(2)}, u32[]{:S(2)}) collective-permute-start(bf16[272,1024]{1,0:T(8,128)(2,1)} %get-tuple-element.118.refs_12_), channel_id=1, source_target_pairs={{0,1},{1,2},{2,3},{3,0},{4,5},{5,6},{6,7},{7,4},{8,9},{9,10},{10,1... | collective-permute-start | bytes 1671176 | tf_op jit(solution)/shard_map/ppermute | solution.py:618
  114.9 2.7 collective-permute-start.7
  114.9 15.5 %collective-permute-start.8 = (bf16[256,1024]{1,0:T(8,128)(2,1)}, bf16[256,1024]{1,0:T(8,128)(2,1)S(1)}, u32[]{:S(2)}, u32[]{:S(2)}) collective-permute-start(bf16[256,1024]{1,0:T(8,128)(2,1)} %get-tuple-element.116.refs_1_), channel_id=1, source_target_pairs={{0,8},{4,12},{8,0},{12,4},{16,24},{20,28},{24,16},{28,20},{1,9},{5... | collective-permute-start | bytes 1572872 | tf_op jit(solution)/shard_map/ppermute | solution.py:615
  117.6 14.3 %collective-permute-start.9 = (bf16[256,1024]{1,0:T(8,128)(2,1)}, bf16[256,1024]{1,0:T(8,128)(2,1)S(1)}, u32[]{:S(2)}, u32[]{:S(2)}) collective-permute-start(bf16[256,1024]{1,0:T(8,128)(2,1)} %get-tuple-element.116.refs_1_), channel_id=1, source_target_pairs={{0,16},{4,20},{8,24},{12,28},{16,0},{20,4},{24,8},{28,12},{1,17},{... | collective-permute-start | bytes 1572872 | tf_op jit(solution)/shard_map/ppermute | solution.py:615
  117.6 14.3 %copy-start.18 = (bf16[256,1024]{1,0:T(8,128)(2,1)}, bf16[256,1024]{1,0:T(8,128)(2,1)S(1)}, u32[]{:S(2)}) copy-start(bf16[256,1024]{1,0:T(8,128)(2,1)S(1)} %collective-permute-done.7.refs_3_.refs_2_) | copy-start | bytes 1572868
  130.4 1.5 copy-start.14
  134.5 13.0 %collective-permute-start.12 = (bf16[256,1024]{1,0:T(8,128)(2,1)}, bf16[256,1024]{1,0:T(8,128)(2,1)S(1)}, u32[]{:S(2)}, u32[]{:S(2)}) collective-permute-start(bf16[256,1024]{1,0:T(8,128)(2,1)} %get-tuple-element.119.refs_3_), channel_id=1, source_target_pairs={{0,4},{4,0},{8,12},{12,8},{16,20},{20,16},{24,28},{28,24},{1,5},{5... | collective-permute-start | bytes 1572872 | tf_op jit(solution)/shard_map/ppermute | solution.py:615
  135.5 10.2 %collective-permute-start.14 = (bf16[128,1024]{1,0:T(8,128)(2,1)S(1)}, bf16[128,1024]{1,0:T(8,128)(2,1)S(1)}, u32[]{:S(2)}, u32[]{:S(2)}) collective-permute-start(bf16[128,1024]{1,0:T(8,128)(2,1)S(1)} %slice.6), channel_id=1, source_target_pairs={{0,8},{4,12},{8,0},{12,4},{16,24},{20,28},{24,16},{28,20},{1,9},{5... | collective-permute-start | bytes 786440 | tf_op jit(solution)/shard_map/ppermute | solution.py:615
  138.7 8.7 %collective-permute-start.13 = (bf16[256,1024]{1,0:T(8,128)(2,1)}, bf16[256,1024]{1,0:T(8,128)(2,1)S(1)}, u32[]{:S(2)}, u32[]{:S(2)}) collective-permute-start(bf16[256,1024]{1,0:T(8,128)(2,1)} %get-tuple-element.120.refs_5_), channel_id=1, source_target_pairs={{0,4},{4,0},{8,12},{12,8},{16,20},{20,16},{24,28},{28,24},{1,5},{5... | collective-permute-start | bytes 1572872 | tf_op jit(solution)/shard_map/ppermute | solution.py:615
  138.9 8.5 %collective-permute-start.15 = (bf16[128,1024]{1,0:T(8,128)(2,1)S(1)}, bf16[128,1024]{1,0:T(8,128)(2,1)S(1)}, u32[]{:S(2)}, u32[]{:S(2)}) collective-permute-start(bf16[128,1024]{1,0:T(8,128)(2,1)S(1)} %slice.7), channel_id=1, source_target_pairs={{0,16},{4,20},{8,24},{12,28},{16,0},{20,4},{24,8},{28,12},{1,17},{... | collective-permute-start | bytes 786440 | tf_op jit(solution)/shard_map/ppermute | solution.py:615
  145.7 3.3 copy-start.35
  145.7 1.8 collective-permute-start.16
  147.4 1.5 copy-start.36
  147.4 1.5 collective-permute-start.17
  147.4 1.5 copy-start.31
  147.5 1.5 copy-start.32
  170.9 1.6 copy-start.11
  170.9 92.8 %reduce-scatter.6.cloned.1.call-start = ((), (), s32[]{:S(2)}) async-start(), calls=%async_computation.12 | async-start | bytes 2359296 | tf_op jit(solution)/shard_map/reduce_scatter | solution.py:633
  172.5 5.8 %collective-permute-start.19 = (bf16[1024,1024]{1,0:T(8,128)(2,1)S(1)}, bf16[1024,1024]{1,0:T(8,128)(2,1)}, u32[]{:S(2)}, u32[]{:S(2)}) collective-permute-start(bf16[1024,1024]{1,0:T(8,128)(2,1)S(1)} %copy-done.11), channel_id=1, source_target_pairs={{0,4},{4,0},{8,12},{12,8},{16,20},{20,16},{24,28},{28,24},{1,5},{5... | collective-permute-start | bytes 6291464 | tf_op jit(solution)/shard_map/ppermute | solution.py:615
  172.6 10.0 %collective-permute-start.18 = (bf16[1024,1024]{1,0:T(8,128)(2,1)}, bf16[1024,1024]{1,0:T(8,128)(2,1)}, u32[]{:S(2)}, u32[]{:S(2)}) collective-permute-start(bf16[1024,1024]{1,0:T(8,128)(2,1)} %get-tuple-element.127), channel_id=1, source_target_pairs={{0,4},{4,0},{8,12},{12,8},{16,20},{20,16},{24,28},{28,24},{1,5},{5... | collective-permute-start | bytes 6291464 | tf_op jit(solution)/shard_map/ppermute | solution.py:615
  182.0 8.6 %collective-permute-start.22 = (bf16[128,1024]{1,0:T(8,128)(2,1)}, bf16[128,1024]{1,0:T(8,128)(2,1)S(1)}, u32[]{:S(2)}, u32[]{:S(2)}) collective-permute-start(bf16[128,1024]{1,0:T(8,128)(2,1)} %get-tuple-element.139), channel_id=1, source_target_pairs={{0,8},{4,12},{8,0},{12,4},{16,24},{20,28},{24,16},{28,20},{1,9},{5... | collective-permute-start | bytes 786440 | tf_op jit(solution)/shard_map/ppermute | solution.py:615
  182.7 8.3 %collective-permute-start.23 = (bf16[128,1024]{1,0:T(8,128)(2,1)}, bf16[128,1024]{1,0:T(8,128)(2,1)S(1)}, u32[]{:S(2)}, u32[]{:S(2)}) collective-permute-start(bf16[128,1024]{1,0:T(8,128)(2,1)} %get-tuple-element.140), channel_id=1, source_target_pairs={{0,16},{4,20},{8,24},{12,28},{16,0},{20,4},{24,8},{28,12},{1,17},{... | collective-permute-start | bytes 786440 | tf_op jit(solution)/shard_map/ppermute | solution.py:615
  194.1 13.1 %collective-permute-start.24 = (bf16[256,1024]{1,0:T(8,128)(2,1)}, bf16[256,1024]{1,0:T(8,128)(2,1)S(1)}, u32[]{:S(2)}, u32[]{:S(2)}) collective-permute-start(bf16[256,1024]{1,0:T(8,128)(2,1)} %get-tuple-element.141.refs_8_), channel_id=1, source_target_pairs={{0,8},{4,12},{8,0},{12,4},{16,24},{20,28},{24,16},{28,20},{1,9},{5... | collective-permute-start | bytes 1572872 | tf_op jit(solution)/shard_map/ppermute | solution.py:615
  195.4 12.8 %collective-permute-start.25 = (bf16[256,1024]{1,0:T(8,128)(2,1)}, bf16[256,1024]{1,0:T(8,128)(2,1)S(1)}, u32[]{:S(2)}, u32[]{:S(2)}) collective-permute-start(bf16[256,1024]{1,0:T(8,128)(2,1)} %get-tuple-element.142), channel_id=1, source_target_pairs={{0,16},{4,20},{8,24},{12,28},{16,0},{20,4},{24,8},{28,12},{1,17},{... | collective-permute-start | bytes 1572872 | tf_op jit(solution)/shard_map/ppermute | solution.py:615
  218.4 3.8 %copy-start.34 = (bf16[128,1024]{1,0:T(8,128)(2,1)S(1)}, bf16[128,1024]{1,0:T(8,128)(2,1)}, u32[]{:S(2)}) copy-start(bf16[128,1024]{1,0:T(8,128)(2,1)} %get-tuple-element.135) | copy-start | bytes 786436
  218.4 5.0 %copy-start.33 = (bf16[128,1024]{1,0:T(8,128)(2,1)S(1)}, bf16[128,1024]{1,0:T(8,128)(2,1)}, u32[]{:S(2)}) copy-start(bf16[128,1024]{1,0:T(8,128)(2,1)} %get-tuple-element.136) | copy-start | bytes 786436
  218.4 16.7 %all-to-all-start.2 = ((bf16[4,256,256]{2,1,0:T(8,128)(2,1)}), bf16[4,256,256]{2,1,0:T(8,128)(2,1)S(1)}, u32[]{:S(2)}, u32[]{:S(2)}) async-start(bf16[4,256,256]{2,1,0:T(8,128)(2,1)} %bitcast.11), calls=%async_computation.3 | async-start | bytes 1048576 | tf_op jit(solution)/shard_map/all_to_all | solution.py:624
  222.2 91.4 %reduce-scatter.8.cloned.1.call-start = ((), (), s32[]{:S(2)}) async-start(), calls=%async_computation.13 | async-start | bytes 2621440 | tf_op jit(solution)/shard_map/reduce_scatter | solution.py:824
  222.2 6.4 %collective-permute-start.20 = (bf16[128,1024]{1,0:T(8,128)(2,1)S(1)}, bf16[128,1024]{1,0:T(8,128)(2,1)S(1)}, u32[]{:S(2)}, u32[]{:S(2)}) collective-permute-start(bf16[128,1024]{1,0:T(8,128)(2,1)S(1)} %copy-done.34), channel_id=1, source_target_pairs={{0,8},{4,12},{8,0},{12,4},{16,24},{20,28},{24,16},{28,20},{1,9},{5... | collective-permute-start | bytes 786440 | tf_op jit(solution)/shard_map/ppermute | solution.py:615
  223.3 6.4 %collective-permute-start.21 = (bf16[128,1024]{1,0:T(8,128)(2,1)S(1)}, bf16[128,1024]{1,0:T(8,128)(2,1)S(1)}, u32[]{:S(2)}, u32[]{:S(2)}) collective-permute-start(bf16[128,1024]{1,0:T(8,128)(2,1)S(1)} %copy-done.33), channel_id=1, source_target_pairs={{0,16},{4,20},{8,24},{12,28},{16,0},{20,4},{24,8},{28,12},{1,17},{... | collective-permute-start | bytes 786440 | tf_op jit(solution)/shard_map/ppermute | solution.py:615
  264.4 3.0 copy-start.16
  264.4 29.2 %collective-permute-start.26 = (bf16[256,1024]{1,0:T(8,128)(2,1)}, bf16[256,1024]{1,0:T(8,128)(2,1)S(1)}, u32[]{:S(2)}, u32[]{:S(2)}) collective-permute-start(bf16[256,1024]{1,0:T(8,128)(2,1)} %get-tuple-element.148.refs_1_), channel_id=1, source_target_pairs={{0,8},{4,12},{8,0},{12,4},{16,24},{20,28},{24,16},{28,20},{1,9},{5... | collective-permute-start | bytes 1572872 | tf_op jit(solution)/shard_map/ppermute | solution.py:615
  265.9 27.7 %collective-permute-start.27 = (bf16[256,1024]{1,0:T(8,128)(2,1)}, bf16[256,1024]{1,0:T(8,128)(2,1)S(1)}, u32[]{:S(2)}, u32[]{:S(2)}) collective-permute-start(bf16[256,1024]{1,0:T(8,128)(2,1)} %get-tuple-element.149), channel_id=1, source_target_pairs={{0,16},{4,20},{8,24},{12,28},{16,0},{20,4},{24,8},{28,12},{1,17},{... | collective-permute-start | bytes 1572872 | tf_op jit(solution)/shard_map/ppermute | solution.py:615
  267.4 3.5 %collective-permute-start.28 = (f32[152,256]{1,0:T(8,128)S(1)}, f32[152,256]{1,0:T(8,128)S(1)}, u32[]{:S(2)}, u32[]{:S(2)}) collective-permute-start(f32[152,256]{1,0:T(8,128)S(1)} %copy-done.16), channel_id=1, source_target_pairs={{0,4},{4,0},{8,12},{12,8},{16,20},{20,16},{24,28},{28,24},{1,5},{5... | collective-permute-start | bytes 466952 | tf_op jit(solution)/shard_map/ppermute | solution.py:615
  267.4 26.3 %all-to-all-start.3 = ((bf16[8,256,128]{2,1,0:T(8,128)(2,1)}), bf16[8,256,128]{2,1,0:T(8,128)(2,1)S(1)}, u32[]{:S(2)}, u32[]{:S(2)}) async-start(bf16[8,256,128]{2,1,0:T(8,128)(2,1)} %bitcast.13), calls=%async_computation.5 | async-start | bytes 1048576 | tf_op jit(solution)/shard_map/all_to_all | solution.py:627
  270.9 15.0 %collective-permute-start.29 = (f32[152,256]{1,0:T(8,128)S(1)}, f32[152,256]{1,0:T(8,128)S(1)}, u32[]{:S(2)}, u32[]{:S(2)}) collective-permute-start(f32[152,256]{1,0:T(8,128)S(1)} %add.60), channel_id=1, source_target_pairs={{0,8},{4,12},{8,0},{12,4},{16,24},{20,28},{24,16},{28,20},{1,9},{5... | collective-permute-start | bytes 466952 | tf_op jit(solution)/shard_map/ppermute | solution.py:615
  286.0 7.0 %collective-permute-start.30 = (f32[152,256]{1,0:T(8,128)S(1)}, f32[152,256]{1,0:T(8,128)S(1)}, u32[]{:S(2)}, u32[]{:S(2)}) collective-permute-start(f32[152,256]{1,0:T(8,128)S(1)} %add.61), channel_id=1, source_target_pairs={{0,16},{4,20},{8,24},{12,28},{16,0},{20,4},{24,8},{28,12},{1,17},{... | collective-permute-start | bytes 466952 | tf_op jit(solution)/shard_map/ppermute | solution.py:615
  295.4 3.8 %copy-start.13 = (f32[152,256]{1,0:T(8,128)S(1)}, f32[152,256]{1,0:T(8,128)}, u32[]{:S(2)}) copy-start(f32[152,256]{1,0:T(8,128)} %get-tuple-element.169) | copy-start | bytes 466948
  295.4 24.7 %all-to-all-start.4 = ((bf16[8,768,128]{2,1,0:T(8,128)(2,1)}), bf16[8,768,128]{2,1,0:T(8,128)(2,1)S(1)}, u32[]{:S(2)}, u32[]{:S(2)}) async-start(bf16[8,768,128]{2,1,0:T(8,128)(2,1)} %bitcast.26), calls=%async_computation.7 | async-start | bytes 3145728 | tf_op jit(solution)/shard_map/all_to_all | solution.py:627
  299.2 5.0 %copy-start.26 = (bf16[152,256]{1,0:T(8,128)(2,1)}, bf16[152,256]{1,0:T(8,128)(2,1)S(1)}, u32[]{:S(2)}) copy-start(bf16[152,256]{1,0:T(8,128)(2,1)S(1)} %convert_element_type.3.refs_1_) | copy-start | bytes 233476
  299.2 12.4 %collective-permute-start.34 = (bf16[152,256]{1,0:T(8,128)(2,1)S(1)}, bf16[152,256]{1,0:T(8,128)(2,1)}, u32[]{:S(2)}, u32[]{:S(2)}) collective-permute-start(bf16[152,256]{1,0:T(8,128)(2,1)S(1)} %convert_element_type.3.refs_1_), channel_id=1, source_target_pairs={{0,1},{1,0},{2,3},{3,2},{4,5},{5,4},{6,7},{7,6},{8,9},{9,8},{10,11... | collective-permute-start | bytes 233480 | tf_op jit(solution)/shard_map/ppermute | solution.py:621
  299.6 24.0 %collective-permute-start.35 = (bf16[152,256]{1,0:T(8,128)(2,1)S(1)}, bf16[152,256]{1,0:T(8,128)(2,1)}, u32[]{:S(2)}, u32[]{:S(2)}) collective-permute-start(bf16[152,256]{1,0:T(8,128)(2,1)S(1)} %convert_element_type.3.refs_1_), channel_id=1, source_target_pairs={{0,2},{1,3},{2,0},{3,1},{4,6},{5,7},{6,4},{7,5},{8,10},{9,11},{10,... | collective-permute-start | bytes 233480 | tf_op jit(solution)/shard_map/ppermute | solution.py:621
  302.0 2.2 copy-start.6
  304.8 12.1 %collective-permute-start.31 = (bf16[256,128]{1,0:T(8,128)(2,1)}, bf16[256,128]{1,0:T(8,128)(2,1)S(1)}, u32[]{:S(2)}, u32[]{:S(2)}) collective-permute-start(bf16[256,128]{1,0:T(8,128)(2,1)} %get-tuple-element.181), channel_id=1, source_target_pairs={{0,1},{1,2},{2,3},{3,0},{4,5},{5,6},{6,7},{7,4},{8,9},{9,10},{10,1... | collective-permute-start | bytes 196616 | tf_op jit(solution)/shard_map/ppermute | solution.py:618
  305.4 11.5 %collective-permute-start.32 = (bf16[256,128]{1,0:T(8,128)(2,1)}, bf16[256,128]{1,0:T(8,128)(2,1)S(1)}, u32[]{:S(2)}, u32[]{:S(2)}) collective-permute-start(bf16[256,128]{1,0:T(8,128)(2,1)} %get-tuple-element.180), channel_id=1, source_target_pairs={{0,2},{1,3},{2,0},{3,1},{4,6},{5,7},{6,4},{7,5},{8,10},{9,11},{10,... | collective-permute-start | bytes 196616 | tf_op jit(solution)/shard_map/ppermute | solution.py:618
  307.1 9.9 %collective-permute-start.33 = (bf16[256,128]{1,0:T(8,128)(2,1)S(1)}, bf16[256,128]{1,0:T(8,128)(2,1)S(1)}, u32[]{:S(2)}, u32[]{:S(2)}) collective-permute-start(bf16[256,128]{1,0:T(8,128)(2,1)S(1)} %get-tuple-element.179), channel_id=1, source_target_pairs={{0,3},{1,0},{2,1},{3,2},{4,7},{5,4},{6,5},{7,6},{8,11},{9,8},{10,9... | collective-permute-start | bytes 196616 | tf_op jit(solution)/shard_map/ppermute | solution.py:618
  311.6 12.1 %collective-permute-start.36 = (bf16[152,256]{1,0:T(8,128)(2,1)}, bf16[152,256]{1,0:T(8,128)(2,1)}, u32[]{:S(2)}, u32[]{:S(2)}) collective-permute-start(bf16[152,256]{1,0:T(8,128)(2,1)} %collective-permute-done.34.refs_2_), channel_id=1, source_target_pairs={{0,2},{1,3},{2,0},{3,1},{4,6},{5,7},{6,4},{7,5},{8,10},{9,11},{10,... | collective-permute-start | bytes 233480 | tf_op jit(solution)/shard_map/ppermute | solution.py:621
  321.2 4.3 %copy-start.1 = (f32[64,1024]{1,0:T(8,128)S(1)}, f32[64,1024]{1,0:T(8,128)}, u32[]{:S(2)}) copy-start(f32[64,1024]{1,0:T(8,128)} %param.42) | copy-start | bytes 786436
  (25 other events, 20.7 us)
Sparse Core Ops, SparseCore 0:
  22.0 28.6 all-gather.3
  53.2 27.8 all-gather.5
  83.6 36.7 all-gather.7
  171.1 41.9 reduce-scatter.3
  218.5 39.8 reduce-scatter.5
  264.5 47.2 reduce-scatter.7
